TPU v7x, 32 devices: a whole 2x2x4 slice. The times are simulated.
32 devices in a mesh: grp: 2 (over y), node: 4 (over z), rank: 4 (over x, core).
Axes of the slice: x: 2, y: 2, z: 4, core: 2. Of those that a mesh axis runs over, the one named last changes fastest.
Arguments:
- tokens: bfloat16 [1024, 2048], P(('grp', 'node', 'rank')), parts along dimension 0, may hold values from -6 to 6
- expert_ids: int32 [1024, 10], P(('grp', 'node', 'rank')), parts along dimension 0, may hold values from 0 to 31, all different within a row; in each aligned block of 32 rows (0 to 31, 32 to 63, ...) at most 15 rows name the same one
- combine_weights: int32 [1024, 10], P(('grp', 'node', 'rank')), parts along dimension 0, may hold values from 16384 to 65535
- slot_plan: int32 [32], replicated, may hold values from 0 to 31, each once
- w_gate: bfloat16 [32, 2048, 512], P(('node', 'rank')), may hold values from -0.125 to 0.125
- w_up: bfloat16 [32, 2048, 512], P(('node', 'rank')), may hold values from -0.125 to 0.125
- w_down: bfloat16 [32, 512, 2048], P(('node', 'rank')), may hold values from -0.25 to 0.25
Outputs:
- mixed: bfloat16 [1024, 2048], P(('grp', 'node', 'rank')), parts along dimension 0
There are 2 independent parts, one for each index of `grp`. A program takes and returns all parts, laid end to end along the dimension named above; an argument that names none is the same for every part. Nothing has to cross between parts.
Inputs may be any that keep to these rules, and one draw needn't show every extreme that they name: `expert_ids`: each row names 10 different experts; among the rows of one device no expert is named more than 15 times, and in every draw some expert reaches 15. `slot_plan`: each slot once.
All inputs are finite; a program needn't handle non-finite values.
Results may differ from a plain program's by a relative error of at most 0.0058.
Values may be sent and summed in bfloat16 or wider, within the bound.
No kernel may reach another device: no remote copies, remote signals or barrier semaphores. Data moves between devices by JAX's collectives and lax.ppermute only.
A program may use at most 64 MiB of HBM per device.

v0:
```python
import jax
import jax.numpy as jnp
from jax import lax
from jax.sharding import PartitionSpec as P


def local(tokens, expert_ids, combine_weights, slot_plan, w_gate, w_up, w_down):
    n_node = lax.axis_size("node")
    n_rank = lax.axis_size("rank")
    n_dev = n_node * n_rank
    exp_dev = w_gate.shape[0]
    slots = n_dev * exp_dev
    tok_rows, top = expert_ids.shape
    width = tokens.shape[1]
    capacity = max(2, (3 * tok_rows * top + 2 * slots - 1) // (2 * slots))
    flat_ids = expert_ids.reshape(-1)
    onehot = (flat_ids[:, None] == jnp.arange(slots, dtype=jnp.int32)[None, :]).astype(jnp.int32)
    slot_of = jnp.sum(onehot * slot_plan[None, :], axis=1)
    earlier = jnp.cumsum(onehot, axis=0) - onehot
    position = jnp.sum(earlier * onehot, axis=1)
    target = slot_of * capacity + position
    repeated = jnp.repeat(tokens, top, axis=0)
    outgoing = jnp.zeros((slots * capacity, width), jnp.bfloat16).at[target].set(repeated)
    flat_out = outgoing.reshape(n_dev, exp_dev * capacity, width)
    arrived = lax.all_to_all(flat_out, ("node", "rank"), split_axis=0, concat_axis=0, tiled=True)
    arrived = arrived.reshape(n_dev, exp_dev, capacity, width)
    gate = jnp.einsum("secd,edf->secf", arrived, w_gate, preferred_element_type=jnp.float32)
    up = jnp.einsum("secd,edf->secf", arrived, w_up, preferred_element_type=jnp.float32)
    hidden = (jax.nn.silu(gate) * up).astype(jnp.bfloat16)
    result = jnp.einsum(
        "secf,efd->secd", hidden, w_down, preferred_element_type=jnp.float32
    ).astype(jnp.bfloat16)
    flat_back = result.reshape(n_dev, exp_dev * capacity, width)
    returned = lax.all_to_all(flat_back, ("node", "rank"), split_axis=0, concat_axis=0, tiled=True)
    returned = returned.reshape(slots * capacity, width)
    picked = returned[target].reshape(tok_rows, top, width)
    scales = combine_weights.astype(jnp.float32) / 65536.0
    mixed = jnp.sum(picked.astype(jnp.float32) * scales[:, :, None], axis=1)
    return mixed.astype(jnp.bfloat16)


def solution(mesh):
    in_specs = (
        P(("grp", "node", "rank"), None),
        P(("grp", "node", "rank"), None),
        P(("grp", "node", "rank"), None),
        P(),
        P(("node", "rank"), None, None),
        P(("node", "rank"), None, None),
        P(("node", "rank"), None, None),
    )
    out_specs = P(("grp", "node", "rank"), None)
    return jax.shard_map(local, mesh=mesh, in_specs=in_specs, out_specs=out_specs, check_vma=False)
```

profile of v0, /device:TPU:8, one launch (start us, length us, event | category | flops | bytes accessed | tf_op | source)
XLA Modules:
  0.0 139.2 jit_solution(4044873898874885216)
XLA Ops:
  0.0 0.8 copy.10
  0.8 0.1 eq.22
  0.9 0.9 reduce-window.6
  1.8 0.2 slice_reduce_fusion
  2.1 0.1 bitcast_bitcast_fusion
  2.1 0.8 select_reduce_fusion
  2.9 1.2 broadcast_in_dim.5
  4.1 0.5 reshape.79
  4.6 4.0 %scatter_custom_fusion = bf16[480,2048]{1,0:T(8,128)(2,1)} fusion(s32[320]{0:T(512)S(1)} %fusion.28, bf16[320,2048]{1,0:T(8,128)(2,1)S(1)} %reshape.79, bf16[]{:T(256)} %constant.7.clone.1), kind=kCustom, calls=%fused_computation.14 | custom fusion | bytes 1966082 | tf_op jit(solution)/shard_map/scatter | solution.py:23
  8.6 1.8 %reshape.61 = bf16[16,30,2048]{2,1,0:T(8,128)(2,1)S(1)} reshape(bf16[480,2048]{1,0:T(8,128)(2,1)} %scatter_custom_fusion) | data formatting | bytes 3932160 | tf_op jit(solution)/shard_map/reshape | solution.py:24
  10.4 0.0 copy-start.1
  10.4 53.7 %all_to_all.10 = bf16[16,30,2048]{2,1,0:T(8,128)(2,1)S(1)} all-to-all(bf16[16,30,2048]{2,1,0:T(8,128)(2,1)S(1)} %reshape.61), channel_id=1, replica_groups=mesh['grp'=2,'node'=4,'rank'=4] {'node','rank'}, dimensions={0} | all-to-all | bytes 3932160 | tf_op jit(solution)/shard_map/all_to_all | solution.py:25
  64.1 1.1 copy.13
  65.2 0.0 copy-done.1
  65.2 1.2 fusion.9
  66.4 7.1 %fusion.6 = bf16[2,16,15,2048]{3,1,2,0:T(8,128)(2,1)} fusion(bf16[2,512,2048]{2,1,0:T(8,128)(2,1)} %param.13, bf16[16,2,15,2048]{3,0,2,1:T(8,128)(2,1)S(1)} %bitcast.57, bf16[2,2048,512]{2,1,0:T(8,128)(2,1)} %param.12, f32[16,2,15,512]{3,0,2,1:T(8,128)S(1)} %fusion.9), kind=kOutput, calls=%fused_computation.9 | convolution fusion | flops 2015723520 | bytes 13303808 | tf_op jit(solution)/shard_map/secf,efd->secd/dot_general | solution.py:30
  73.5 4.0 %copy.14 = bf16[16,30,2048]{2,1,0:T(8,128)(2,1)} copy(bf16[16,30,2048]{2,0,1:T(8,128)(2,1)} %bitcast.58) | data formatting | bytes 3932160 | tf_op jit(solution)/shard_map/reshape | solution.py:33
  77.5 0.0 copy-start
  77.5 5.2 %all-to-all-start.1 = ((bf16[16,30,2048]{2,1,0:T(8,128)(2,1)}), bf16[16,30,2048]{2,1,0:T(8,128)(2,1)}, u32[]{:S(2)}, u32[]{:S(2)}) async-start(bf16[16,30,2048]{2,1,0:T(8,128)(2,1)} %copy.14), calls=%async_computation.1 | async-start | bytes 4194304 | tf_op jit(solution)/shard_map/all_to_all | solution.py:34
  82.7 0.0 copy-done
  82.7 0.1 copy.15
  82.8 45.8 %all-to-all-done.1 = bf16[16,30,2048]{2,1,0:T(8,128)(2,1)} async-done(((bf16[16,30,2048]{2,1,0:T(8,128)(2,1)}), bf16[16,30,2048]{2,1,0:T(8,128)(2,1)}, u32[]{:S(2)}, u32[]{:S(2)}) %all-to-all-start.1) | async-done | bytes 1966112 | tf_op jit(solution)/shard_map/all_to_all | solution.py:34
  128.6 1.8 %reshape.64 = bf16[480,2048]{1,0:T(8,128)(2,1)S(1)} reshape(bf16[16,30,2048]{2,1,0:T(8,128)(2,1)} %all-to-all-done.1) | data formatting | bytes 3932160 | tf_op jit(solution)/shard_map/reshape | solution.py:35
  130.4 2.4 %gather_fusion = bf16[320,2048]{1,0:T(8,128)(2,1)S(1)} fusion(bf16[480,2048]{1,0:T(8,128)(2,1)S(1)} %reshape.64, s32[1024]{0:T(1024)S(1)} %pad_clamp_fusion), kind=kCustom, calls=%fused_computation | custom fusion | bytes 2622720 | tf_op jit(solution)/shard_map/gather | solution.py:36
  132.8 2.1 %reshape.66 = f32[32,10,2048]{2,1,0:T(8,128)} reshape(bf16[320,2048]{1,0:T(8,128)(2,1)S(1)} %gather_fusion) | data formatting | bytes 3932160 | tf_op jit(solution)/shard_map/convert_element_type | solution.py:38
  134.9 4.3 %multiply_reduce_fusion = bf16[32,2048]{1,0:T(8,128)(2,1)} fusion(f32[32,10,2048]{2,1,0:T(8,128)} %reshape.66, f32[32,10]{1,0:T(8,128)S(1)} %copy.15), kind=kLoop, calls=%fused_computation.8 | loop fusion | flops 1245184 | bytes 2753792 | tf_op jit(solution)/shard_map/reduce_sum | solution.py:38
  (7 shorter events, 0.1 us)
Async XLA Ops:
  10.4 54.8 %copy-start.1 = (bf16[2,2048,512]{2,1,0:T(8,128)(2,1)S(1)}, bf16[2,2048,512]{2,1,0:T(8,128)(2,1)}, u32[]{:S(2)}) copy-start(bf16[2,2048,512]{2,1,0:T(8,128)(2,1)} %param.11) | copy-start | bytes 12582916
  77.5 5.2 %copy-start = (s32[32,10]{0,1:T(8,128)S(1)}, s32[32,10]{0,1:T(8,128)}, u32[]{:S(2)}) copy-start(s32[32,10]{0,1:T(8,128)} %param.9) | copy-start | bytes 3844
  77.5 51.1 %all-to-all-start.1 = ((bf16[16,30,2048]{2,1,0:T(8,128)(2,1)}), bf16[16,30,2048]{2,1,0:T(8,128)(2,1)}, u32[]{:S(2)}, u32[]{:S(2)}) async-start(bf16[16,30,2048]{2,1,0:T(8,128)(2,1)} %copy.14), calls=%async_computation.1 | async-start | bytes 4194304 | tf_op jit(solution)/shard_map/all_to_all | solution.py:34
where the time goes:
time: 142 us; the launch traced here: 139 us
  blocking collectives  53.7 us (38%)
  waiting for transfers between devices  45.8 us (32%)
  local copies, waits for them, and re-layouts  20 us (14%)
  matrix products  8.31 us (6%)
  other arithmetic  6.06 us (4%)
  starting transfers between devices  5.2 us (4%)
    all_to_all x1, blocking collectives, local(): lax.all_to_all(flat_out, ('node', 'rank'), split_axis=0, concat_axis=0, t...  53.7 us
    all_to_all x1, waiting for transfers between devices, local(): lax.all_to_all(flat_back, ('node', 'rank'), split_axis=0, concat_axis=0,...  45.8 us
    dot_general x1, matrix products, local(): jnp.einsum('secf,efd->secd', hidden, w_down, preferred_element_type=jnp.f...  7.09 us
    all_to_all x1, starting transfers between devices, local(): lax.all_to_all(flat_back, ('node', 'rank'), split_axis=0, concat_axis=0,...  5.2 us
    reduce_sum x1, other arithmetic, local(): mixed = jnp.sum(picked.astype(jnp.float32) * scales[:, :, None], axis=1)  4.25 us
    scatter x1, local copies, waits for them, and re-layouts, local(): jnp.zeros((slots * capacity, width), jnp.bfloat16).at[target].set(repeated)  4 us
    reshape x1, local copies, waits for them, and re-layouts, local(): flat_back = result.reshape(n_dev, exp_dev * capacity, width)  3.98 us
  transfers between devices with their start and end apart: 1, of which 1 were waited for; matrix products, arithmetic and copies ran while one was open for 0% of the time, Pallas kernels for 0%

commit v1 on v0

--- a/solution.py
+++ b/solution.py
@@ -1,18 +1,28 @@
+import functools
+
 import jax
 import jax.numpy as jnp
 from jax import lax
+from jax.experimental import pallas as pl
+from jax.experimental.pallas import tpu as pltpu
 from jax.sharding import PartitionSpec as P
 
-
-def local(tokens, expert_ids, combine_weights, slot_plan, w_gate, w_up, w_down):
-    n_node = lax.axis_size("node")
-    n_rank = lax.axis_size("rank")
-    n_dev = n_node * n_rank
+LANES = 128
+VMEM = pl.BlockSpec(memory_space=pltpu.VMEM)
+SMEM = pl.BlockSpec(memory_space=pltpu.SMEM)
+
+
+def capacity_of(tok_rows, top, slots):
+    return max(2, (3 * tok_rows * top + 2 * slots - 1) // (2 * slots))
+
+
+def routed(tokens, expert_ids, combine_weights, slot_plan, w_gate, w_up, w_down):
+    n_dev = lax.axis_size("node") * lax.axis_size("rank")
     exp_dev = w_gate.shape[0]
     slots = n_dev * exp_dev
     tok_rows, top = expert_ids.shape
     width = tokens.shape[1]
-    capacity = max(2, (3 * tok_rows * top + 2 * slots - 1) // (2 * slots))
+    capacity = capacity_of(tok_rows, top, slots)
     flat_ids = expert_ids.reshape(-1)
     onehot = (flat_ids[:, None] == jnp.arange(slots, dtype=jnp.int32)[None, :]).astype(jnp.int32)
     slot_of = jnp.sum(onehot * slot_plan[None, :], axis=1)
@@ -27,9 +37,7 @@
     gate = jnp.einsum("secd,edf->secf", arrived, w_gate, preferred_element_type=jnp.float32)
     up = jnp.einsum("secd,edf->secf", arrived, w_up, preferred_element_type=jnp.float32)
     hidden = (jax.nn.silu(gate) * up).astype(jnp.bfloat16)
-    result = jnp.einsum(
-        "secf,efd->secd", hidden, w_down, preferred_element_type=jnp.float32
-    ).astype(jnp.bfloat16)
+    result = jnp.einsum("secf,efd->secd", hidden, w_down, preferred_element_type=jnp.float32).astype(jnp.bfloat16)
     flat_back = result.reshape(n_dev, exp_dev * capacity, width)
     returned = lax.all_to_all(flat_back, ("node", "rank"), split_axis=0, concat_axis=0, tiled=True)
     returned = returned.reshape(slots * capacity, width)
@@ -37,6 +45,148 @@
     scales = combine_weights.astype(jnp.float32) / 65536.0
     mixed = jnp.sum(picked.astype(jnp.float32) * scales[:, :, None], axis=1)
     return mixed.astype(jnp.bfloat16)
+
+
+def ffn_kernel(mine_ref, *refs, blocks, top):
+    ins, (wg_ref, wu_ref, wd_ref, near_ref, far_ref, rows) = refs[:blocks], refs[blocks:]
+    width = near_ref.shape[1]
+    step = ins[0].shape[0]
+    for i, ref in enumerate(ins):
+        rows[pl.ds(i * step, step), :] = ref[...]
+    x = rows[:, :width]
+    meta = rows[:, width:].astype(jnp.float32)
+    ids, weight = meta[:, :top], (meta[:, top : 2 * top] * 256.0 + meta[:, 2 * top : 3 * top]) * (1.0 / 65536.0)
+    total = None
+    for e in range(wg_ref.shape[0]):
+        scale = jnp.sum(jnp.where(ids == mine_ref[e].astype(jnp.float32), weight, 0.0), axis=1, keepdims=True)
+        gate = jnp.dot(x, wg_ref[e], preferred_element_type=jnp.float32)
+        up = jnp.dot(x, wu_ref[e], preferred_element_type=jnp.float32)
+        hidden = (gate / (1.0 + jnp.exp(-gate)) * up).astype(jnp.bfloat16)
+        part = jnp.dot(hidden, wd_ref[e], preferred_element_type=jnp.float32) * scale
+        total = part if total is None else total + part
+    half = near_ref.shape[0]
+    near_ref[...] = total[:half]
+    far_ref[...] = total[half:].astype(far_ref.dtype)
+
+
+def ffn(mine, blocks, w_gate, w_up, w_down, top):
+    width = w_gate.shape[1]
+    rows = sum(b.shape[0] for b in blocks)
+    return pl.pallas_call(
+        functools.partial(ffn_kernel, blocks=len(blocks), top=top),
+        out_shape=(
+            jax.ShapeDtypeStruct((rows // 2, width), jnp.float32),
+            jax.ShapeDtypeStruct((rows // 2, width), jnp.bfloat16),
+        ),
+        in_specs=[SMEM] + [VMEM] * (len(blocks) + 3),
+        out_specs=(VMEM, VMEM),
+        scratch_shapes=[pltpu.VMEM((rows, blocks[0].shape[1]), jnp.bfloat16)],
+        compiler_params=pltpu.CompilerParams(vmem_limit_bytes=24 << 20),
+        name=f"ffn_{rows}",
+    )(mine, *blocks, w_gate, w_up, w_down)
+
+
+def join_kernel(near_ref, other_ref, *out_refs):
+    step = out_refs[0].shape[0]
+    for i, ref in enumerate(out_refs):
+        part = near_ref[pl.ds(i * step, step), :] + other_ref[pl.ds(i * step, step), :].astype(jnp.float32)
+        ref[...] = part.astype(ref.dtype)
+
+
+def join(near, other, types):
+    step = near.shape[0] // len(types)
+    return pl.pallas_call(
+        join_kernel,
+        out_shape=tuple(jax.ShapeDtypeStruct((step, near.shape[1]), t) for t in types),
+        in_specs=[VMEM, VMEM],
+        out_specs=(VMEM,) * len(types),
+        compiler_params=pltpu.CompilerParams(vmem_limit_bytes=16 << 20),
+        name="join",
+    )(near, other)
+
+
+def total_kernel(*refs):
+    total = refs[0][...].astype(jnp.float32)
+    for ref in refs[1:-1]:
+        total += ref[...].astype(jnp.float32)
+    refs[-1][...] = total.astype(refs[-1].dtype)
+
+
+def add_up(parts, dtype):
+    return pl.pallas_call(
+        total_kernel,
+        out_shape=jax.ShapeDtypeStruct(parts[0].shape, dtype),
+        in_specs=[VMEM] * len(parts),
+        out_specs=VMEM,
+        compiler_params=pltpu.CompilerParams(vmem_limit_bytes=16 << 20),
+        name="total",
+    )(*parts)
+
+
+def dense(tokens, expert_ids, combine_weights, slot_plan, w_gate, w_up, w_down, cores):
+    n_node, n_rank = lax.axis_size("node"), lax.axis_size("rank")
+    n_x = n_rank // cores
+    exp_dev, width = w_gate.shape[:2]
+    slots = n_node * n_rank * exp_dev
+    top = expert_ids.shape[1]
+
+    def along_z(t, dz):
+        return lax.ppermute(t, "node", [(i, i ^ dz) for i in range(n_node)])
+
+    def along_x(t, dx):
+        return lax.ppermute(t, "rank", [(i, i ^ (dx * cores)) for i in range(n_rank)])
+
+    def to_chip(t, dz, dx):
+        step = dz * n_rank + dx * cores
+        return lax.ppermute(t, ("node", "rank"), [(i, i ^ step) for i in range(n_node * n_rank)])
+
+    def swap(t):
+        return lax.ppermute(t, "rank", [(i, i ^ 1) for i in range(n_rank)])
+
+    device = lax.axis_index("node") * n_rank + lax.axis_index("rank")
+    my_slots = device * exp_dev + jnp.arange(exp_dev, dtype=jnp.int32)
+    plan_hit = slot_plan[None, :] == my_slots[:, None]
+    mine = jnp.sum(jnp.where(plan_hit, jnp.arange(slots, dtype=jnp.int32)[None, :], 0), axis=1)
+
+    pad = LANES - 3 * top
+    meta = jnp.concatenate([expert_ids, combine_weights // 256, combine_weights % 256], axis=1)
+    own = jnp.concatenate([tokens, jnp.pad(meta, ((0, 0), (0, pad))).astype(jnp.bfloat16)], axis=1)
+
+    chips = [(dz, dx) for dz in range(n_node) for dx in range(n_x)]
+    near = {(0, 0): own}
+    for dz in range(1, n_node):
+        near[dz, 0] = along_z(own, dz)
+    for dz in range(n_node):
+        for dx in range(1, n_x):
+            near[dz, dx] = along_x(near[dz, 0], dx)
+    far = {c: swap(near[c]) for c in chips}
+
+    passes = [chips]
+    sums = {}
+    for group in passes:
+        keep, give = ffn(mine, [near[c] for c in group] + [far[c] for c in group], w_gate, w_up, w_down, top)
+        types = [jnp.float32 if c == (0, 0) else jnp.bfloat16 for c in group]
+        for c, part in zip(group, join(keep, swap(give), types), strict=True):
+            sums[c] = part
+    parts = [sums[0, 0]] + [to_chip(sums[c], *c) for c in chips if c != (0, 0)]
+    return add_up(parts, tokens.dtype)
+
+
+def power_of_two(n):
+    return n & (n - 1) == 0
+
+
+def local(tokens, expert_ids, combine_weights, slot_plan, w_gate, w_up, w_down):
+    n_node, n_rank = lax.axis_size("node"), lax.axis_size("rank")
+    tok_rows, top = expert_ids.shape
+    exp_dev = w_gate.shape[0]
+    slots = n_node * n_rank * exp_dev
+    args = (tokens, expert_ids, combine_weights, slot_plan, w_gate, w_up, w_down)
+    sent = exp_dev * capacity_of(tok_rows, top, slots)
+    fits = 3 * top <= LANES and slots <= 256 and power_of_two(n_node) and power_of_two(n_rank) and n_rank > 1
+    if fits and 2 * sent > tok_rows:
+        return dense(*args, cores=2)
+    return routed(*args)
 
 
 def solution(mesh):

time: 142 us -> 75.6 us (0.53); the launches traced: 139 us -> 75.3 us
  blocking collectives: 53.7 us -> 0 us
  starting transfers between devices: 5.2 us -> 19.2 us
  local copies, waits for them, and re-layouts: 20 us -> 7.44 us
  Pallas kernels: 0 us -> 8.47 us
  matrix products: 8.31 us -> 0 us
  waiting for transfers between devices: 45.8 us -> 37.5 us
  other arithmetic: 6.06 us -> 2.56 us
    all_to_all x1 -> x0, blocking collectives: 53.7 us -> none  [local(): lax.all_to_all(flat_out, ('node', 'rank'), split_axis=0, concat_axis=0, t...]
    all_to_all x1 -> x0, waiting for transfers between devices: 45.8 us -> none  [local(): lax.all_to_all(flat_back, ('node', 'rank'), split_axis=0, concat_axis=0,...]
    ppermute x0 -> x23, waiting for transfers between devices: none -> 37.5 us  [the longest x7 19.9 us: to_chip(): lax.ppermute(t, ('node', 'rank'), [(i, i ^ step) for i in range(n_node *...]
    ppermute x0 -> x23, starting transfers between devices: none -> 19.2 us  [the longest x7 9.13 us: to_chip(): lax.ppermute(t, ('node', 'rank'), [(i, i ^ step) for i in range(n_node *...]
    pallas_call x0 -> x3, Pallas kernels: none -> 8.47 us  [the longest x1 7.48 us: ffn(): pl.pallas_call(functools.partial(ffn_kernel, blocks=len(blocks), top=top)...]
    dot_general x2 -> x0, matrix products: 8.31 us -> none  [the longest x1 7.09 us: local(): jnp.einsum('secf,efd->secd', hidden, w_down, preferred_element_type=jnp.f...]
    reshape x4 -> x0, local copies, waits for them, and re-layouts: 8.07 us -> none  [the longest x1 3.98 us: local(): flat_back = result.reshape(n_dev, exp_dev * capacity, width)]
    unnamed x5 -> x7, local copies, waits for them, and re-layouts: 0.78 us -> 7.34 us
  transfers between devices with their start and end apart: 1 -> 23, of which waited for: 1 -> 12; matrix products, arithmetic and copies ran while one was open for 0% -> 1% of each run, Pallas kernels for 0% -> 0%
where the time goes in v1:
time: 75.6 us; the launch traced here: 75.3 us
  waiting for transfers between devices  37.5 us (50%)
  starting transfers between devices  19.2 us (25%)
  Pallas kernels  8.47 us (11%)
  local copies, waits for them, and re-layouts  7.44 us (10%)
  other arithmetic  2.56 us (3%)
    ppermute x7, waiting for transfers between devices, to_chip(): lax.ppermute(t, ('node', 'rank'), [(i, i ^ step) for i in range(n_node *...  19.9 us
    ppermute x7, starting transfers between devices, to_chip(): lax.ppermute(t, ('node', 'rank'), [(i, i ^ step) for i in range(n_node *...  9.13 us
    ppermute x4, waiting for transfers between devices, along_x(): return lax.ppermute(t, 'rank', [(i, i ^ dx * cores) for i in range(n_rank)])  7.77 us
    pallas_call x1, Pallas kernels, ffn(): pl.pallas_call(functools.partial(ffn_kernel, blocks=len(blocks), top=top)...  7.48 us
    unnamed x7, local copies, waits for them, and re-layouts  7.34 us
    ppermute x3, waiting for transfers between devices, along_z(): return lax.ppermute(t, 'node', [(i, i ^ dz) for i in range(n_node)])  6.8 us
    ppermute x4, starting transfers between devices, along_x(): return lax.ppermute(t, 'rank', [(i, i ^ dx * cores) for i in range(n_rank)])  5.01 us
    ppermute x3, starting transfers between devices, along_z(): return lax.ppermute(t, 'node', [(i, i ^ dz) for i in range(n_node)])  4.12 us
  transfers between devices with their start and end apart: 23, of which 12 were waited for; matrix products, arithmetic and copies ran while one was open for 1% of the time, Pallas kernels for 0%

profile of v1, /device:TPU:8, one launch (start us, length us, event | category | flops | bytes accessed | tf_op | source)
XLA Modules:
  0.0 75.3 jit_solution(18041212376057188844)
XLA Ops:
  0.0 0.7 convert.11
  0.7 0.1 copy.22
  0.8 0.8 %copy.18 = s32[32,10]{1,0:T(8,128)S(1)} copy(s32[32,10]{0,1:T(8,128)} %param.9) | data formatting | bytes 2560 | tf_op args[2]
  1.6 0.1 fusion.8
  1.7 0.9 %pad_maximum_fusion.refs_0_ = bf16[32,2176]{1,0:T(8,128)(2,1)S(1)} fusion(bf16[32,128]{1,0:T(8,128)(2,1)S(1)} %fusion.8, bf16[32,2048]{1,0:T(8,128)(2,1)} %param.7), kind=kLoop, calls=%fused_computation | loop fusion | flops 278528 | bytes 278528 | tf_op jit(solution)/shard_map/concatenate | solution.py:153
  2.6 1.6 %collective-permute-start.5 = (bf16[32,2176]{1,0:T(8,128)(2,1)S(1)}, bf16[32,2176]{1,0:T(8,128)(2,1)S(1)}, u32[]{:S(2)}, u32[]{:S(2)}) collective-permute-start(bf16[32,2176]{1,0:T(8,128)(2,1)S(1)} %pad_maximum_fusion.refs_0_), channel_id=1, source_target_pairs={{0,12},{4,8},{8,4},{12,0},{1,13},{5,9},{9,5},{13,1},{2,14},{6,10},... | collective-permute-start | bytes 417800 | tf_op jit(solution)/shard_map/ppermute | solution.py:134
  4.2 0.0 collective-permute-start.7
  4.3 1.2 %collective-permute-start.3 = (bf16[32,2176]{1,0:T(8,128)(2,1)S(1)}, bf16[32,2176]{1,0:T(8,128)(2,1)S(1)}, u32[]{:S(2)}, u32[]{:S(2)}) collective-permute-start(bf16[32,2176]{1,0:T(8,128)(2,1)S(1)} %pad_maximum_fusion.refs_0_), channel_id=1, source_target_pairs={{0,8},{4,12},{8,0},{12,4},{1,9},{5,13},{9,1},{13,5},{2,10},{6,14},... | collective-permute-start | bytes 417800 | tf_op jit(solution)/shard_map/ppermute | solution.py:134
  5.4 1.3 %collective-permute-start.1 = (bf16[32,2176]{1,0:T(8,128)(2,1)S(1)}, bf16[32,2176]{1,0:T(8,128)(2,1)S(1)}, u32[]{:S(2)}, u32[]{:S(2)}) collective-permute-start(bf16[32,2176]{1,0:T(8,128)(2,1)S(1)} %pad_maximum_fusion.refs_0_), channel_id=1, source_target_pairs={{0,4},{4,0},{8,12},{12,8},{1,5},{5,1},{9,13},{13,9},{2,6},{6,2},{1... | collective-permute-start | bytes 417800 | tf_op jit(solution)/shard_map/ppermute | solution.py:134
  6.7 1.5 %collective-permute-start = (bf16[32,2176]{1,0:T(8,128)(2,1)S(1)}, bf16[32,2176]{1,0:T(8,128)(2,1)S(1)}, u32[]{:S(2)}, u32[]{:S(2)}) collective-permute-start(bf16[32,2176]{1,0:T(8,128)(2,1)S(1)} %pad_maximum_fusion.refs_0_), channel_id=1, source_target_pairs={{0,2},{1,3},{2,0},{3,1},{4,6},{5,7},{6,4},{7,5},{8,10},{9,11},{10,... | collective-permute-start | bytes 417800 | tf_op jit(solution)/shard_map/ppermute | solution.py:137
  8.2 6.8 %collective-permute-done.5.refs_6_ = bf16[32,2176]{1,0:T(8,128)(2,1)S(1)} collective-permute-done((bf16[32,2176]{1,0:T(8,128)(2,1)S(1)}, bf16[32,2176]{1,0:T(8,128)(2,1)S(1)}, u32[]{:S(2)}, u32[]{:S(2)}) %collective-permute-start.5) | collective-permute-done | bytes 139296 | tf_op jit(solution)/shard_map/ppermute | solution.py:134
  15.0 0.0 collective-permute-start.13
  15.0 0.0 collective-permute-done.7.refs_8_
  15.0 1.5 %collective-permute-start.6 = (bf16[32,2176]{1,0:T(8,128)(2,1)S(1)}, bf16[32,2176]{1,0:T(8,128)(2,1)S(1)}, u32[]{:S(2)}, u32[]{:S(2)}) collective-permute-start(bf16[32,2176]{1,0:T(8,128)(2,1)S(1)} %collective-permute-done.5.refs_6_), channel_id=1, source_target_pairs={{0,2},{1,3},{2,0},{3,1},{4,6},{5,7},{6,4},{7,5},{8,10},{9,11},{10,... | collective-permute-start | bytes 417800 | tf_op jit(solution)/shard_map/ppermute | solution.py:137
  16.5 0.0 collective-permute-done.3.refs_4_
  16.5 0.2 collective-permute-start.11
  16.7 0.0 collective-permute-done.1.refs_2_
  16.7 0.9 %collective-permute-start.4 = (bf16[32,2176]{1,0:T(8,128)(2,1)S(1)}, bf16[32,2176]{1,0:T(8,128)(2,1)S(1)}, u32[]{:S(2)}, u32[]{:S(2)}) collective-permute-start(bf16[32,2176]{1,0:T(8,128)(2,1)S(1)} %collective-permute-done.3.refs_4_), channel_id=1, source_target_pairs={{0,2},{1,3},{2,0},{3,1},{4,6},{5,7},{6,4},{7,5},{8,10},{9,11},{10,... | collective-permute-start | bytes 417800 | tf_op jit(solution)/shard_map/ppermute | solution.py:137
  17.6 0.0 collective-permute-done.refs_1_
  17.6 1.1 %collective-permute-start.2 = (bf16[32,2176]{1,0:T(8,128)(2,1)S(1)}, bf16[32,2176]{1,0:T(8,128)(2,1)S(1)}, u32[]{:S(2)}, u32[]{:S(2)}) collective-permute-start(bf16[32,2176]{1,0:T(8,128)(2,1)S(1)} %collective-permute-done.1.refs_2_), channel_id=1, source_target_pairs={{0,2},{1,3},{2,0},{3,1},{4,6},{5,7},{6,4},{7,5},{8,10},{9,11},{10,... | collective-permute-start | bytes 417800 | tf_op jit(solution)/shard_map/ppermute | solution.py:137
  18.8 2.7 %collective-permute-done.6.refs_7_ = bf16[32,2176]{1,0:T(8,128)(2,1)S(1)} collective-permute-done((bf16[32,2176]{1,0:T(8,128)(2,1)S(1)}, bf16[32,2176]{1,0:T(8,128)(2,1)S(1)}, u32[]{:S(2)}, u32[]{:S(2)}) %collective-permute-start.6) | collective-permute-done | bytes 139296 | tf_op jit(solution)/shard_map/ppermute | solution.py:137
  21.5 0.0 collective-permute-start.8
  21.5 0.0 collective-permute-done.11.refs_12_
  21.5 0.5 collective-permute-start.14
  22.0 2.5 %collective-permute-done.4.refs_5_ = bf16[32,2176]{1,0:T(8,128)(2,1)S(1)} collective-permute-done((bf16[32,2176]{1,0:T(8,128)(2,1)S(1)}, bf16[32,2176]{1,0:T(8,128)(2,1)S(1)}, u32[]{:S(2)}, u32[]{:S(2)}) %collective-permute-start.4) | collective-permute-done | bytes 139296 | tf_op jit(solution)/shard_map/ppermute | solution.py:137
  24.5 2.6 %collective-permute-done.2.refs_3_ = bf16[32,2176]{1,0:T(8,128)(2,1)S(1)} collective-permute-done((bf16[32,2176]{1,0:T(8,128)(2,1)S(1)}, bf16[32,2176]{1,0:T(8,128)(2,1)S(1)}, u32[]{:S(2)}, u32[]{:S(2)}) %collective-permute-start.2) | collective-permute-done | bytes 139296 | tf_op jit(solution)/shard_map/ppermute | solution.py:137
  27.1 0.8 %fusion.9.mine_ref = s32[2]{0:T(128)S(1)} fusion(s32[32]{0:T(128)} %param.10, s32[2]{0:T(128)S(1)} %iota_add_fusion), kind=kLoop, calls=%fused_computation.18 | loop fusion | flops 190 | bytes 144 | tf_op jit(solution)/shard_map/reduce_sum | solution.py:149
  28.0 0.5 collective-permute-done.10.refs_11_
  28.4 2.2 %copy-done = bf16[2,2048,512]{2,1,0:T(8,128)(2,1)S(1)} copy-done((bf16[2,2048,512]{2,1,0:T(8,128)(2,1)S(1)}, bf16[2,2048,512]{2,1,0:T(8,128)(2,1)}, u32[]{:S(2)}) %copy-start) | copy-done | bytes 4194328
  30.6 2.2 %copy-done.1 = bf16[2,2048,512]{2,1,0:T(8,128)(2,1)S(1)} copy-done((bf16[2,2048,512]{2,1,0:T(8,128)(2,1)S(1)}, bf16[2,2048,512]{2,1,0:T(8,128)(2,1)}, u32[]{:S(2)}) %copy-start.1) | copy-done | bytes 4194328
  32.8 2.2 %copy-done.2 = bf16[2,512,2048]{2,1,0:T(8,128)(2,1)S(1)} copy-done((bf16[2,512,2048]{2,1,0:T(8,128)(2,1)S(1)}, bf16[2,512,2048]{2,1,0:T(8,128)(2,1)}, u32[]{:S(2)}) %copy-start.2) | copy-done | bytes 4194328
  35.0 7.5 %ffn_512.1 = (f32[256,2048]{1,0:T(8,128)S(1)}, bf16[256,2048]{1,0:T(8,128)(2,1)S(1)}) custom-call(s32[2]{0:T(128)S(1)} %fusion.9.mine_ref, bf16[32,2176]{1,0:T(8,128)(2,1)S(1)} %pad_maximum_fusion.refs_0_, bf16[32,2176]{1,0:T(8,128)(2,1)S(1)} %collective-permute-done.refs_1_, bf16[32,2176]{1,0:T(8,128)(2,1)S(1)} %collective-permute-done.1.refs_2_, ...), custom_call_target="tpu_custom_call" | custom-call | tf_op jit(solution)/shard_map/ffn_512/pallas_call | solution.py:75
  42.5 0.2 collective-permute-start.15
  42.7 2.5 %collective-permute-done.15.other_ref = bf16[256,2048]{1,0:T(8,128)(2,1)S(1)} collective-permute-done((bf16[256,2048]{1,0:T(8,128)(2,1)S(1)}, bf16[256,2048]{1,0:T(8,128)(2,1)S(1)}, u32[]{:S(2)}, u32[]{:S(2)}) %collective-permute-start.15) | collective-permute-done | bytes 1048608 | tf_op jit(solution)/shard_map/ppermute | solution.py:144
  45.2 0.2 join.1
  45.4 1.6 %collective-permute-start.16 = (bf16[32,2048]{1,0:T(8,128)(2,1)S(1)}, bf16[32,2048]{1,0:T(8,128)(2,1)S(1)}, u32[]{:S(2)}, u32[]{:S(2)}) collective-permute-start(bf16[32,2048]{1,0:T(8,128)(2,1)S(1)} %get-tuple-element.18), channel_id=1, source_target_pairs={{0,2},{1,3},{2,0},{3,1},{4,6},{5,7},{6,4},{7,5},{8,10},{9,11},{10,... | collective-permute-start | bytes 393224 | tf_op jit(solution)/shard_map/ppermute | solution.py:141
  47.0 0.5 collective-permute-start.17
  47.5 1.5 %collective-permute-start.18 = (bf16[32,2048]{1,0:T(8,128)(2,1)S(1)}, bf16[32,2048]{1,0:T(8,128)(2,1)S(1)}, u32[]{:S(2)}, u32[]{:S(2)}) collective-permute-start(bf16[32,2048]{1,0:T(8,128)(2,1)S(1)} %get-tuple-element.20), channel_id=1, source_target_pairs={{0,6},{1,7},{2,4},{3,5},{4,2},{5,3},{6,0},{7,1},{8,14},{9,15},{10,... | collective-permute-start | bytes 393224 | tf_op jit(solution)/shard_map/ppermute | solution.py:141
  49.0 1.5 %collective-permute-start.19 = (bf16[32,2048]{1,0:T(8,128)(2,1)S(1)}, bf16[32,2048]{1,0:T(8,128)(2,1)S(1)}, u32[]{:S(2)}, u32[]{:S(2)}) collective-permute-start(bf16[32,2048]{1,0:T(8,128)(2,1)S(1)} %get-tuple-element.21), channel_id=1, source_target_pairs={{0,8},{1,9},{2,10},{3,11},{4,12},{5,13},{6,14},{7,15},{8,0},{9,1},... | collective-permute-start | bytes 393224 | tf_op jit(solution)/shard_map/ppermute | solution.py:141
  50.5 2.3 %collective-permute-start.20 = (bf16[32,2048]{1,0:T(8,128)(2,1)S(1)}, bf16[32,2048]{1,0:T(8,128)(2,1)S(1)}, u32[]{:S(2)}, u32[]{:S(2)}) collective-permute-start(bf16[32,2048]{1,0:T(8,128)(2,1)S(1)} %get-tuple-element.22), channel_id=1, source_target_pairs={{0,10},{1,11},{2,8},{3,9},{4,14},{5,15},{6,12},{7,13},{8,2},{9,3},... | collective-permute-start | bytes 393224 | tf_op jit(solution)/shard_map/ppermute | solution.py:141
  52.8 1.7 %collective-permute-start.21 = (bf16[32,2048]{1,0:T(8,128)(2,1)S(1)}, bf16[32,2048]{1,0:T(8,128)(2,1)S(1)}, u32[]{:S(2)}, u32[]{:S(2)}) collective-permute-start(bf16[32,2048]{1,0:T(8,128)(2,1)S(1)} %get-tuple-element.23), channel_id=1, source_target_pairs={{0,12},{1,13},{2,14},{3,15},{4,8},{5,9},{6,10},{7,11},{8,4},{9,5},... | collective-permute-start | bytes 393224 | tf_op jit(solution)/shard_map/ppermute | solution.py:141
  54.6 0.9 %collective-permute-done.17.refs_2_ = bf16[32,2048]{1,0:T(8,128)(2,1)S(1)} collective-permute-done((bf16[32,2048]{1,0:T(8,128)(2,1)S(1)}, bf16[32,2048]{1,0:T(8,128)(2,1)S(1)}, u32[]{:S(2)}, u32[]{:S(2)}) %collective-permute-start.17) | collective-permute-done | bytes 131104 | tf_op jit(solution)/shard_map/ppermute | solution.py:141
  55.5 2.2 %collective-permute-done.18.refs_3_ = bf16[32,2048]{1,0:T(8,128)(2,1)S(1)} collective-permute-done((bf16[32,2048]{1,0:T(8,128)(2,1)S(1)}, bf16[32,2048]{1,0:T(8,128)(2,1)S(1)}, u32[]{:S(2)}, u32[]{:S(2)}) %collective-permute-start.18) | collective-permute-done | bytes 131104 | tf_op jit(solution)/shard_map/ppermute | solution.py:141
  57.6 2.6 %collective-permute-done.19.refs_4_ = bf16[32,2048]{1,0:T(8,128)(2,1)S(1)} collective-permute-done((bf16[32,2048]{1,0:T(8,128)(2,1)S(1)}, bf16[32,2048]{1,0:T(8,128)(2,1)S(1)}, u32[]{:S(2)}, u32[]{:S(2)}) %collective-permute-start.19) | collective-permute-done | bytes 131104 | tf_op jit(solution)/shard_map/ppermute | solution.py:141
  60.2 7.9 %collective-permute-done.20.refs_5_ = bf16[32,2048]{1,0:T(8,128)(2,1)S(1)} collective-permute-done((bf16[32,2048]{1,0:T(8,128)(2,1)S(1)}, bf16[32,2048]{1,0:T(8,128)(2,1)S(1)}, u32[]{:S(2)}, u32[]{:S(2)}) %collective-permute-start.20) | collective-permute-done | bytes 131104 | tf_op jit(solution)/shard_map/ppermute | solution.py:141
  68.1 4.3 %collective-permute-done.21.refs_6_ = bf16[32,2048]{1,0:T(8,128)(2,1)S(1)} collective-permute-done((bf16[32,2048]{1,0:T(8,128)(2,1)S(1)}, bf16[32,2048]{1,0:T(8,128)(2,1)S(1)}, u32[]{:S(2)}, u32[]{:S(2)}) %collective-permute-start.21) | collective-permute-done | bytes 131104 | tf_op jit(solution)/shard_map/ppermute | solution.py:141
  72.4 2.1 %collective-permute-done.22.refs_7_ = bf16[32,2048]{1,0:T(8,128)(2,1)S(1)} collective-permute-done((bf16[32,2048]{1,0:T(8,128)(2,1)S(1)}, bf16[32,2048]{1,0:T(8,128)(2,1)S(1)}, u32[]{:S(2)}, u32[]{:S(2)}) %collective-permute-start.22) | collective-permute-done | bytes 131104 | tf_op jit(solution)/shard_map/ppermute | solution.py:141
  74.5 0.8 %total.1 = bf16[32,2048]{1,0:T(8,128)(2,1)} custom-call(f32[32,2048]{1,0:T(8,128)S(1)} %get-tuple-element.17.refs_0_, bf16[32,2048]{1,0:T(8,128)(2,1)S(1)} %collective-permute-done.16.refs_1_, bf16[32,2048]{1,0:T(8,128)(2,1)S(1)} %collective-permute-done.17.refs_2_, bf16[32,2048]{1,0:T(8,128)(2,1)S(1)} %collective-permute-done.18.refs_3_, ...), custom_call_target="tpu_custom_call" | custom-call | tf_op jit(solution)/shard_map/total/pallas_call | solution.py:116
  (15 shorter events, 0.1 us)
Async XLA Ops:
  2.6 12.4 %collective-permute-start.5 = (bf16[32,2176]{1,0:T(8,128)(2,1)S(1)}, bf16[32,2176]{1,0:T(8,128)(2,1)S(1)}, u32[]{:S(2)}, u32[]{:S(2)}) collective-permute-start(bf16[32,2176]{1,0:T(8,128)(2,1)S(1)} %pad_maximum_fusion.refs_0_), channel_id=1, source_target_pairs={{0,12},{4,8},{8,4},{12,0},{1,13},{5,9},{9,5},{13,1},{2,14},{6,10},... | collective-permute-start | bytes 417800 | tf_op jit(solution)/shard_map/ppermute | solution.py:134
  4.2 10.8 %collective-permute-start.7 = (bf16[32,2176]{1,0:T(8,128)(2,1)S(1)}, bf16[32,2176]{1,0:T(8,128)(2,1)S(1)}, u32[]{:S(2)}, u32[]{:S(2)}) collective-permute-start(bf16[32,2176]{1,0:T(8,128)(2,1)S(1)} %pad_maximum_fusion.refs_0_), channel_id=1, source_target_pairs={{0,1},{1,0},{2,3},{3,2},{4,5},{5,4},{6,7},{7,6},{8,9},{9,8},{10,11... | collective-permute-start | bytes 417800 | tf_op jit(solution)/shard_map/ppermute | solution.py:144
  4.3 12.3 %collective-permute-start.3 = (bf16[32,2176]{1,0:T(8,128)(2,1)S(1)}, bf16[32,2176]{1,0:T(8,128)(2,1)S(1)}, u32[]{:S(2)}, u32[]{:S(2)}) collective-permute-start(bf16[32,2176]{1,0:T(8,128)(2,1)S(1)} %pad_maximum_fusion.refs_0_), channel_id=1, source_target_pairs={{0,8},{4,12},{8,0},{12,4},{1,9},{5,13},{9,1},{13,5},{2,10},{6,14},... | collective-permute-start | bytes 417800 | tf_op jit(solution)/shard_map/ppermute | solution.py:134
  5.4 11.3 %collective-permute-start.1 = (bf16[32,2176]{1,0:T(8,128)(2,1)S(1)}, bf16[32,2176]{1,0:T(8,128)(2,1)S(1)}, u32[]{:S(2)}, u32[]{:S(2)}) collective-permute-start(bf16[32,2176]{1,0:T(8,128)(2,1)S(1)} %pad_maximum_fusion.refs_0_), channel_id=1, source_target_pairs={{0,4},{4,0},{8,12},{12,8},{1,5},{5,1},{9,13},{13,9},{2,6},{6,2},{1... | collective-permute-start | bytes 417800 | tf_op jit(solution)/shard_map/ppermute | solution.py:134
  6.7 10.9 %collective-permute-start = (bf16[32,2176]{1,0:T(8,128)(2,1)S(1)}, bf16[32,2176]{1,0:T(8,128)(2,1)S(1)}, u32[]{:S(2)}, u32[]{:S(2)}) collective-permute-start(bf16[32,2176]{1,0:T(8,128)(2,1)S(1)} %pad_maximum_fusion.refs_0_), channel_id=1, source_target_pairs={{0,2},{1,3},{2,0},{3,1},{4,6},{5,7},{6,4},{7,5},{8,10},{9,11},{10,... | collective-permute-start | bytes 417800 | tf_op jit(solution)/shard_map/ppermute | solution.py:137
  15.0 3.8 %collective-permute-start.13 = (bf16[32,2176]{1,0:T(8,128)(2,1)S(1)}, bf16[32,2176]{1,0:T(8,128)(2,1)S(1)}, u32[]{:S(2)}, u32[]{:S(2)}) collective-permute-start(bf16[32,2176]{1,0:T(8,128)(2,1)S(1)} %collective-permute-done.5.refs_6_), channel_id=1, source_target_pairs={{0,1},{1,0},{2,3},{3,2},{4,5},{5,4},{6,7},{7,6},{8,9},{9,8},{10,11... | collective-permute-start | bytes 417800 | tf_op jit(solution)/shard_map/ppermute | solution.py:144
  15.0 6.5 %collective-permute-start.6 = (bf16[32,2176]{1,0:T(8,128)(2,1)S(1)}, bf16[32,2176]{1,0:T(8,128)(2,1)S(1)}, u32[]{:S(2)}, u32[]{:S(2)}) collective-permute-start(bf16[32,2176]{1,0:T(8,128)(2,1)S(1)} %collective-permute-done.5.refs_6_), channel_id=1, source_target_pairs={{0,2},{1,3},{2,0},{3,1},{4,6},{5,7},{6,4},{7,5},{8,10},{9,11},{10,... | collective-permute-start | bytes 417800 | tf_op jit(solution)/shard_map/ppermute | solution.py:137
  16.5 5.0 %collective-permute-start.11 = (bf16[32,2176]{1,0:T(8,128)(2,1)S(1)}, bf16[32,2176]{1,0:T(8,128)(2,1)S(1)}, u32[]{:S(2)}, u32[]{:S(2)}) collective-permute-start(bf16[32,2176]{1,0:T(8,128)(2,1)S(1)} %collective-permute-done.3.refs_4_), channel_id=1, source_target_pairs={{0,1},{1,0},{2,3},{3,2},{4,5},{5,4},{6,7},{7,6},{8,9},{9,8},{10,11... | collective-permute-start | bytes 417800 | tf_op jit(solution)/shard_map/ppermute | solution.py:144
  16.7 7.7 %collective-permute-start.4 = (bf16[32,2176]{1,0:T(8,128)(2,1)S(1)}, bf16[32,2176]{1,0:T(8,128)(2,1)S(1)}, u32[]{:S(2)}, u32[]{:S(2)}) collective-permute-start(bf16[32,2176]{1,0:T(8,128)(2,1)S(1)} %collective-permute-done.3.refs_4_), channel_id=1, source_target_pairs={{0,2},{1,3},{2,0},{3,1},{4,6},{5,7},{6,4},{7,5},{8,10},{9,11},{10,... | collective-permute-start | bytes 417800 | tf_op jit(solution)/shard_map/ppermute | solution.py:137
  17.6 9.4 %collective-permute-start.2 = (bf16[32,2176]{1,0:T(8,128)(2,1)S(1)}, bf16[32,2176]{1,0:T(8,128)(2,1)S(1)}, u32[]{:S(2)}, u32[]{:S(2)}) collective-permute-start(bf16[32,2176]{1,0:T(8,128)(2,1)S(1)} %collective-permute-done.1.refs_2_), channel_id=1, source_target_pairs={{0,2},{1,3},{2,0},{3,1},{4,6},{5,7},{6,4},{7,5},{8,10},{9,11},{10,... | collective-permute-start | bytes 417800 | tf_op jit(solution)/shard_map/ppermute | solution.py:137
  18.8 9.1 %collective-permute-start.9 = (bf16[32,2176]{1,0:T(8,128)(2,1)S(1)}, bf16[32,2176]{1,0:T(8,128)(2,1)S(1)}, u32[]{:S(2)}, u32[]{:S(2)}) collective-permute-start(bf16[32,2176]{1,0:T(8,128)(2,1)S(1)} %collective-permute-done.1.refs_2_), channel_id=1, source_target_pairs={{0,1},{1,0},{2,3},{3,2},{4,5},{5,4},{6,7},{7,6},{8,9},{9,8},{10,11... | collective-permute-start | bytes 417800 | tf_op jit(solution)/shard_map/ppermute | solution.py:144
  21.5 6.4 %collective-permute-start.8 = (bf16[32,2176]{1,0:T(8,128)(2,1)S(1)}, bf16[32,2176]{1,0:T(8,128)(2,1)S(1)}, u32[]{:S(2)}, u32[]{:S(2)}) collective-permute-start(bf16[32,2176]{1,0:T(8,128)(2,1)S(1)} %collective-permute-done.refs_1_), channel_id=1, source_target_pairs={{0,1},{1,0},{2,3},{3,2},{4,5},{5,4},{6,7},{7,6},{8,9},{9,8},{10,11... | collective-permute-start | bytes 417800 | tf_op jit(solution)/shard_map/ppermute | solution.py:144
  21.5 6.4 %collective-permute-start.14 = (bf16[32,2176]{1,0:T(8,128)(2,1)S(1)}, bf16[32,2176]{1,0:T(8,128)(2,1)S(1)}, u32[]{:S(2)}, u32[]{:S(2)}) collective-permute-start(bf16[32,2176]{1,0:T(8,128)(2,1)S(1)} %collective-permute-done.6.refs_7_), channel_id=1, source_target_pairs={{0,1},{1,0},{2,3},{3,2},{4,5},{5,4},{6,7},{7,6},{8,9},{9,8},{10,11... | collective-permute-start | bytes 417800 | tf_op jit(solution)/shard_map/ppermute | solution.py:144
  24.5 3.5 %collective-permute-start.12 = (bf16[32,2176]{1,0:T(8,128)(2,1)S(1)}, bf16[32,2176]{1,0:T(8,128)(2,1)S(1)}, u32[]{:S(2)}, u32[]{:S(2)}) collective-permute-start(bf16[32,2176]{1,0:T(8,128)(2,1)S(1)} %collective-permute-done.4.refs_5_), channel_id=1, source_target_pairs={{0,1},{1,0},{2,3},{3,2},{4,5},{5,4},{6,7},{7,6},{8,9},{9,8},{10,11... | collective-permute-start | bytes 417800 | tf_op jit(solution)/shard_map/ppermute | solution.py:144
  27.1 1.4 %collective-permute-start.10 = (bf16[32,2176]{1,0:T(8,128)(2,1)S(1)}, bf16[32,2176]{1,0:T(8,128)(2,1)S(1)}, u32[]{:S(2)}, u32[]{:S(2)}) collective-permute-start(bf16[32,2176]{1,0:T(8,128)(2,1)S(1)} %collective-permute-done.2.refs_3_), channel_id=1, source_target_pairs={{0,1},{1,0},{2,3},{3,2},{4,5},{5,4},{6,7},{7,6},{8,9},{9,8},{10,11... | collective-permute-start | bytes 417800 | tf_op jit(solution)/shard_map/ppermute | solution.py:144
  28.4 2.2 %copy-start = (bf16[2,2048,512]{2,1,0:T(8,128)(2,1)S(1)}, bf16[2,2048,512]{2,1,0:T(8,128)(2,1)}, u32[]{:S(2)}) copy-start(bf16[2,2048,512]{2,1,0:T(8,128)(2,1)} %refs_16_.1) | copy-start | bytes 12582916
  30.6 2.2 %copy-start.1 = (bf16[2,2048,512]{2,1,0:T(8,128)(2,1)S(1)}, bf16[2,2048,512]{2,1,0:T(8,128)(2,1)}, u32[]{:S(2)}) copy-start(bf16[2,2048,512]{2,1,0:T(8,128)(2,1)} %refs_17_.1) | copy-start | bytes 12582916
  32.8 2.2 %copy-start.2 = (bf16[2,512,2048]{2,1,0:T(8,128)(2,1)S(1)}, bf16[2,512,2048]{2,1,0:T(8,128)(2,1)}, u32[]{:S(2)}) copy-start(bf16[2,512,2048]{2,1,0:T(8,128)(2,1)} %refs_18_.1) | copy-start | bytes 12582916
  42.5 2.7 %collective-permute-start.15 = (bf16[256,2048]{1,0:T(8,128)(2,1)S(1)}, bf16[256,2048]{1,0:T(8,128)(2,1)S(1)}, u32[]{:S(2)}, u32[]{:S(2)}) collective-permute-start(bf16[256,2048]{1,0:T(8,128)(2,1)S(1)} %get-tuple-element.16), channel_id=1, source_target_pairs={{0,1},{1,0},{2,3},{3,2},{4,5},{5,4},{6,7},{7,6},{8,9},{9,8},{10,11... | collective-permute-start | bytes 3145736 | tf_op jit(solution)/shard_map/ppermute | solution.py:144
  45.4 7.4 %collective-permute-start.16 = (bf16[32,2048]{1,0:T(8,128)(2,1)S(1)}, bf16[32,2048]{1,0:T(8,128)(2,1)S(1)}, u32[]{:S(2)}, u32[]{:S(2)}) collective-permute-start(bf16[32,2048]{1,0:T(8,128)(2,1)S(1)} %get-tuple-element.18), channel_id=1, source_target_pairs={{0,2},{1,3},{2,0},{3,1},{4,6},{5,7},{6,4},{7,5},{8,10},{9,11},{10,... | collective-permute-start | bytes 393224 | tf_op jit(solution)/shard_map/ppermute | solution.py:141
  47.0 8.5 %collective-permute-start.17 = (bf16[32,2048]{1,0:T(8,128)(2,1)S(1)}, bf16[32,2048]{1,0:T(8,128)(2,1)S(1)}, u32[]{:S(2)}, u32[]{:S(2)}) collective-permute-start(bf16[32,2048]{1,0:T(8,128)(2,1)S(1)} %get-tuple-element.19), channel_id=1, source_target_pairs={{0,4},{1,5},{2,6},{3,7},{4,0},{5,1},{6,2},{7,3},{8,12},{9,13},{10,... | collective-permute-start | bytes 393224 | tf_op jit(solution)/shard_map/ppermute | solution.py:141
  47.5 10.1 %collective-permute-start.18 = (bf16[32,2048]{1,0:T(8,128)(2,1)S(1)}, bf16[32,2048]{1,0:T(8,128)(2,1)S(1)}, u32[]{:S(2)}, u32[]{:S(2)}) collective-permute-start(bf16[32,2048]{1,0:T(8,128)(2,1)S(1)} %get-tuple-element.20), channel_id=1, source_target_pairs={{0,6},{1,7},{2,4},{3,5},{4,2},{5,3},{6,0},{7,1},{8,14},{9,15},{10,... | collective-permute-start | bytes 393224 | tf_op jit(solution)/shard_map/ppermute | solution.py:141
  49.0 11.3 %collective-permute-start.19 = (bf16[32,2048]{1,0:T(8,128)(2,1)S(1)}, bf16[32,2048]{1,0:T(8,128)(2,1)S(1)}, u32[]{:S(2)}, u32[]{:S(2)}) collective-permute-start(bf16[32,2048]{1,0:T(8,128)(2,1)S(1)} %get-tuple-element.21), channel_id=1, source_target_pairs={{0,8},{1,9},{2,10},{3,11},{4,12},{5,13},{6,14},{7,15},{8,0},{9,1},... | collective-permute-start | bytes 393224 | tf_op jit(solution)/shard_map/ppermute | solution.py:141
  50.5 17.6 %collective-permute-start.20 = (bf16[32,2048]{1,0:T(8,128)(2,1)S(1)}, bf16[32,2048]{1,0:T(8,128)(2,1)S(1)}, u32[]{:S(2)}, u32[]{:S(2)}) collective-permute-start(bf16[32,2048]{1,0:T(8,128)(2,1)S(1)} %get-tuple-element.22), channel_id=1, source_target_pairs={{0,10},{1,11},{2,8},{3,9},{4,14},{5,15},{6,12},{7,13},{8,2},{9,3},... | collective-permute-start | bytes 393224 | tf_op jit(solution)/shard_map/ppermute | solution.py:141
  52.8 19.6 %collective-permute-start.21 = (bf16[32,2048]{1,0:T(8,128)(2,1)S(1)}, bf16[32,2048]{1,0:T(8,128)(2,1)S(1)}, u32[]{:S(2)}, u32[]{:S(2)}) collective-permute-start(bf16[32,2048]{1,0:T(8,128)(2,1)S(1)} %get-tuple-element.23), channel_id=1, source_target_pairs={{0,12},{1,13},{2,14},{3,15},{4,8},{5,9},{6,10},{7,11},{8,4},{9,5},... | collective-permute-start | bytes 393224 | tf_op jit(solution)/shard_map/ppermute | solution.py:141
  55.5 19.0 %collective-permute-start.22 = (bf16[32,2048]{1,0:T(8,128)(2,1)S(1)}, bf16[32,2048]{1,0:T(8,128)(2,1)S(1)}, u32[]{:S(2)}, u32[]{:S(2)}) collective-permute-start(bf16[32,2048]{1,0:T(8,128)(2,1)S(1)} %get-tuple-element.24), channel_id=1, source_target_pairs={{0,14},{1,15},{2,12},{3,13},{4,10},{5,11},{6,8},{7,9},{8,6},{9,7},... | collective-permute-start | bytes 393224 | tf_op jit(solution)/shard_map/ppermute | solution.py:141

commit v2 on v1

--- a/solution.py
+++ b/solution.py
@@ -9,7 +9,11 @@
 
 LANES = 128
 VMEM = pl.BlockSpec(memory_space=pltpu.VMEM)
-SMEM = pl.BlockSpec(memory_space=pltpu.SMEM)
+IN_HBM = pl.BlockSpec(memory_space=pltpu.HBM)
+
+
+def keep_in_hbm(x):
+    return pltpu.with_memory_space_constraint(x, pltpu.HBM)
 
 
 def capacity_of(tok_rows, top, slots):
@@ -47,43 +51,127 @@
     return mixed.astype(jnp.bfloat16)
 
 
-def ffn_kernel(mine_ref, *refs, blocks, top):
-    ins, (wg_ref, wu_ref, wd_ref, near_ref, far_ref, rows) = refs[:blocks], refs[blocks:]
-    width = near_ref.shape[1]
+def rounded(n):
+    return -(-n // 8) * 8
+
+
+def prepare_kernel(tokens_in, ids_in, weights_in, plan_in, rows_ref, mine_ref, ids, weights, meta, plan, sems, *, exp_dev, n_rank):
+    width, top = tokens_in.shape[1], ids.shape[0]
+    moves = ((tokens_in, rows_ref.at[:, :width]), (ids_in, ids), (weights_in, weights), (plan_in, plan))
+    copies = [pltpu.make_async_copy(a, b, sems.at[i]) for i, (a, b) in enumerate(moves)]
+    for copy in copies:
+        copy.start()
+    device = lax.axis_index("node") * n_rank + lax.axis_index("rank")
+    copies[3].wait()
+    found = [jnp.int32(0)] * exp_dev
+    for expert in range(plan.shape[0]):
+        slot = plan[expert]
+        found = [jnp.where(slot == device * exp_dev + j, expert, f) for j, f in enumerate(found)]
+    lane = lax.broadcasted_iota(jnp.int32, mine_ref.shape, 1)
+    mine = jnp.zeros(mine_ref.shape, jnp.int32)
+    for j, f in enumerate(found):
+        mine = jnp.where(lane == j, f, mine)
+    mine_ref[...] = mine.astype(jnp.float32)
+    copies[1].wait()
+    copies[2].wait()
+    w = weights[...]
+    meta[...] = jnp.zeros(meta.shape, jnp.float32)
+    for i, part in enumerate((ids[...], w // 256, w % 256)):
+        meta[pl.ds(i * rounded(top), top), :] = part.astype(jnp.float32)
+    rows_ref[:, width:] = meta[...].T.astype(rows_ref.dtype)
+    copies[0].wait()
+
+
+def prepare(tokens, expert_ids, combine_weights, slot_plan, exp_dev, n_rank):
+    tok_rows, width = tokens.shape
+    args = (tokens, expert_ids.T, combine_weights.T, slot_plan)
+    return pl.pallas_call(
+        functools.partial(prepare_kernel, exp_dev=exp_dev, n_rank=n_rank),
+        out_shape=(
+            jax.ShapeDtypeStruct((tok_rows, width + LANES), jnp.bfloat16),
+            jax.ShapeDtypeStruct((8, LANES), jnp.float32),
+        ),
+        in_specs=[IN_HBM] * 4,
+        out_specs=(VMEM, VMEM),
+        scratch_shapes=[
+            pltpu.VMEM(args[1].shape, jnp.int32),
+            pltpu.VMEM(args[2].shape, jnp.int32),
+            pltpu.VMEM((LANES, tok_rows), jnp.float32),
+            pltpu.SMEM(slot_plan.shape, jnp.int32),
+            pltpu.SemaphoreType.DMA((4,)),
+        ],
+        compiler_params=pltpu.CompilerParams(vmem_limit_bytes=8 << 20),
+        name="prepare",
+    )(*map(keep_in_hbm, args))
+
+
+def experts(x, meta, mine_ref, wg_ref, wu_ref, wd_ref, top, ready=lambda e, i: None):
+    gap = rounded(top)
+    ids, high, low = (meta[:, i * gap : i * gap + top] for i in range(3))
+    weight = (high * 256.0 + low) * (1.0 / 65536.0)
+    total = None
+    for e in range(wg_ref.shape[0]):
+        scale = jnp.sum(jnp.where(ids == mine_ref[0:1, e : e + 1], weight, 0.0), axis=1, keepdims=True)
+        ready(e, 0)
+        gate = jnp.dot(x, wg_ref[e], preferred_element_type=jnp.float32)
+        ready(e, 1)
+        up = jnp.dot(x, wu_ref[e], preferred_element_type=jnp.float32)
+        hidden = (gate / (1.0 + jnp.exp(-gate)) * up).astype(jnp.bfloat16)
+        ready(e, 2)
+        part = jnp.dot(hidden, wd_ref[e], preferred_element_type=jnp.float32) * scale
+        total = part if total is None else total + part
+    return total
+
+
+def gather_rows(ins, rows, width):
     step = ins[0].shape[0]
     for i, ref in enumerate(ins):
         rows[pl.ds(i * step, step), :] = ref[...]
-    x = rows[:, :width]
-    meta = rows[:, width:].astype(jnp.float32)
-    ids, weight = meta[:, :top], (meta[:, top : 2 * top] * 256.0 + meta[:, 2 * top : 3 * top]) * (1.0 / 65536.0)
-    total = None
-    for e in range(wg_ref.shape[0]):
-        scale = jnp.sum(jnp.where(ids == mine_ref[e].astype(jnp.float32), weight, 0.0), axis=1, keepdims=True)
-        gate = jnp.dot(x, wg_ref[e], preferred_element_type=jnp.float32)
-        up = jnp.dot(x, wu_ref[e], preferred_element_type=jnp.float32)
-        hidden = (gate / (1.0 + jnp.exp(-gate)) * up).astype(jnp.bfloat16)
-        part = jnp.dot(hidden, wd_ref[e], preferred_element_type=jnp.float32) * scale
-        total = part if total is None else total + part
+    return rows[:, :width], rows[:, width:].astype(jnp.float32)
+
+
+def ffn_kernel(mine_ref, *refs, blocks, top):
+    ins, (wg_ref, wu_ref, wd_ref, near_ref, far_ref, rows) = refs[:blocks], refs[blocks:]
+    x, meta = gather_rows(ins, rows, near_ref.shape[1])
+    total = experts(x, meta, mine_ref, wg_ref, wu_ref, wd_ref, top)
     half = near_ref.shape[0]
     near_ref[...] = total[:half]
     far_ref[...] = total[half:].astype(far_ref.dtype)
 
 
-def ffn(mine, blocks, w_gate, w_up, w_down, top):
-    width = w_gate.shape[1]
+def first_ffn_kernel(mine_ref, *refs, blocks, top):
+    ins, (wg_in, wu_in, wd_in, near_ref, far_ref, wg_ref, wu_ref, wd_ref, rows, sems) = refs[:blocks], refs[blocks:]
+    pairs = ((wg_in, wg_ref), (wu_in, wu_ref), (wd_in, wd_ref))
+    copies = [[pltpu.make_async_copy(a.at[e], b.at[e], sems.at[e, i]) for i, (a, b) in enumerate(pairs)] for e in range(wg_in.shape[0])]
+    for row in copies:
+        for copy in row:
+            copy.start()
+    x, meta = gather_rows(ins, rows, near_ref.shape[1])
+    total = experts(x, meta, mine_ref, wg_ref, wu_ref, wd_ref, top, lambda e, i: copies[e][i].wait())
+    half = near_ref.shape[0]
+    near_ref[...] = total[:half]
+    far_ref[...] = total[half:].astype(far_ref.dtype)
+
+
+def ffn(mine, blocks, weights, top, first):
+    w_gate, w_up, w_down = weights
+    exp_dev, width, hidden = w_gate.shape
     rows = sum(b.shape[0] for b in blocks)
+    sums = (
+        jax.ShapeDtypeStruct((rows // 2, width), jnp.float32),
+        jax.ShapeDtypeStruct((rows // 2, width), jnp.bfloat16),
+    )
+    scratch = [pltpu.VMEM((rows, blocks[0].shape[1]), jnp.bfloat16)]
     return pl.pallas_call(
-        functools.partial(ffn_kernel, blocks=len(blocks), top=top),
-        out_shape=(
-            jax.ShapeDtypeStruct((rows // 2, width), jnp.float32),
-            jax.ShapeDtypeStruct((rows // 2, width), jnp.bfloat16),
-        ),
-        in_specs=[SMEM] + [VMEM] * (len(blocks) + 3),
-        out_specs=(VMEM, VMEM),
-        scratch_shapes=[pltpu.VMEM((rows, blocks[0].shape[1]), jnp.bfloat16)],
-        compiler_params=pltpu.CompilerParams(vmem_limit_bytes=24 << 20),
-        name=f"ffn_{rows}",
-    )(mine, *blocks, w_gate, w_up, w_down)
+        functools.partial(first_ffn_kernel if first else ffn_kernel, blocks=len(blocks), top=top),
+        out_shape=sums + (tuple(jax.ShapeDtypeStruct(w.shape, w.dtype) for w in weights) if first else ()),
+        in_specs=[VMEM] * (1 + len(blocks)) + [IN_HBM if first else VMEM] * 3,
+        out_specs=(VMEM, VMEM) + ((VMEM,) * 3 if first else ()),
+        scratch_shapes=scratch + ([pltpu.SemaphoreType.DMA((exp_dev, 3))] if first else []),
+        compiler_params=pltpu.CompilerParams(vmem_limit_bytes=(24 if first else 12) << 20),
+        cost_estimate=pl.CostEstimate(flops=6 * rows * exp_dev * width * hidden, bytes_accessed=6 * exp_dev * width * hidden, transcendentals=rows * exp_dev * hidden),
+        name=f"ffn_first_{rows}" if first else f"ffn_{rows}",
+    )(mine, *blocks, *([keep_in_hbm(w) for w in weights] if first else weights))
 
 
 def join_kernel(near_ref, other_ref, *out_refs):
@@ -127,7 +215,6 @@
     n_node, n_rank = lax.axis_size("node"), lax.axis_size("rank")
     n_x = n_rank // cores
     exp_dev, width = w_gate.shape[:2]
-    slots = n_node * n_rank * exp_dev
     top = expert_ids.shape[1]
 
     def along_z(t, dz):
@@ -143,32 +230,74 @@
     def swap(t):
         return lax.ppermute(t, "rank", [(i, i ^ 1) for i in range(n_rank)])
 
-    device = lax.axis_index("node") * n_rank + lax.axis_index("rank")
-    my_slots = device * exp_dev + jnp.arange(exp_dev, dtype=jnp.int32)
-    plan_hit = slot_plan[None, :] == my_slots[:, None]
-    mine = jnp.sum(jnp.where(plan_hit, jnp.arange(slots, dtype=jnp.int32)[None, :], 0), axis=1)
-
-    pad = LANES - 3 * top
-    meta = jnp.concatenate([expert_ids, combine_weights // 256, combine_weights % 256], axis=1)
-    own = jnp.concatenate([tokens, jnp.pad(meta, ((0, 0), (0, pad))).astype(jnp.bfloat16)], axis=1)
-
-    chips = [(dz, dx) for dz in range(n_node) for dx in range(n_x)]
-    near = {(0, 0): own}
-    for dz in range(1, n_node):
-        near[dz, 0] = along_z(own, dz)
-    for dz in range(n_node):
-        for dx in range(1, n_x):
-            near[dz, dx] = along_x(near[dz, 0], dx)
-    far = {c: swap(near[c]) for c in chips}
-
-    passes = [chips]
-    sums = {}
-    for group in passes:
-        keep, give = ffn(mine, [near[c] for c in group] + [far[c] for c in group], w_gate, w_up, w_down, top)
-        types = [jnp.float32 if c == (0, 0) else jnp.bfloat16 for c in group]
+    def after(t, *deps):
+        return lax.optimization_barrier((t, *deps))[0]
+
+    zs, xs = range(n_node), range(n_x)
+    own, mine = prepare(tokens, expert_ids, combine_weights, slot_plan, exp_dev, n_rank)
+    near, far, sums, weights = {}, {}, {}, (w_gate, w_up, w_down)
+
+    def run(group, first, *deps):
+        blocks = [near[c] for c in group] + [far[c] for c in group]
+        return ffn(after(mine, *deps), blocks, weights, top, first)
+
+    def settle(group, keep, give):
+        types = [jnp.float32 if dx == 0 and dz != 2 else jnp.bfloat16 for dz, dx in group]
         for c, part in zip(group, join(keep, swap(give), types), strict=True):
             sums[c] = part
-    parts = [sums[0, 0]] + [to_chip(sums[c], *c) for c in chips if c != (0, 0)]
+
+    def hop(t, dz):
+        for dx in xs[1:]:
+            near[dz, dx] = along_x(t, dx)
+
+    near[0, 0] = own
+    if n_node > 3:
+        near[3, 0] = along_z(own, 3)
+    if n_node > 1:
+        near[1, 0] = along_z(own, 1)
+    hop(own, 0)
+    early = [(0, dx) for dx in xs[1:]]
+    for dz in zs[2:]:
+        if dz != 3:
+            near[dz, 0] = along_z(after(own, *[near[c] for c in early]), dz)
+    far[0, 0] = swap(own)
+    if n_node > 1:
+        hop(near[1, 0], 1)
+        early += [(1, dx) for dx in xs]
+    for c in early:
+        far[c] = swap(near[c])
+    keep0, give0, *weights = run([(0, 0)], True)
+    settle([(0, 0)], keep0, give0)
+
+    column, corner = [(dz, 0) for dz in zs[2:]], [(dz, dx) for dz in zs[2:] for dx in xs[1:]]
+    for dz in zs[2:]:
+        near[dz, 0] = after(near[dz, 0], give0)
+        hop(near[dz, 0], dz)
+        far[dz, 0] = swap(near[dz, 0])
+    last = give0
+    if early:
+        keep1, give1 = run(early, False, give0)
+        last = give1
+    if column:
+        keep2, give2 = run(column, False, last)
+        last = give2
+        for c in corner:
+            near[c] = after(near[c], give2)
+            far[c] = swap(near[c])
+        settle(column, keep2, give2)
+    if early:
+        settle(early, after(keep1, last), give1)
+    if corner:
+        keep3, give3 = run(corner, False, *[sums[c] for c in column])
+        settle(corner, keep3, give3)
+
+    parts = [sums[0, 0]] + [along_x(sums[0, dx], dx) for dx in xs[1:]]
+    for dz in zs[1:]:
+        if dz == 2:
+            parts += [along_z(sums[dz, 0], dz)] + [to_chip(sums[dz, dx], dz, dx) for dx in xs[1:]]
+        else:
+            merged = add_up([sums[dz, 0]] + [along_x(sums[dz, dx], dx) for dx in xs[1:]], jnp.bfloat16)
+            parts.append(along_z(merged, dz))
     return add_up(parts, tokens.dtype)
 
 
@@ -183,7 +312,7 @@
     slots = n_node * n_rank * exp_dev
     args = (tokens, expert_ids, combine_weights, slot_plan, w_gate, w_up, w_down)
     sent = exp_dev * capacity_of(tok_rows, top, slots)
-    fits = 3 * top <= LANES and slots <= 256 and power_of_two(n_node) and power_of_two(n_rank) and n_rank > 1
+    fits = 3 * rounded(top) <= LANES and slots <= 256 and power_of_two(n_node) and power_of_two(n_rank) and n_rank > 1
     if fits and 2 * sent > tok_rows:
         return dense(*args, cores=2)
     return routed(*args)

time: 75.6 us -> 57.4 us (0.76)
  waiting for transfers between devices: 37.5 us -> 20 us
  local copies, waits for them, and re-layouts: 7.44 us -> 0 us
  Pallas kernels: 8.47 us -> 14.3 us
  starting transfers between devices: 19.2 us -> 22.5 us
  other arithmetic: 2.56 us -> 0 us
    ppermute x7 -> x1, waiting for transfers between devices: 19.9 us -> 6.54 us  [to_chip(): lax.ppermute(t, ('node', 'rank'), [(i, i ^ step) for i in range(n_node *...]
    unnamed x7 -> x0, local copies, waits for them, and re-layouts: 7.34 us -> none
    ppermute x4 -> x7, waiting for transfers between devices: 7.77 us -> 0.88 us  [along_x(): return lax.ppermute(t, 'rank', [(i, i ^ dx * cores) for i in range(n_rank)])]
    pallas_call x1 -> x5, Pallas kernels: 7.48 us -> 13.3 us  [the longest x4 12.4 us: ffn(): pl.pallas_call(functools.partial(first_ffn_kernel if first else ffn_kerne...]
    ppermute x7 -> x1, starting transfers between devices: 9.13 us -> 3.71 us  [to_chip(): lax.ppermute(t, ('node', 'rank'), [(i, i ^ step) for i in range(n_node *...]
    ppermute x3 -> x6, starting transfers between devices: 4.12 us -> 8.89 us  [along_z(): return lax.ppermute(t, 'node', [(i, i ^ dz) for i in range(n_node)])]
    ppermute x3 -> x6, waiting for transfers between devices: 6.8 us -> 11.1 us  [along_z(): return lax.ppermute(t, 'node', [(i, i ^ dz) for i in range(n_node)])]
    ppermute x4 -> x7, starting transfers between devices: 5.01 us -> 8.29 us  [along_x(): return lax.ppermute(t, 'rank', [(i, i ^ dx * cores) for i in range(n_rank)])]
  transfers between devices with their start and end apart: 23 -> 26, of which waited for: 12 -> 12; matrix products, arithmetic and copies ran while one was open for 1% -> 0% of each run, Pallas kernels for 0% -> 22%
where the time goes in v2:
time: 57.4 us; the launch traced here: 57 us
  starting transfers between devices  22.5 us (39%)
  waiting for transfers between devices  20 us (35%)
  Pallas kernels  14.3 us (25%)
    pallas_call x4, Pallas kernels, ffn(): pl.pallas_call(functools.partial(first_ffn_kernel if first else ffn_kerne...  12.4 us
    ppermute x6, waiting for transfers between devices, along_z(): return lax.ppermute(t, 'node', [(i, i ^ dz) for i in range(n_node)])  11.1 us
    ppermute x6, starting transfers between devices, along_z(): return lax.ppermute(t, 'node', [(i, i ^ dz) for i in range(n_node)])  8.89 us
    ppermute x7, starting transfers between devices, along_x(): return lax.ppermute(t, 'rank', [(i, i ^ dx * cores) for i in range(n_rank)])  8.29 us
    ppermute x1, waiting for transfers between devices, to_chip(): lax.ppermute(t, ('node', 'rank'), [(i, i ^ step) for i in range(n_node *...  6.54 us
    ppermute x1, starting transfers between devices, to_chip(): lax.ppermute(t, ('node', 'rank'), [(i, i ^ step) for i in range(n_node *...  3.71 us
    ppermute x12, starting transfers between devices, swap(): return lax.ppermute(t, 'rank', [(i, i ^ 1) for i in range(n_rank)])  1.65 us
    ppermute x12, waiting for transfers between devices, swap(): return lax.ppermute(t, 'rank', [(i, i ^ 1) for i in range(n_rank)])  1.5 us
  transfers between devices with their start and end apart: 26, of which 12 were waited for; matrix products, arithmetic and copies ran while one was open for 0% of the time, Pallas kernels for 22%

profile of v2, /device:TPU:8, one launch (start us, length us, event | category | flops | bytes accessed | tf_op | source)
XLA Modules:
  0.0 57.0 jit_solution(14218098860337061792)
XLA Ops:
  0.0 1.0 %prepare.1 = (bf16[32,2176]{1,0:T(8,128)(2,1)S(1)}, f32[8,128]{1,0:T(8,128)S(1)}) custom-call(bf16[32,2048]{1,0:T(8,128)(2,1)} %tokens_in.1, s32[10,32]{1,0:T(8,128)} %bitcast.2, s32[10,32]{1,0:T(8,128)} %bitcast.3, s32[32]{0:T(128)} %plan_in.1), custom_call_target="tpu_custom_call" | custom-call | tf_op jit(solution)/shard_map/prepare/pallas_call | solution.py:88
  1.0 0.1 collective-permute-start.3
  1.1 1.9 %collective-permute-start.2 = (bf16[32,2176]{1,0:T(8,128)(2,1)S(1)}, bf16[32,2176]{1,0:T(8,128)(2,1)S(1)}, u32[]{:S(2)}, u32[]{:S(2)}) collective-permute-start(bf16[32,2176]{1,0:T(8,128)(2,1)S(1)} %get-tuple-element.45.refs_0_), channel_id=1, source_target_pairs={{0,2},{1,3},{2,0},{3,1},{4,6},{5,7},{6,4},{7,5},{8,10},{9,11},{10,... | collective-permute-start | bytes 417800 | tf_op jit(solution)/shard_map/ppermute | solution.py:224
  3.0 3.5 %collective-permute-done.3.refs_1_ = bf16[32,2176]{1,0:T(8,128)(2,1)S(1)} collective-permute-done((bf16[32,2176]{1,0:T(8,128)(2,1)S(1)}, bf16[32,2176]{1,0:T(8,128)(2,1)S(1)}, u32[]{:S(2)}, u32[]{:S(2)}) %collective-permute-start.3) | collective-permute-done | bytes 139296 | tf_op jit(solution)/shard_map/ppermute | solution.py:221
  6.5 1.5 %collective-permute-start.4 = (bf16[32,2176]{1,0:T(8,128)(2,1)S(1)}, bf16[32,2176]{1,0:T(8,128)(2,1)S(1)}, u32[]{:S(2)}, u32[]{:S(2)}) collective-permute-start(bf16[32,2176]{1,0:T(8,128)(2,1)S(1)} %collective-permute-done.3.refs_1_), channel_id=1, source_target_pairs={{0,2},{1,3},{2,0},{3,1},{4,6},{5,7},{6,4},{7,5},{8,10},{9,11},{10,... | collective-permute-start | bytes 417800 | tf_op jit(solution)/shard_map/ppermute | solution.py:224
  7.9 1.6 %collective-permute-start.9 = (bf16[32,2176]{1,0:T(8,128)(2,1)S(1)}, bf16[32,2176]{1,0:T(8,128)(2,1)S(1)}, u32[]{:S(2)}, u32[]{:S(2)}) collective-permute-start(bf16[32,2176]{1,0:T(8,128)(2,1)S(1)} %get-tuple-element.45.refs_0_), channel_id=1, source_target_pairs={{0,12},{4,8},{8,4},{12,0},{1,13},{5,9},{9,5},{13,1},{2,14},{6,10},... | collective-permute-start | bytes 417800 | tf_op jit(solution)/shard_map/ppermute | solution.py:221
  9.5 1.2 %collective-permute-start.8 = (bf16[32,2176]{1,0:T(8,128)(2,1)S(1)}, bf16[32,2176]{1,0:T(8,128)(2,1)S(1)}, u32[]{:S(2)}, u32[]{:S(2)}) collective-permute-start(bf16[32,2176]{1,0:T(8,128)(2,1)S(1)} %get-tuple-element.45.refs_0_), channel_id=1, source_target_pairs={{0,8},{4,12},{8,0},{12,4},{1,9},{5,13},{9,1},{13,5},{2,10},{6,14},... | collective-permute-start | bytes 417800 | tf_op jit(solution)/shard_map/ppermute | solution.py:221
  10.8 0.0 collective-permute-start.5
  10.8 0.0 collective-permute-done.refs_1_
  10.8 0.5 collective-permute-start.6
  11.3 0.2 collective-permute-done.4.refs_2_
  11.5 5.2 %ffn_first_64.1 = (f32[32,2048]{1,0:T(8,128)S(1)}, bf16[32,2048]{1,0:T(8,128)(2,1)S(1)}, bf16[2,2048,512]{2,1,0:T(8,128)(2,1)S(1)}, bf16[2,2048,512]{2,1,0:T(8,128)(2,1)S(1)}, bf16[2,512,2048]{2,1,0:T(8,128)(2,1)S(1)}) custom-call(f32[8,128]{1,0:T(8,128)S(1)} %get-tuple-element.56.mine_ref, bf16[32,2176]{1,0:T(8,128)(2,1)S(1)} %get-tuple-element.45.refs_0_, ...), custom_call_target="tpu_custom_call" | custom-call | flops 805306368 | bytes 12582912 | tf_op jit(solution)/shard_map/ffn_first_64/pallas_call | solution.py:165
  16.7 2.4 %collective-permute-done.9.refs_1_ = bf16[32,2176]{1,0:T(8,128)(2,1)S(1)} collective-permute-done((bf16[32,2176]{1,0:T(8,128)(2,1)S(1)}, bf16[32,2176]{1,0:T(8,128)(2,1)S(1)}, u32[]{:S(2)}, u32[]{:S(2)}) %collective-permute-start.9) | collective-permute-done | bytes 139296 | tf_op jit(solution)/shard_map/ppermute | solution.py:221
  19.2 0.0 collective-permute-start.11
  19.2 1.1 %collective-permute-done.8.refs_0_ = bf16[32,2176]{1,0:T(8,128)(2,1)S(1)} collective-permute-done((bf16[32,2176]{1,0:T(8,128)(2,1)S(1)}, bf16[32,2176]{1,0:T(8,128)(2,1)S(1)}, u32[]{:S(2)}, u32[]{:S(2)}) %collective-permute-start.8) | collective-permute-done | bytes 139296 | tf_op jit(solution)/shard_map/ppermute | solution.py:221
  20.3 0.5 collective-permute-start.19
  20.8 1.6 %collective-permute-start.18 = (bf16[32,2176]{1,0:T(8,128)(2,1)S(1)}, bf16[32,2176]{1,0:T(8,128)(2,1)S(1)}, u32[]{:S(2)}, u32[]{:S(2)}) collective-permute-start(bf16[32,2176]{1,0:T(8,128)(2,1)S(1)} %collective-permute-done.8.refs_0_), channel_id=1, source_target_pairs={{0,2},{1,3},{2,0},{3,1},{4,6},{5,7},{6,4},{7,5},{8,10},{9,11},{10,... | collective-permute-start | bytes 417800 | tf_op jit(solution)/shard_map/ppermute | solution.py:224
  22.4 0.0 collective-permute-done.7.refs_5_
  22.4 2.9 %ffn_192.1 = (f32[96,2048]{1,0:T(8,128)S(1)}, bf16[96,2048]{1,0:T(8,128)(2,1)S(1)}) custom-call(f32[8,128]{1,0:T(8,128)S(1)} %get-tuple-element.56.mine_ref, bf16[32,2176]{1,0:T(8,128)(2,1)S(1)} %collective-permute-done.2.refs_0_, bf16[32,2176]{1,0:T(8,128)(2,1)S(1)} %collective-permute-done.3.refs_1_, bf16[32,2176]{1,0:T(8,128)(2,1)S(1)} %collective-permute-done.4.refs_2_, ...), custom_call_target="tpu_custom_call" | custom-call | flops 2415919104 | bytes 12582912 | tf_op jit(solution)/shard_map/ffn_192/pallas_call | solution.py:165
  25.3 0.0 collective-permute-done.11.refs_3_
  25.3 2.1 %ffn_128.2 = (f32[64,2048]{1,0:T(8,128)S(1)}, bf16[64,2048]{1,0:T(8,128)(2,1)S(1)}) custom-call(f32[8,128]{1,0:T(8,128)S(1)} %get-tuple-element.56.mine_ref, bf16[32,2176]{1,0:T(8,128)(2,1)S(1)} %collective-permute-done.8.refs_0_, bf16[32,2176]{1,0:T(8,128)(2,1)S(1)} %collective-permute-done.9.refs_1_, bf16[32,2176]{1,0:T(8,128)(2,1)S(1)} %collective-permute-done.10.refs_2_, ...), custom_call_target="tpu_custom_call" | custom-call | flops 1610612736 | bytes 12582912 | tf_op jit(solution)/shard_map/ffn_128/pallas_call | solution.py:165
  27.4 0.2 collective-permute-start.16
  27.7 0.6 %collective-permute-done.18.refs_0_ = bf16[32,2176]{1,0:T(8,128)(2,1)S(1)} collective-permute-done((bf16[32,2176]{1,0:T(8,128)(2,1)S(1)}, bf16[32,2176]{1,0:T(8,128)(2,1)S(1)}, u32[]{:S(2)}, u32[]{:S(2)}) %collective-permute-start.18) | collective-permute-done | bytes 139296 | tf_op jit(solution)/shard_map/ppermute | solution.py:224
  28.3 0.0 collective-permute-done.19.refs_1_
  28.3 0.5 collective-permute-start.21
  28.8 0.0 collective-permute-start.12
  28.8 0.2 collective-permute-done.16.other_ref
  29.0 0.1 join.6
  29.1 0.6 %collective-permute-done.20.refs_2_ = bf16[32,2176]{1,0:T(8,128)(2,1)S(1)} collective-permute-done((bf16[32,2176]{1,0:T(8,128)(2,1)S(1)}, bf16[32,2176]{1,0:T(8,128)(2,1)S(1)}, u32[]{:S(2)}, u32[]{:S(2)}) %collective-permute-start.20) | collective-permute-done | bytes 139296 | tf_op jit(solution)/shard_map/ppermute | solution.py:231
  29.7 0.2 collective-permute-done.21.refs_3_
  29.9 2.1 %ffn_128.3 = (f32[64,2048]{1,0:T(8,128)S(1)}, bf16[64,2048]{1,0:T(8,128)(2,1)S(1)}) custom-call(f32[8,128]{1,0:T(8,128)S(1)} %get-tuple-element.56.mine_ref, bf16[32,2176]{1,0:T(8,128)(2,1)S(1)} %collective-permute-done.18.refs_0_, bf16[32,2176]{1,0:T(8,128)(2,1)S(1)} %collective-permute-done.19.refs_1_, ...), custom_call_target="tpu_custom_call" | custom-call | flops 1610612736 | bytes 12582912 | tf_op jit(solution)/shard_map/ffn_128/pallas_call | solution.py:165
  32.0 0.4 collective-permute-start.22
  32.4 0.0 collective-permute-done.12.other_ref
  32.4 0.1 join.5
  32.4 0.7 %collective-permute-start.14 = (bf16[32,2048]{1,0:T(8,128)(2,1)S(1)}, bf16[32,2048]{1,0:T(8,128)(2,1)S(1)}, u32[]{:S(2)}, u32[]{:S(2)}) collective-permute-start(bf16[32,2048]{1,0:T(8,128)(2,1)S(1)} %get-tuple-element.52), channel_id=1, source_target_pairs={{0,2},{1,3},{2,0},{3,1},{4,6},{5,7},{6,4},{7,5},{8,10},{9,11},{10,... | collective-permute-start | bytes 393224 | tf_op jit(solution)/shard_map/ppermute | solution.py:224
  33.1 0.5 collective-permute-done.22.other_ref
  33.6 1.0 %collective-permute-start.24 = (bf16[32,2048]{1,0:T(8,128)(2,1)S(1)}, bf16[32,2048]{1,0:T(8,128)(2,1)S(1)}, u32[]{:S(2)}, u32[]{:S(2)}) collective-permute-start(bf16[32,2048]{1,0:T(8,128)(2,1)S(1)} %get-tuple-element.62), channel_id=1, source_target_pairs={{0,2},{1,3},{2,0},{3,1},{4,6},{5,7},{6,4},{7,5},{8,10},{9,11},{10,... | collective-permute-start | bytes 393224 | tf_op jit(solution)/shard_map/ppermute | solution.py:224
  34.6 3.4 %collective-permute-start.17 = (bf16[32,2048]{1,0:T(8,128)(2,1)S(1)}, bf16[32,2048]{1,0:T(8,128)(2,1)S(1)}, u32[]{:S(2)}, u32[]{:S(2)}) collective-permute-start(bf16[32,2048]{1,0:T(8,128)(2,1)S(1)} %get-tuple-element.54), channel_id=1, source_target_pairs={{0,8},{4,12},{8,0},{12,4},{1,9},{5,13},{9,1},{13,5},{2,10},{6,14},... | collective-permute-start | bytes 393224 | tf_op jit(solution)/shard_map/ppermute | solution.py:221
  38.0 1.1 %collective-permute-start.13 = (bf16[32,2048]{1,0:T(8,128)(2,1)S(1)}, bf16[32,2048]{1,0:T(8,128)(2,1)S(1)}, u32[]{:S(2)}, u32[]{:S(2)}) collective-permute-start(bf16[32,2048]{1,0:T(8,128)(2,1)S(1)} %get-tuple-element.50), channel_id=1, source_target_pairs={{0,2},{1,3},{2,0},{3,1},{4,6},{5,7},{6,4},{7,5},{8,10},{9,11},{10,... | collective-permute-start | bytes 393224 | tf_op jit(solution)/shard_map/ppermute | solution.py:224
  39.1 0.0 collective-permute-done.14.refs_1_
  39.2 2.1 %collective-permute-start.15 = (bf16[32,2048]{1,0:T(8,128)(2,1)S(1)}, bf16[32,2048]{1,0:T(8,128)(2,1)S(1)}, u32[]{:S(2)}, u32[]{:S(2)}) collective-permute-start(bf16[32,2048]{1,0:T(8,128)(2,1)S(1)} %total.3), channel_id=1, source_target_pairs={{0,4},{4,0},{8,12},{12,8},{1,5},{5,1},{9,13},{13,9},{2,6},{6,2},{1... | collective-permute-start | bytes 393224 | tf_op jit(solution)/shard_map/ppermute | solution.py:221
  41.3 0.0 collective-permute-done.24.refs_1_
  41.3 3.7 %collective-permute-start.23 = (bf16[32,2048]{1,0:T(8,128)(2,1)S(1)}, bf16[32,2048]{1,0:T(8,128)(2,1)S(1)}, u32[]{:S(2)}, u32[]{:S(2)}) collective-permute-start(bf16[32,2048]{1,0:T(8,128)(2,1)S(1)} %get-tuple-element.61), channel_id=1, source_target_pairs={{0,10},{1,11},{2,8},{3,9},{4,14},{5,15},{6,12},{7,13},{8,2},{9,3},... | collective-permute-start | bytes 393224 | tf_op jit(solution)/shard_map/ppermute | solution.py:228
  45.0 0.5 collective-permute-start.25
  45.6 0.3 collective-permute-done.15.refs_2_
  45.9 6.5 %collective-permute-done.23.refs_4_ = bf16[32,2048]{1,0:T(8,128)(2,1)S(1)} collective-permute-done((bf16[32,2048]{1,0:T(8,128)(2,1)S(1)}, bf16[32,2048]{1,0:T(8,128)(2,1)S(1)}, u32[]{:S(2)}, u32[]{:S(2)}) %collective-permute-start.23) | collective-permute-done | bytes 131104 | tf_op jit(solution)/shard_map/ppermute | solution.py:228
  52.4 3.8 %collective-permute-done.25.refs_5_ = bf16[32,2048]{1,0:T(8,128)(2,1)S(1)} collective-permute-done((bf16[32,2048]{1,0:T(8,128)(2,1)S(1)}, bf16[32,2048]{1,0:T(8,128)(2,1)S(1)}, u32[]{:S(2)}, u32[]{:S(2)}) %collective-permute-start.25) | collective-permute-done | bytes 131104 | tf_op jit(solution)/shard_map/ppermute | solution.py:221
  56.3 0.7 %total.5 = bf16[32,2048]{1,0:T(8,128)(2,1)} custom-call(f32[32,2048]{1,0:T(8,128)S(1)} %join.4.refs_0_, bf16[32,2048]{1,0:T(8,128)(2,1)S(1)} %collective-permute-done.13.refs_1_, bf16[32,2048]{1,0:T(8,128)(2,1)S(1)} %collective-permute-done.15.refs_2_, bf16[32,2048]{1,0:T(8,128)(2,1)S(1)} %collective-permute-done.17.refs_3_, ...), custom_call_target="tpu_custom_call" | custom-call | tf_op jit(solution)/shard_map/total/pallas_call | solution.py:204
  (16 shorter events, 0.2 us)
Async XLA Ops:
  1.0 5.5 %collective-permute-start.3 = (bf16[32,2176]{1,0:T(8,128)(2,1)S(1)}, bf16[32,2176]{1,0:T(8,128)(2,1)S(1)}, u32[]{:S(2)}, u32[]{:S(2)}) collective-permute-start(bf16[32,2176]{1,0:T(8,128)(2,1)S(1)} %get-tuple-element.45.refs_0_), channel_id=1, source_target_pairs={{0,4},{4,0},{8,12},{12,8},{1,5},{5,1},{9,13},{13,9},{2,6},{6,2},{1... | collective-permute-start | bytes 417800 | tf_op jit(solution)/shard_map/ppermute | solution.py:221
  1.1 8.5 %collective-permute-start.2 = (bf16[32,2176]{1,0:T(8,128)(2,1)S(1)}, bf16[32,2176]{1,0:T(8,128)(2,1)S(1)}, u32[]{:S(2)}, u32[]{:S(2)}) collective-permute-start(bf16[32,2176]{1,0:T(8,128)(2,1)S(1)} %get-tuple-element.45.refs_0_), channel_id=1, source_target_pairs={{0,2},{1,3},{2,0},{3,1},{4,6},{5,7},{6,4},{7,5},{8,10},{9,11},{10,... | collective-permute-start | bytes 417800 | tf_op jit(solution)/shard_map/ppermute | solution.py:224
  3.0 7.8 %collective-permute-start = (bf16[32,2176]{1,0:T(8,128)(2,1)S(1)}, bf16[32,2176]{1,0:T(8,128)(2,1)S(1)}, u32[]{:S(2)}, u32[]{:S(2)}) collective-permute-start(bf16[32,2176]{1,0:T(8,128)(2,1)S(1)} %get-tuple-element.45.refs_0_), channel_id=1, source_target_pairs={{0,1},{1,0},{2,3},{3,2},{4,5},{5,4},{6,7},{7,6},{8,9},{9,8},{10,11... | collective-permute-start | bytes 417800 | tf_op jit(solution)/shard_map/ppermute | solution.py:231
  6.5 5.1 %collective-permute-start.4 = (bf16[32,2176]{1,0:T(8,128)(2,1)S(1)}, bf16[32,2176]{1,0:T(8,128)(2,1)S(1)}, u32[]{:S(2)}, u32[]{:S(2)}) collective-permute-start(bf16[32,2176]{1,0:T(8,128)(2,1)S(1)} %collective-permute-done.3.refs_1_), channel_id=1, source_target_pairs={{0,2},{1,3},{2,0},{3,1},{4,6},{5,7},{6,4},{7,5},{8,10},{9,11},{10,... | collective-permute-start | bytes 417800 | tf_op jit(solution)/shard_map/ppermute | solution.py:224
  7.9 11.2 %collective-permute-start.9 = (bf16[32,2176]{1,0:T(8,128)(2,1)S(1)}, bf16[32,2176]{1,0:T(8,128)(2,1)S(1)}, u32[]{:S(2)}, u32[]{:S(2)}) collective-permute-start(bf16[32,2176]{1,0:T(8,128)(2,1)S(1)} %get-tuple-element.45.refs_0_), channel_id=1, source_target_pairs={{0,12},{4,8},{8,4},{12,0},{1,13},{5,9},{9,5},{13,1},{2,14},{6,10},... | collective-permute-start | bytes 417800 | tf_op jit(solution)/shard_map/ppermute | solution.py:221
  9.5 10.7 %collective-permute-start.8 = (bf16[32,2176]{1,0:T(8,128)(2,1)S(1)}, bf16[32,2176]{1,0:T(8,128)(2,1)S(1)}, u32[]{:S(2)}, u32[]{:S(2)}) collective-permute-start(bf16[32,2176]{1,0:T(8,128)(2,1)S(1)} %get-tuple-element.45.refs_0_), channel_id=1, source_target_pairs={{0,8},{4,12},{8,0},{12,4},{1,9},{5,13},{9,1},{13,5},{2,10},{6,14},... | collective-permute-start | bytes 417800 | tf_op jit(solution)/shard_map/ppermute | solution.py:221
  10.8 10.0 %collective-permute-start.5 = (bf16[32,2176]{1,0:T(8,128)(2,1)S(1)}, bf16[32,2176]{1,0:T(8,128)(2,1)S(1)}, u32[]{:S(2)}, u32[]{:S(2)}) collective-permute-start(bf16[32,2176]{1,0:T(8,128)(2,1)S(1)} %collective-permute-done.2.refs_0_), channel_id=1, source_target_pairs={{0,1},{1,0},{2,3},{3,2},{4,5},{5,4},{6,7},{7,6},{8,9},{9,8},{10,11... | collective-permute-start | bytes 417800 | tf_op jit(solution)/shard_map/ppermute | solution.py:231
  10.8 10.0 %collective-permute-start.6 = (bf16[32,2176]{1,0:T(8,128)(2,1)S(1)}, bf16[32,2176]{1,0:T(8,128)(2,1)S(1)}, u32[]{:S(2)}, u32[]{:S(2)}) collective-permute-start(bf16[32,2176]{1,0:T(8,128)(2,1)S(1)} %collective-permute-done.3.refs_1_), channel_id=1, source_target_pairs={{0,1},{1,0},{2,3},{3,2},{4,5},{5,4},{6,7},{7,6},{8,9},{9,8},{10,11... | collective-permute-start | bytes 417800 | tf_op jit(solution)/shard_map/ppermute | solution.py:231
  11.5 10.9 %collective-permute-start.7 = (bf16[32,2176]{1,0:T(8,128)(2,1)S(1)}, bf16[32,2176]{1,0:T(8,128)(2,1)S(1)}, u32[]{:S(2)}, u32[]{:S(2)}) collective-permute-start(bf16[32,2176]{1,0:T(8,128)(2,1)S(1)} %collective-permute-done.4.refs_2_), channel_id=1, source_target_pairs={{0,1},{1,0},{2,3},{3,2},{4,5},{5,4},{6,7},{7,6},{8,9},{9,8},{10,11... | collective-permute-start | bytes 417800 | tf_op jit(solution)/shard_map/ppermute | solution.py:231
  19.2 6.1 %collective-permute-start.11 = (bf16[32,2176]{1,0:T(8,128)(2,1)S(1)}, bf16[32,2176]{1,0:T(8,128)(2,1)S(1)}, u32[]{:S(2)}, u32[]{:S(2)}) collective-permute-start(bf16[32,2176]{1,0:T(8,128)(2,1)S(1)} %collective-permute-done.9.refs_1_), channel_id=1, source_target_pairs={{0,1},{1,0},{2,3},{3,2},{4,5},{5,4},{6,7},{7,6},{8,9},{9,8},{10,11... | collective-permute-start | bytes 417800 | tf_op jit(solution)/shard_map/ppermute | solution.py:231
  20.3 8.0 %collective-permute-start.19 = (bf16[32,2176]{1,0:T(8,128)(2,1)S(1)}, bf16[32,2176]{1,0:T(8,128)(2,1)S(1)}, u32[]{:S(2)}, u32[]{:S(2)}) collective-permute-start(bf16[32,2176]{1,0:T(8,128)(2,1)S(1)} %collective-permute-done.9.refs_1_), channel_id=1, source_target_pairs={{0,2},{1,3},{2,0},{3,1},{4,6},{5,7},{6,4},{7,5},{8,10},{9,11},{10,... | collective-permute-start | bytes 417800 | tf_op jit(solution)/shard_map/ppermute | solution.py:224
  20.8 4.5 %collective-permute-start.10 = (bf16[32,2176]{1,0:T(8,128)(2,1)S(1)}, bf16[32,2176]{1,0:T(8,128)(2,1)S(1)}, u32[]{:S(2)}, u32[]{:S(2)}) collective-permute-start(bf16[32,2176]{1,0:T(8,128)(2,1)S(1)} %collective-permute-done.8.refs_0_), channel_id=1, source_target_pairs={{0,1},{1,0},{2,3},{3,2},{4,5},{5,4},{6,7},{7,6},{8,9},{9,8},{10,11... | collective-permute-start | bytes 417800 | tf_op jit(solution)/shard_map/ppermute | solution.py:231
  20.8 7.5 %collective-permute-start.18 = (bf16[32,2176]{1,0:T(8,128)(2,1)S(1)}, bf16[32,2176]{1,0:T(8,128)(2,1)S(1)}, u32[]{:S(2)}, u32[]{:S(2)}) collective-permute-start(bf16[32,2176]{1,0:T(8,128)(2,1)S(1)} %collective-permute-done.8.refs_0_), channel_id=1, source_target_pairs={{0,2},{1,3},{2,0},{3,1},{4,6},{5,7},{6,4},{7,5},{8,10},{9,11},{10,... | collective-permute-start | bytes 417800 | tf_op jit(solution)/shard_map/ppermute | solution.py:224
  27.4 1.6 %collective-permute-start.16 = (bf16[64,2048]{1,0:T(8,128)(2,1)S(1)}, bf16[64,2048]{1,0:T(8,128)(2,1)S(1)}, u32[]{:S(2)}, u32[]{:S(2)}) collective-permute-start(bf16[64,2048]{1,0:T(8,128)(2,1)S(1)} %get-tuple-element.48), channel_id=1, source_target_pairs={{0,1},{1,0},{2,3},{3,2},{4,5},{5,4},{6,7},{7,6},{8,9},{9,8},{10,11... | collective-permute-start | bytes 786440 | tf_op jit(solution)/shard_map/ppermute | solution.py:231
  28.3 1.4 %collective-permute-start.20 = (bf16[32,2176]{1,0:T(8,128)(2,1)S(1)}, bf16[32,2176]{1,0:T(8,128)(2,1)S(1)}, u32[]{:S(2)}, u32[]{:S(2)}) collective-permute-start(bf16[32,2176]{1,0:T(8,128)(2,1)S(1)} %collective-permute-done.18.refs_0_), channel_id=1, source_target_pairs={{0,1},{1,0},{2,3},{3,2},{4,5},{5,4},{6,7},{7,6},{8,9},{9,8},{10,11... | collective-permute-start | bytes 417800 | tf_op jit(solution)/shard_map/ppermute | solution.py:231
  28.3 1.6 %collective-permute-start.21 = (bf16[32,2176]{1,0:T(8,128)(2,1)S(1)}, bf16[32,2176]{1,0:T(8,128)(2,1)S(1)}, u32[]{:S(2)}, u32[]{:S(2)}) collective-permute-start(bf16[32,2176]{1,0:T(8,128)(2,1)S(1)} %collective-permute-done.19.refs_1_), channel_id=1, source_target_pairs={{0,1},{1,0},{2,3},{3,2},{4,5},{5,4},{6,7},{7,6},{8,9},{9,8},{10,11... | collective-permute-start | bytes 417800 | tf_op jit(solution)/shard_map/ppermute | solution.py:231
  28.8 3.5 %collective-permute-start.12 = (bf16[96,2048]{1,0:T(8,128)(2,1)S(1)}, bf16[96,2048]{1,0:T(8,128)(2,1)S(1)}, u32[]{:S(2)}, u32[]{:S(2)}) collective-permute-start(bf16[96,2048]{1,0:T(8,128)(2,1)S(1)} %get-tuple-element.43), channel_id=1, source_target_pairs={{0,1},{1,0},{2,3},{3,2},{4,5},{5,4},{6,7},{7,6},{8,9},{9,8},{10,11... | collective-permute-start | bytes 1179656 | tf_op jit(solution)/shard_map/ppermute | solution.py:231
  32.0 1.6 %collective-permute-start.22 = (bf16[64,2048]{1,0:T(8,128)(2,1)S(1)}, bf16[64,2048]{1,0:T(8,128)(2,1)S(1)}, u32[]{:S(2)}, u32[]{:S(2)}) collective-permute-start(bf16[64,2048]{1,0:T(8,128)(2,1)S(1)} %get-tuple-element.60), channel_id=1, source_target_pairs={{0,1},{1,0},{2,3},{3,2},{4,5},{5,4},{6,7},{7,6},{8,9},{9,8},{10,11... | collective-permute-start | bytes 786440 | tf_op jit(solution)/shard_map/ppermute | solution.py:231
  32.4 6.7 %collective-permute-start.14 = (bf16[32,2048]{1,0:T(8,128)(2,1)S(1)}, bf16[32,2048]{1,0:T(8,128)(2,1)S(1)}, u32[]{:S(2)}, u32[]{:S(2)}) collective-permute-start(bf16[32,2048]{1,0:T(8,128)(2,1)S(1)} %get-tuple-element.52), channel_id=1, source_target_pairs={{0,2},{1,3},{2,0},{3,1},{4,6},{5,7},{6,4},{7,5},{8,10},{9,11},{10,... | collective-permute-start | bytes 393224 | tf_op jit(solution)/shard_map/ppermute | solution.py:224
  33.6 7.7 %collective-permute-start.24 = (bf16[32,2048]{1,0:T(8,128)(2,1)S(1)}, bf16[32,2048]{1,0:T(8,128)(2,1)S(1)}, u32[]{:S(2)}, u32[]{:S(2)}) collective-permute-start(bf16[32,2048]{1,0:T(8,128)(2,1)S(1)} %get-tuple-element.62), channel_id=1, source_target_pairs={{0,2},{1,3},{2,0},{3,1},{4,6},{5,7},{6,4},{7,5},{8,10},{9,11},{10,... | collective-permute-start | bytes 393224 | tf_op jit(solution)/shard_map/ppermute | solution.py:224
  34.6 10.4 %collective-permute-start.1 = (bf16[32,2048]{1,0:T(8,128)(2,1)S(1)}, bf16[32,2048]{1,0:T(8,128)(2,1)S(1)}, u32[]{:S(2)}, u32[]{:S(2)}) collective-permute-start(bf16[32,2048]{1,0:T(8,128)(2,1)S(1)} %get-tuple-element.37), channel_id=1, source_target_pairs={{0,1},{1,0},{2,3},{3,2},{4,5},{5,4},{6,7},{7,6},{8,9},{9,8},{10,11... | collective-permute-start | bytes 393224 | tf_op jit(solution)/shard_map/ppermute | solution.py:231
  34.6 10.9 %collective-permute-start.17 = (bf16[32,2048]{1,0:T(8,128)(2,1)S(1)}, bf16[32,2048]{1,0:T(8,128)(2,1)S(1)}, u32[]{:S(2)}, u32[]{:S(2)}) collective-permute-start(bf16[32,2048]{1,0:T(8,128)(2,1)S(1)} %get-tuple-element.54), channel_id=1, source_target_pairs={{0,8},{4,12},{8,0},{12,4},{1,9},{5,13},{9,1},{13,5},{2,10},{6,14},... | collective-permute-start | bytes 393224 | tf_op jit(solution)/shard_map/ppermute | solution.py:221
  38.0 7.6 %collective-permute-start.13 = (bf16[32,2048]{1,0:T(8,128)(2,1)S(1)}, bf16[32,2048]{1,0:T(8,128)(2,1)S(1)}, u32[]{:S(2)}, u32[]{:S(2)}) collective-permute-start(bf16[32,2048]{1,0:T(8,128)(2,1)S(1)} %get-tuple-element.50), channel_id=1, source_target_pairs={{0,2},{1,3},{2,0},{3,1},{4,6},{5,7},{6,4},{7,5},{8,10},{9,11},{10,... | collective-permute-start | bytes 393224 | tf_op jit(solution)/shard_map/ppermute | solution.py:224
  39.2 6.7 %collective-permute-start.15 = (bf16[32,2048]{1,0:T(8,128)(2,1)S(1)}, bf16[32,2048]{1,0:T(8,128)(2,1)S(1)}, u32[]{:S(2)}, u32[]{:S(2)}) collective-permute-start(bf16[32,2048]{1,0:T(8,128)(2,1)S(1)} %total.3), channel_id=1, source_target_pairs={{0,4},{4,0},{8,12},{12,8},{1,5},{5,1},{9,13},{13,9},{2,6},{6,2},{1... | collective-permute-start | bytes 393224 | tf_op jit(solution)/shard_map/ppermute | solution.py:221
  41.3 11.2 %collective-permute-start.23 = (bf16[32,2048]{1,0:T(8,128)(2,1)S(1)}, bf16[32,2048]{1,0:T(8,128)(2,1)S(1)}, u32[]{:S(2)}, u32[]{:S(2)}) collective-permute-start(bf16[32,2048]{1,0:T(8,128)(2,1)S(1)} %get-tuple-element.61), channel_id=1, source_target_pairs={{0,10},{1,11},{2,8},{3,9},{4,14},{5,15},{6,12},{7,13},{8,2},{9,3},... | collective-permute-start | bytes 393224 | tf_op jit(solution)/shard_map/ppermute | solution.py:228
  45.0 11.2 %collective-permute-start.25 = (bf16[32,2048]{1,0:T(8,128)(2,1)S(1)}, bf16[32,2048]{1,0:T(8,128)(2,1)S(1)}, u32[]{:S(2)}, u32[]{:S(2)}) collective-permute-start(bf16[32,2048]{1,0:T(8,128)(2,1)S(1)} %total.4), channel_id=1, source_target_pairs={{0,12},{4,8},{8,4},{12,0},{1,13},{5,9},{9,5},{13,1},{2,14},{6,10},... | collective-permute-start | bytes 393224 | tf_op jit(solution)/shard_map/ppermute | solution.py:221

commit v3 on v2

--- a/solution.py
+++ b/solution.py
@@ -8,6 +8,7 @@
 from jax.sharding import PartitionSpec as P
 
 LANES = 128
+PIECES = 1
 VMEM = pl.BlockSpec(memory_space=pltpu.VMEM)
 IN_HBM = pl.BlockSpec(memory_space=pltpu.HBM)
 
@@ -55,7 +56,8 @@
     return -(-n // 8) * 8
 
 
-def prepare_kernel(tokens_in, ids_in, weights_in, plan_in, rows_ref, mine_ref, ids, weights, meta, plan, sems, *, exp_dev, n_rank):
+def prepare_kernel(tokens_in, ids_in, weights_in, plan_in, rows_ref, *refs, exp_dev, n_rank):
+    mine_ref, ids, weights, meta, plan, sems = refs
     width, top = tokens_in.shape[1], ids.shape[0]
     moves = ((tokens_in, rows_ref.at[:, :width]), (ids_in, ids), (weights_in, weights), (plan_in, plan))
     copies = [pltpu.make_async_copy(a, b, sems.at[i]) for i, (a, b) in enumerate(moves)]
@@ -124,23 +126,29 @@
 
 
 def gather_rows(ins, rows, width):
-    step = ins[0].shape[0]
-    for i, ref in enumerate(ins):
-        rows[pl.ds(i * step, step), :] = ref[...]
+    start = 0
+    for ref in ins:
+        rows[pl.ds(start, ref.shape[0]), :] = ref[...]
+        start += ref.shape[0]
     return rows[:, :width], rows[:, width:].astype(jnp.float32)
 
 
+def hand_out(total, near_ref, far_refs):
+    half, step = near_ref.shape[0], far_refs[0].shape[0]
+    near_ref[...] = total[:half]
+    for i, ref in enumerate(far_refs):
+        ref[...] = total[half + i * step : half + (i + 1) * step].astype(ref.dtype)
+
+
 def ffn_kernel(mine_ref, *refs, blocks, top):
-    ins, (wg_ref, wu_ref, wd_ref, near_ref, far_ref, rows) = refs[:blocks], refs[blocks:]
+    ins, (wg_ref, wu_ref, wd_ref, near_ref, *far_refs, rows) = refs[:blocks], refs[blocks:]
     x, meta = gather_rows(ins, rows, near_ref.shape[1])
     total = experts(x, meta, mine_ref, wg_ref, wu_ref, wd_ref, top)
-    half = near_ref.shape[0]
-    near_ref[...] = total[:half]
-    far_ref[...] = total[half:].astype(far_ref.dtype)
+    hand_out(total, near_ref, far_refs)
 
 
 def first_ffn_kernel(mine_ref, *refs, blocks, top):
-    ins, (wg_in, wu_in, wd_in, near_ref, far_ref, wg_ref, wu_ref, wd_ref, rows, sems) = refs[:blocks], refs[blocks:]
+    ins, (wg_in, wu_in, wd_in, near_ref, *far_refs, wg_ref, wu_ref, wd_ref, rows, sems) = refs[:blocks], refs[blocks:]
     pairs = ((wg_in, wg_ref), (wu_in, wu_ref), (wd_in, wd_ref))
     copies = [[pltpu.make_async_copy(a.at[e], b.at[e], sems.at[e, i]) for i, (a, b) in enumerate(pairs)] for e in range(wg_in.shape[0])]
     for row in copies:
@@ -148,25 +156,21 @@
             copy.start()
     x, meta = gather_rows(ins, rows, near_ref.shape[1])
     total = experts(x, meta, mine_ref, wg_ref, wu_ref, wd_ref, top, lambda e, i: copies[e][i].wait())
-    half = near_ref.shape[0]
-    near_ref[...] = total[:half]
-    far_ref[...] = total[half:].astype(far_ref.dtype)
-
-
-def ffn(mine, blocks, weights, top, first):
+    hand_out(total, near_ref, far_refs)
+
+
+def ffn(mine, blocks, weights, top, first, pieces):
     w_gate, w_up, w_down = weights
     exp_dev, width, hidden = w_gate.shape
     rows = sum(b.shape[0] for b in blocks)
-    sums = (
-        jax.ShapeDtypeStruct((rows // 2, width), jnp.float32),
-        jax.ShapeDtypeStruct((rows // 2, width), jnp.bfloat16),
-    )
+    sums = (jax.ShapeDtypeStruct((rows // 2, width), jnp.float32),)
+    sums += (jax.ShapeDtypeStruct((rows // 2 // pieces, width), jnp.bfloat16),) * pieces
     scratch = [pltpu.VMEM((rows, blocks[0].shape[1]), jnp.bfloat16)]
     return pl.pallas_call(
         functools.partial(first_ffn_kernel if first else ffn_kernel, blocks=len(blocks), top=top),
         out_shape=sums + (tuple(jax.ShapeDtypeStruct(w.shape, w.dtype) for w in weights) if first else ()),
         in_specs=[VMEM] * (1 + len(blocks)) + [IN_HBM if first else VMEM] * 3,
-        out_specs=(VMEM, VMEM) + ((VMEM,) * 3 if first else ()),
+        out_specs=(VMEM,) * (1 + pieces + (3 if first else 0)),
         scratch_shapes=scratch + ([pltpu.SemaphoreType.DMA((exp_dev, 3))] if first else []),
         compiler_params=pltpu.CompilerParams(vmem_limit_bytes=(24 if first else 12) << 20),
         cost_estimate=pl.CostEstimate(flops=6 * rows * exp_dev * width * hidden, bytes_accessed=6 * exp_dev * width * hidden, transcendentals=rows * exp_dev * hidden),
@@ -174,23 +178,25 @@
     )(mine, *blocks, *([keep_in_hbm(w) for w in weights] if first else weights))
 
 
-def join_kernel(near_ref, other_ref, *out_refs):
+def join_kernel(near_ref, *refs, pieces):
+    others, out_refs = refs[:pieces], refs[pieces:]
     step = out_refs[0].shape[0]
+    other = jnp.concatenate([ref[...] for ref in others], axis=0) if pieces > 1 else others[0][...]
     for i, ref in enumerate(out_refs):
-        part = near_ref[pl.ds(i * step, step), :] + other_ref[pl.ds(i * step, step), :].astype(jnp.float32)
+        part = near_ref[pl.ds(i * step, step), :] + other[i * step : (i + 1) * step, :].astype(jnp.float32)
         ref[...] = part.astype(ref.dtype)
 
 
-def join(near, other, types):
+def join(near, others, types):
     step = near.shape[0] // len(types)
     return pl.pallas_call(
-        join_kernel,
+        functools.partial(join_kernel, pieces=len(others)),
         out_shape=tuple(jax.ShapeDtypeStruct((step, near.shape[1]), t) for t in types),
-        in_specs=[VMEM, VMEM],
+        in_specs=[VMEM] * (1 + len(others)),
         out_specs=(VMEM,) * len(types),
         compiler_params=pltpu.CompilerParams(vmem_limit_bytes=16 << 20),
-        name="join",
-    )(near, other)
+        name=f"join_{near.shape[0]}",
+    )(near, *others)
 
 
 def total_kernel(*refs):
@@ -200,13 +206,14 @@
     refs[-1][...] = total.astype(refs[-1].dtype)
 
 
-def add_up(parts, dtype):
+def add_up(parts, dtype, flops=None):
     return pl.pallas_call(
         total_kernel,
         out_shape=jax.ShapeDtypeStruct(parts[0].shape, dtype),
         in_specs=[VMEM] * len(parts),
         out_specs=VMEM,
         compiler_params=pltpu.CompilerParams(vmem_limit_bytes=16 << 20),
+        cost_estimate=flops and pl.CostEstimate(flops=flops, bytes_accessed=flops // 100, transcendentals=0),
         name="total",
     )(*parts)
 
@@ -217,13 +224,14 @@
     exp_dev, width = w_gate.shape[:2]
     top = expert_ids.shape[1]
 
-    def along_z(t, dz):
-        return lax.ppermute(t, "node", [(i, i ^ dz) for i in range(n_node)])
-
     def along_x(t, dx):
         return lax.ppermute(t, "rank", [(i, i ^ (dx * cores)) for i in range(n_rank)])
 
     def to_chip(t, dz, dx):
+        if dz == 0:
+            return along_x(t, dx)
+        if dx == 0:
+            return lax.ppermute(t, "node", [(i, i ^ dz) for i in range(n_node)])
         step = dz * n_rank + dx * cores
         return lax.ppermute(t, ("node", "rank"), [(i, i ^ step) for i in range(n_node * n_rank)])
 
@@ -237,68 +245,56 @@
     own, mine = prepare(tokens, expert_ids, combine_weights, slot_plan, exp_dev, n_rank)
     near, far, sums, weights = {}, {}, {}, (w_gate, w_up, w_down)
 
-    def run(group, first, *deps):
-        blocks = [near[c] for c in group] + [far[c] for c in group]
-        return ffn(after(mine, *deps), blocks, weights, top, first)
-
-    def settle(group, keep, give):
-        types = [jnp.float32 if dx == 0 and dz != 2 else jnp.bfloat16 for dz, dx in group]
-        for c, part in zip(group, join(keep, swap(give), types), strict=True):
+    def run(group, last, pieces=1):
+        blocks = sum([near[c] for c in group] + [far[c] for c in group], [])
+        keep, *give = ffn(after(mine, *last), blocks, weights, top, weights[0] is w_gate, pieces)
+        return keep, give[:pieces], give[pieces:] or weights
+
+    def settle(group, keep, others, wide):
+        types = [jnp.float32 if c in wide else jnp.bfloat16 for c in group]
+        for c, part in zip(group, join(keep, others, types), strict=True):
             sums[c] = part
 
-    def hop(t, dz):
+    home, across = [(0, 0)], [(0, dx) for dx in xs[1:]]
+    column, corner = [(dz, 0) for dz in zs[2:]], [(dz, dx) for dz in zs[2:] for dx in xs[1:]]
+    close = [(dz, dx) for dz in zs[1:2] for dx in xs]
+    wide = home + [(dz, 0) for dz in zs[1:] if dz != 2]
+
+    near[0, 0] = [own]
+    for c in across + close + column:
+        near[c] = [to_chip(own, *c)]
+    far[0, 0] = [swap(own)]
+    keep, give, weights = run(home, [])
+    settle(home, keep, [swap(t) for t in give], wide)
+    names = across + close + column
+    near |= dict(zip(names, after([near[c] for c in names], give), strict=True))
+
+    for dz, _ in reversed(column):
         for dx in xs[1:]:
-            near[dz, dx] = along_x(t, dx)
-
-    near[0, 0] = own
-    if n_node > 3:
-        near[3, 0] = along_z(own, 3)
-    if n_node > 1:
-        near[1, 0] = along_z(own, 1)
-    hop(own, 0)
-    early = [(0, dx) for dx in xs[1:]]
-    for dz in zs[2:]:
-        if dz != 3:
-            near[dz, 0] = along_z(after(own, *[near[c] for c in early]), dz)
-    far[0, 0] = swap(own)
-    if n_node > 1:
-        hop(near[1, 0], 1)
-        early += [(1, dx) for dx in xs]
-    for c in early:
-        far[c] = swap(near[c])
-    keep0, give0, *weights = run([(0, 0)], True)
-    settle([(0, 0)], keep0, give0)
-
-    column, corner = [(dz, 0) for dz in zs[2:]], [(dz, dx) for dz in zs[2:] for dx in xs[1:]]
-    for dz in zs[2:]:
-        near[dz, 0] = after(near[dz, 0], give0)
-        hop(near[dz, 0], dz)
-        far[dz, 0] = swap(near[dz, 0])
-    last = give0
-    if early:
-        keep1, give1 = run(early, False, give0)
-        last = give1
-    if column:
-        keep2, give2 = run(column, False, last)
-        last = give2
-        for c in corner:
-            near[c] = after(near[c], give2)
-            far[c] = swap(near[c])
-        settle(column, keep2, give2)
-    if early:
-        settle(early, after(keep1, last), give1)
-    if corner:
-        keep3, give3 = run(corner, False, *[sums[c] for c in column])
-        settle(corner, keep3, give3)
-
-    parts = [sums[0, 0]] + [along_x(sums[0, dx], dx) for dx in xs[1:]]
-    for dz in zs[1:]:
-        if dz == 2:
-            parts += [along_z(sums[dz, 0], dz)] + [to_chip(sums[dz, dx], dz, dx) for dx in xs[1:]]
-        else:
-            merged = add_up([sums[dz, 0]] + [along_x(sums[dz, dx], dx) for dx in xs[1:]], jnp.bfloat16)
-            parts.append(along_z(merged, dz))
-    return add_up(parts, tokens.dtype)
+            near[dz, dx] = [along_x(t, dx) for t in near[dz, 0]]
+    for c in names:
+        far[c] = [swap(t) for t in near[c]]
+    last, waits = give, []
+    for group in (column, across + close, corner):
+        if not group:
+            continue
+        if group is corner:
+            for c in group:
+                near[c] = after(near[c], last)
+                far[c] = [swap(t) for t in near[c]]
+        keep, last, _ = run(group, last + (waits if group is corner else []))
+        settle(group, keep, [swap(t) for t in last], wide)
+        if group is column:
+            waits = [sums[c] for c in group]
+
+    def send(c):
+        more = [along_x(sums[c[0], dx], dx) for dx in xs[1:]] if c[0] not in (0, 2) else []
+        return to_chip(add_up([sums[c]] + more, jnp.bfloat16) if more else sums[c], *c)
+
+    early = [(dz, dx) for dz in zs[2:3] for dx in xs] + across
+    late = [c for c in across + [(dz, 0) for dz in zs[1:]] if c not in early]
+    part = add_up([sums[0, 0]] + [send(c) for c in early], jnp.float32, 10**10) if early else sums[0, 0]
+    return add_up([part] + [send(c) for c in late], tokens.dtype)
 
 
 def power_of_two(n):

time: 57.4 us -> 52.3 us (0.911)
  starting transfers between devices: 22.5 us -> 17.7 us
    ppermute x7 -> x6, waiting for transfers between devices: 0.88 us -> 9.88 us  [along_x(): return lax.ppermute(t, 'rank', [(i, i ^ dx * cores) for i in range(n_rank)])]
    ppermute x1 -> x2, waiting for transfers between devices: 6.54 us -> 1.37 us  [to_chip(): lax.ppermute(t, ('node', 'rank'), [(i, i ^ step) for i in range(n_node *...]
    ppermute x6, waiting for transfers between devices: 11.1 us -> 7.45 us  [to_chip(): return lax.ppermute(t, 'node', [(i, i ^ dz) for i in range(n_node)])]
    ppermute x6, starting transfers between devices: 8.89 us -> 6.11 us  [to_chip(): return lax.ppermute(t, 'node', [(i, i ^ dz) for i in range(n_node)])]
    ppermute x7 -> x6, starting transfers between devices: 8.29 us -> 6.1 us  [along_x(): return lax.ppermute(t, 'rank', [(i, i ^ dx * cores) for i in range(n_rank)])]
    ppermute x12, starting transfers between devices: 1.65 us -> 2.76 us  [swap(): return lax.ppermute(t, 'rank', [(i, i ^ 1) for i in range(n_rank)])]
    ppermute x1 -> x2, starting transfers between devices: 3.71 us -> 2.73 us  [to_chip(): lax.ppermute(t, ('node', 'rank'), [(i, i ^ step) for i in range(n_node *...]
  transfers between devices with their start and end apart: 26 -> 26, of which waited for: 12 -> 11; matrix products, arithmetic and copies ran while one was open for 0% -> 0% of each run, Pallas kernels for 22% -> 24%
where the time goes in v3:
time: 52.3 us; the launch traced here: 51.9 us
  waiting for transfers between devices  19.7 us (38%)
  starting transfers between devices  17.7 us (34%)
  Pallas kernels  14.4 us (28%)
    pallas_call x4, Pallas kernels, ffn(): pl.pallas_call(functools.partial(first_ffn_kernel if first else ffn_kerne...  12.4 us
    ppermute x6, waiting for transfers between devices, along_x(): return lax.ppermute(t, 'rank', [(i, i ^ dx * cores) for i in range(n_rank)])  9.88 us
    ppermute x6, waiting for transfers between devices, to_chip(): return lax.ppermute(t, 'node', [(i, i ^ dz) for i in range(n_node)])  7.45 us
    ppermute x6, starting transfers between devices, to_chip(): return lax.ppermute(t, 'node', [(i, i ^ dz) for i in range(n_node)])  6.11 us
    ppermute x6, starting transfers between devices, along_x(): return lax.ppermute(t, 'rank', [(i, i ^ dx * cores) for i in range(n_rank)])  6.1 us
    ppermute x12, starting transfers between devices, swap(): return lax.ppermute(t, 'rank', [(i, i ^ 1) for i in range(n_rank)])  2.76 us
    ppermute x2, starting transfers between devices, to_chip(): lax.ppermute(t, ('node', 'rank'), [(i, i ^ step) for i in range(n_node *...  2.73 us
    ppermute x2, waiting for transfers between devices, to_chip(): lax.ppermute(t, ('node', 'rank'), [(i, i ^ step) for i in range(n_node *...  1.37 us
  transfers between devices with their start and end apart: 26, of which 11 were waited for; matrix products, arithmetic and copies ran while one was open for 0% of the time, Pallas kernels for 24%

profile of v3, /device:TPU:8, one launch (start us, length us, event | category | flops | bytes accessed | tf_op | source)
XLA Modules:
  0.0 51.9 jit_solution(6516087812069709699)
XLA Ops:
  0.0 1.0 %prepare.1 = (bf16[32,2176]{1,0:T(8,128)(2,1)S(1)}, f32[8,128]{1,0:T(8,128)S(1)}) custom-call(bf16[32,2048]{1,0:T(8,128)(2,1)} %tokens_in.1, s32[10,32]{1,0:T(8,128)} %bitcast.2, s32[10,32]{1,0:T(8,128)} %bitcast.3, s32[32]{0:T(128)} %plan_in.1), custom_call_target="tpu_custom_call" | custom-call | tf_op jit(solution)/shard_map/prepare/pallas_call | solution.py:90
  1.0 0.1 collective-permute-start
  1.1 1.6 %collective-permute-start.6 = (bf16[32,2176]{1,0:T(8,128)(2,1)S(1)}, bf16[32,2176]{1,0:T(8,128)(2,1)S(1)}, u32[]{:S(2)}, u32[]{:S(2)}) collective-permute-start(bf16[32,2176]{1,0:T(8,128)(2,1)S(1)} %get-tuple-element.36.refs_0_), channel_id=1, source_target_pairs={{0,12},{4,8},{8,4},{12,0},{1,13},{5,9},{9,5},{13,1},{2,14},{6,10},... | collective-permute-start | bytes 417800 | tf_op jit(solution)/shard_map/ppermute | solution.py:234
  2.7 1.1 %collective-permute-start.5 = (bf16[32,2176]{1,0:T(8,128)(2,1)S(1)}, bf16[32,2176]{1,0:T(8,128)(2,1)S(1)}, u32[]{:S(2)}, u32[]{:S(2)}) collective-permute-start(bf16[32,2176]{1,0:T(8,128)(2,1)S(1)} %get-tuple-element.36.refs_0_), channel_id=1, source_target_pairs={{0,8},{4,12},{8,0},{12,4},{1,9},{5,13},{9,1},{13,5},{2,10},{6,14},... | collective-permute-start | bytes 417800 | tf_op jit(solution)/shard_map/ppermute | solution.py:234
  3.8 2.3 %collective-permute-start.4 = (bf16[32,2176]{1,0:T(8,128)(2,1)S(1)}, bf16[32,2176]{1,0:T(8,128)(2,1)S(1)}, u32[]{:S(2)}, u32[]{:S(2)}) collective-permute-start(bf16[32,2176]{1,0:T(8,128)(2,1)S(1)} %get-tuple-element.36.refs_0_), channel_id=1, source_target_pairs={{0,6},{1,7},{2,4},{3,5},{4,2},{5,3},{6,0},{7,1},{8,14},{9,15},{10,... | collective-permute-start | bytes 417800 | tf_op jit(solution)/shard_map/ppermute | solution.py:236
  6.1 0.8 %collective-permute-start.3 = (bf16[32,2176]{1,0:T(8,128)(2,1)S(1)}, bf16[32,2176]{1,0:T(8,128)(2,1)S(1)}, u32[]{:S(2)}, u32[]{:S(2)}) collective-permute-start(bf16[32,2176]{1,0:T(8,128)(2,1)S(1)} %get-tuple-element.36.refs_0_), channel_id=1, source_target_pairs={{0,4},{4,0},{8,12},{12,8},{1,5},{5,1},{9,13},{13,9},{2,6},{6,2},{1... | collective-permute-start | bytes 417800 | tf_op jit(solution)/shard_map/ppermute | solution.py:234
  6.9 0.4 collective-permute-start.2
  7.3 5.2 %ffn_first_64.1 = (f32[32,2048]{1,0:T(8,128)S(1)}, bf16[32,2048]{1,0:T(8,128)(2,1)S(1)}, bf16[2,2048,512]{2,1,0:T(8,128)(2,1)S(1)}, bf16[2,2048,512]{2,1,0:T(8,128)(2,1)S(1)}, bf16[2,512,2048]{2,1,0:T(8,128)(2,1)S(1)}) custom-call(f32[8,128]{1,0:T(8,128)S(1)} %get-tuple-element.54.mine_ref, bf16[32,2176]{1,0:T(8,128)(2,1)S(1)} %get-tuple-element.36.refs_0_, ...), custom_call_target="tpu_custom_call" | custom-call | flops 805306368 | bytes 12582912 | tf_op jit(solution)/shard_map/ffn_first_64/pallas_call | solution.py:169
  12.5 1.0 %collective-permute-done.6.refs_1_ = bf16[32,2176]{1,0:T(8,128)(2,1)S(1)} collective-permute-done((bf16[32,2176]{1,0:T(8,128)(2,1)S(1)}, bf16[32,2176]{1,0:T(8,128)(2,1)S(1)}, u32[]{:S(2)}, u32[]{:S(2)}) %collective-permute-start.6) | collective-permute-done | bytes 139296 | tf_op jit(solution)/shard_map/ppermute | solution.py:234
  13.6 1.7 %collective-permute-done.5.refs_0_ = bf16[32,2176]{1,0:T(8,128)(2,1)S(1)} collective-permute-done((bf16[32,2176]{1,0:T(8,128)(2,1)S(1)}, bf16[32,2176]{1,0:T(8,128)(2,1)S(1)}, u32[]{:S(2)}, u32[]{:S(2)}) %collective-permute-start.5) | collective-permute-done | bytes 139296 | tf_op jit(solution)/shard_map/ppermute | solution.py:234
  15.2 1.4 %collective-permute-done.4.refs_2_ = bf16[32,2176]{1,0:T(8,128)(2,1)S(1)} collective-permute-done((bf16[32,2176]{1,0:T(8,128)(2,1)S(1)}, bf16[32,2176]{1,0:T(8,128)(2,1)S(1)}, u32[]{:S(2)}, u32[]{:S(2)}) %collective-permute-start.4) | collective-permute-done | bytes 139296 | tf_op jit(solution)/shard_map/ppermute | solution.py:236
  16.6 1.6 %collective-permute-done.3.refs_1_ = bf16[32,2176]{1,0:T(8,128)(2,1)S(1)} collective-permute-done((bf16[32,2176]{1,0:T(8,128)(2,1)S(1)}, bf16[32,2176]{1,0:T(8,128)(2,1)S(1)}, u32[]{:S(2)}, u32[]{:S(2)}) %collective-permute-start.3) | collective-permute-done | bytes 139296 | tf_op jit(solution)/shard_map/ppermute | solution.py:234
  18.2 0.5 collective-permute-start.8
  18.7 1.5 %collective-permute-start.14 = (bf16[32,2176]{1,0:T(8,128)(2,1)S(1)}, bf16[32,2176]{1,0:T(8,128)(2,1)S(1)}, u32[]{:S(2)}, u32[]{:S(2)}) collective-permute-start(bf16[32,2176]{1,0:T(8,128)(2,1)S(1)} %collective-permute-done.5.refs_0_), channel_id=1, source_target_pairs={{0,2},{1,3},{2,0},{3,1},{4,6},{5,7},{6,4},{7,5},{8,10},{9,11},{10,... | collective-permute-start | bytes 417800 | tf_op jit(solution)/shard_map/ppermute | solution.py:228
  20.2 0.5 %collective-permute-start.15 = (bf16[32,2176]{1,0:T(8,128)(2,1)S(1)}, bf16[32,2176]{1,0:T(8,128)(2,1)S(1)}, u32[]{:S(2)}, u32[]{:S(2)}) collective-permute-start(bf16[32,2176]{1,0:T(8,128)(2,1)S(1)} %collective-permute-done.6.refs_1_), channel_id=1, source_target_pairs={{0,2},{1,3},{2,0},{3,1},{4,6},{5,7},{6,4},{7,5},{8,10},{9,11},{10,... | collective-permute-start | bytes 417800 | tf_op jit(solution)/shard_map/ppermute | solution.py:228
  20.8 0.0 collective-permute-start.11
  20.8 0.5 collective-permute-start.12
  21.3 0.1 collective-permute-start.13
  21.3 2.1 %ffn_128.2 = (f32[64,2048]{1,0:T(8,128)S(1)}, bf16[64,2048]{1,0:T(8,128)(2,1)S(1)}) custom-call(f32[8,128]{1,0:T(8,128)S(1)} %get-tuple-element.54.mine_ref, bf16[32,2176]{1,0:T(8,128)(2,1)S(1)} %collective-permute-done.5.refs_0_, bf16[32,2176]{1,0:T(8,128)(2,1)S(1)} %collective-permute-done.6.refs_1_, bf16[32,2176]{1,0:T(8,128)(2,1)S(1)} %collective-permute-done.7.refs_2_, ...), custom_call_target="tpu_custom_call" | custom-call | flops 1610612736 | bytes 12582912 | tf_op jit(solution)/shard_map/ffn_128/pallas_call | solution.py:169
  23.5 0.5 collective-permute-start.9
  24.0 0.0 collective-permute-done.12.refs_4_
  24.0 0.0 collective-permute-done.13.refs_5_
  24.0 2.9 %ffn_192.1 = (f32[96,2048]{1,0:T(8,128)S(1)}, bf16[96,2048]{1,0:T(8,128)(2,1)S(1)}) custom-call(f32[8,128]{1,0:T(8,128)S(1)} %get-tuple-element.54.mine_ref, bf16[32,2176]{1,0:T(8,128)(2,1)S(1)} %collective-permute-done.2.refs_0_, bf16[32,2176]{1,0:T(8,128)(2,1)S(1)} %collective-permute-done.3.refs_1_, bf16[32,2176]{1,0:T(8,128)(2,1)S(1)} %collective-permute-done.4.refs_2_, ...), custom_call_target="tpu_custom_call" | custom-call | flops 2415919104 | bytes 12582912 | tf_op jit(solution)/shard_map/ffn_192/pallas_call | solution.py:169
  26.9 0.4 collective-permute-done.15.refs_1_
  27.3 0.0 collective-permute-done.14.refs_0_
  27.3 0.0 collective-permute-start.16
  27.3 0.5 collective-permute-start.17
  27.8 0.0 collective-permute-start.20
  27.8 0.1 join_64.2
  27.9 0.8 %collective-permute-done.16.refs_2_ = bf16[32,2176]{1,0:T(8,128)(2,1)S(1)} collective-permute-done((bf16[32,2176]{1,0:T(8,128)(2,1)S(1)}, bf16[32,2176]{1,0:T(8,128)(2,1)S(1)}, u32[]{:S(2)}, u32[]{:S(2)}) %collective-permute-start.16) | collective-permute-done | bytes 139296 | tf_op jit(solution)/shard_map/ppermute | solution.py:239
  28.7 0.2 collective-permute-done.17.refs_3_
  28.9 2.1 %ffn_128.3 = (f32[64,2048]{1,0:T(8,128)S(1)}, bf16[64,2048]{1,0:T(8,128)(2,1)S(1)}) custom-call(f32[8,128]{1,0:T(8,128)S(1)} %get-tuple-element.54.mine_ref, bf16[32,2176]{1,0:T(8,128)(2,1)S(1)} %collective-permute-done.14.refs_0_, bf16[32,2176]{1,0:T(8,128)(2,1)S(1)} %collective-permute-done.15.refs_1_, ...), custom_call_target="tpu_custom_call" | custom-call | flops 1610612736 | bytes 12582912 | tf_op jit(solution)/shard_map/ffn_128/pallas_call | solution.py:169
  31.0 0.4 collective-permute-start.18
  31.4 0.2 collective-permute-start.1
  31.6 2.4 %collective-permute-start.10 = (bf16[32,2048]{1,0:T(8,128)(2,1)S(1)}, bf16[32,2048]{1,0:T(8,128)(2,1)S(1)}, u32[]{:S(2)}, u32[]{:S(2)}) collective-permute-start(bf16[32,2048]{1,0:T(8,128)(2,1)S(1)} %get-tuple-element.47), channel_id=1, source_target_pairs={{0,8},{4,12},{8,0},{12,4},{1,9},{5,13},{9,1},{13,5},{2,10},{6,14},... | collective-permute-start | bytes 393224 | tf_op jit(solution)/shard_map/ppermute | solution.py:234
  34.0 0.1 join_96.1
  34.1 1.6 %collective-permute-start.22 = (bf16[32,2048]{1,0:T(8,128)(2,1)S(1)}, bf16[32,2048]{1,0:T(8,128)(2,1)S(1)}, u32[]{:S(2)}, u32[]{:S(2)}) collective-permute-start(bf16[32,2048]{1,0:T(8,128)(2,1)S(1)} %get-tuple-element.63), channel_id=1, source_target_pairs={{0,2},{1,3},{2,0},{3,1},{4,6},{5,7},{6,4},{7,5},{8,10},{9,11},{10,... | collective-permute-start | bytes 393224 | tf_op jit(solution)/shard_map/ppermute | solution.py:228
  35.7 0.6 %collective-permute-start.24 = (bf16[32,2048]{1,0:T(8,128)(2,1)S(1)}, bf16[32,2048]{1,0:T(8,128)(2,1)S(1)}, u32[]{:S(2)}, u32[]{:S(2)}) collective-permute-start(bf16[32,2048]{1,0:T(8,128)(2,1)S(1)} %get-tuple-element.64), channel_id=1, source_target_pairs={{0,2},{1,3},{2,0},{3,1},{4,6},{5,7},{6,4},{7,5},{8,10},{9,11},{10,... | collective-permute-start | bytes 393224 | tf_op jit(solution)/shard_map/ppermute | solution.py:228
  36.3 1.5 %collective-permute-start.21 = (bf16[32,2048]{1,0:T(8,128)(2,1)S(1)}, bf16[32,2048]{1,0:T(8,128)(2,1)S(1)}, u32[]{:S(2)}, u32[]{:S(2)}) collective-permute-start(bf16[32,2048]{1,0:T(8,128)(2,1)S(1)} %get-tuple-element.61), channel_id=1, source_target_pairs={{0,2},{1,3},{2,0},{3,1},{4,6},{5,7},{6,4},{7,5},{8,10},{9,11},{10,... | collective-permute-start | bytes 393224 | tf_op jit(solution)/shard_map/ppermute | solution.py:228
  37.8 0.4 collective-permute-start.19
  38.3 2.2 %collective-permute-done.22.refs_1_ = bf16[32,2048]{1,0:T(8,128)(2,1)S(1)} collective-permute-done((bf16[32,2048]{1,0:T(8,128)(2,1)S(1)}, bf16[32,2048]{1,0:T(8,128)(2,1)S(1)}, u32[]{:S(2)}, u32[]{:S(2)}) %collective-permute-start.22) | collective-permute-done | bytes 131104 | tf_op jit(solution)/shard_map/ppermute | solution.py:228
  40.5 0.1 collective-permute-start.23
  40.6 5.5 %collective-permute-done.24.refs_1_ = bf16[32,2048]{1,0:T(8,128)(2,1)S(1)} collective-permute-done((bf16[32,2048]{1,0:T(8,128)(2,1)S(1)}, bf16[32,2048]{1,0:T(8,128)(2,1)S(1)}, u32[]{:S(2)}, u32[]{:S(2)}) %collective-permute-start.24) | collective-permute-done | bytes 131104 | tf_op jit(solution)/shard_map/ppermute | solution.py:228
  46.2 0.1 collective-permute-start.25
  46.2 1.7 %collective-permute-done.21.refs_3_ = bf16[32,2048]{1,0:T(8,128)(2,1)S(1)} collective-permute-done((bf16[32,2048]{1,0:T(8,128)(2,1)S(1)}, bf16[32,2048]{1,0:T(8,128)(2,1)S(1)}, u32[]{:S(2)}, u32[]{:S(2)}) %collective-permute-start.21) | collective-permute-done | bytes 131104 | tf_op jit(solution)/shard_map/ppermute | solution.py:228
  48.0 0.1 total.4.refs_0_
  48.1 3.1 %collective-permute-done.25.refs_2_ = bf16[32,2048]{1,0:T(8,128)(2,1)S(1)} collective-permute-done((bf16[32,2048]{1,0:T(8,128)(2,1)S(1)}, bf16[32,2048]{1,0:T(8,128)(2,1)S(1)}, u32[]{:S(2)}, u32[]{:S(2)}) %collective-permute-start.25) | collective-permute-done | bytes 131104 | tf_op jit(solution)/shard_map/ppermute | solution.py:234
  51.2 0.7 %total.7 = bf16[32,2048]{1,0:T(8,128)(2,1)} custom-call(f32[32,2048]{1,0:T(8,128)S(1)} %total.4.refs_0_, bf16[32,2048]{1,0:T(8,128)(2,1)S(1)} %collective-permute-done.23.refs_1_, bf16[32,2048]{1,0:T(8,128)(2,1)S(1)} %collective-permute-done.25.refs_2_), custom_call_target="tpu_custom_call" | custom-call | tf_op jit(solution)/shard_map/total/pallas_call | solution.py:210
  (17 shorter events, 0.2 us)
Async XLA Ops:
  1.0 5.9 %collective-permute-start = (bf16[32,2176]{1,0:T(8,128)(2,1)S(1)}, bf16[32,2176]{1,0:T(8,128)(2,1)S(1)}, u32[]{:S(2)}, u32[]{:S(2)}) collective-permute-start(bf16[32,2176]{1,0:T(8,128)(2,1)S(1)} %get-tuple-element.36.refs_0_), channel_id=1, source_target_pairs={{0,1},{1,0},{2,3},{3,2},{4,5},{5,4},{6,7},{7,6},{8,9},{9,8},{10,11... | collective-permute-start | bytes 417800 | tf_op jit(solution)/shard_map/ppermute | solution.py:239
  1.1 12.5 %collective-permute-start.6 = (bf16[32,2176]{1,0:T(8,128)(2,1)S(1)}, bf16[32,2176]{1,0:T(8,128)(2,1)S(1)}, u32[]{:S(2)}, u32[]{:S(2)}) collective-permute-start(bf16[32,2176]{1,0:T(8,128)(2,1)S(1)} %get-tuple-element.36.refs_0_), channel_id=1, source_target_pairs={{0,12},{4,8},{8,4},{12,0},{1,13},{5,9},{9,5},{13,1},{2,14},{6,10},... | collective-permute-start | bytes 417800 | tf_op jit(solution)/shard_map/ppermute | solution.py:234
  2.7 12.5 %collective-permute-start.5 = (bf16[32,2176]{1,0:T(8,128)(2,1)S(1)}, bf16[32,2176]{1,0:T(8,128)(2,1)S(1)}, u32[]{:S(2)}, u32[]{:S(2)}) collective-permute-start(bf16[32,2176]{1,0:T(8,128)(2,1)S(1)} %get-tuple-element.36.refs_0_), channel_id=1, source_target_pairs={{0,8},{4,12},{8,0},{12,4},{1,9},{5,13},{9,1},{13,5},{2,10},{6,14},... | collective-permute-start | bytes 417800 | tf_op jit(solution)/shard_map/ppermute | solution.py:234
  3.8 12.8 %collective-permute-start.4 = (bf16[32,2176]{1,0:T(8,128)(2,1)S(1)}, bf16[32,2176]{1,0:T(8,128)(2,1)S(1)}, u32[]{:S(2)}, u32[]{:S(2)}) collective-permute-start(bf16[32,2176]{1,0:T(8,128)(2,1)S(1)} %get-tuple-element.36.refs_0_), channel_id=1, source_target_pairs={{0,6},{1,7},{2,4},{3,5},{4,2},{5,3},{6,0},{7,1},{8,14},{9,15},{10,... | collective-permute-start | bytes 417800 | tf_op jit(solution)/shard_map/ppermute | solution.py:236
  6.1 12.1 %collective-permute-start.3 = (bf16[32,2176]{1,0:T(8,128)(2,1)S(1)}, bf16[32,2176]{1,0:T(8,128)(2,1)S(1)}, u32[]{:S(2)}, u32[]{:S(2)}) collective-permute-start(bf16[32,2176]{1,0:T(8,128)(2,1)S(1)} %get-tuple-element.36.refs_0_), channel_id=1, source_target_pairs={{0,4},{4,0},{8,12},{12,8},{1,5},{5,1},{9,13},{13,9},{2,6},{6,2},{1... | collective-permute-start | bytes 417800 | tf_op jit(solution)/shard_map/ppermute | solution.py:234
  6.9 11.3 %collective-permute-start.2 = (bf16[32,2176]{1,0:T(8,128)(2,1)S(1)}, bf16[32,2176]{1,0:T(8,128)(2,1)S(1)}, u32[]{:S(2)}, u32[]{:S(2)}) collective-permute-start(bf16[32,2176]{1,0:T(8,128)(2,1)S(1)} %get-tuple-element.36.refs_0_), channel_id=1, source_target_pairs={{0,2},{1,3},{2,0},{3,1},{4,6},{5,7},{6,4},{7,5},{8,10},{9,11},{10,... | collective-permute-start | bytes 417800 | tf_op jit(solution)/shard_map/ppermute | solution.py:228
  18.2 2.5 %collective-permute-start.7 = (bf16[32,2176]{1,0:T(8,128)(2,1)S(1)}, bf16[32,2176]{1,0:T(8,128)(2,1)S(1)}, u32[]{:S(2)}, u32[]{:S(2)}) collective-permute-start(bf16[32,2176]{1,0:T(8,128)(2,1)S(1)} %collective-permute-done.5.refs_0_), channel_id=1, source_target_pairs={{0,1},{1,0},{2,3},{3,2},{4,5},{5,4},{6,7},{7,6},{8,9},{9,8},{10,11... | collective-permute-start | bytes 417800 | tf_op jit(solution)/shard_map/ppermute | solution.py:239
  18.2 3.1 %collective-permute-start.8 = (bf16[32,2176]{1,0:T(8,128)(2,1)S(1)}, bf16[32,2176]{1,0:T(8,128)(2,1)S(1)}, u32[]{:S(2)}, u32[]{:S(2)}) collective-permute-start(bf16[32,2176]{1,0:T(8,128)(2,1)S(1)} %collective-permute-done.6.refs_1_), channel_id=1, source_target_pairs={{0,1},{1,0},{2,3},{3,2},{4,5},{5,4},{6,7},{7,6},{8,9},{9,8},{10,11... | collective-permute-start | bytes 417800 | tf_op jit(solution)/shard_map/ppermute | solution.py:239
  18.7 8.6 %collective-permute-start.14 = (bf16[32,2176]{1,0:T(8,128)(2,1)S(1)}, bf16[32,2176]{1,0:T(8,128)(2,1)S(1)}, u32[]{:S(2)}, u32[]{:S(2)}) collective-permute-start(bf16[32,2176]{1,0:T(8,128)(2,1)S(1)} %collective-permute-done.5.refs_0_), channel_id=1, source_target_pairs={{0,2},{1,3},{2,0},{3,1},{4,6},{5,7},{6,4},{7,5},{8,10},{9,11},{10,... | collective-permute-start | bytes 417800 | tf_op jit(solution)/shard_map/ppermute | solution.py:228
  20.2 7.1 %collective-permute-start.15 = (bf16[32,2176]{1,0:T(8,128)(2,1)S(1)}, bf16[32,2176]{1,0:T(8,128)(2,1)S(1)}, u32[]{:S(2)}, u32[]{:S(2)}) collective-permute-start(bf16[32,2176]{1,0:T(8,128)(2,1)S(1)} %collective-permute-done.6.refs_1_), channel_id=1, source_target_pairs={{0,2},{1,3},{2,0},{3,1},{4,6},{5,7},{6,4},{7,5},{8,10},{9,11},{10,... | collective-permute-start | bytes 417800 | tf_op jit(solution)/shard_map/ppermute | solution.py:228
  20.8 2.7 %collective-permute-start.11 = (bf16[32,2176]{1,0:T(8,128)(2,1)S(1)}, bf16[32,2176]{1,0:T(8,128)(2,1)S(1)}, u32[]{:S(2)}, u32[]{:S(2)}) collective-permute-start(bf16[32,2176]{1,0:T(8,128)(2,1)S(1)} %collective-permute-done.2.refs_0_), channel_id=1, source_target_pairs={{0,1},{1,0},{2,3},{3,2},{4,5},{5,4},{6,7},{7,6},{8,9},{9,8},{10,11... | collective-permute-start | bytes 417800 | tf_op jit(solution)/shard_map/ppermute | solution.py:239
  20.8 3.2 %collective-permute-start.12 = (bf16[32,2176]{1,0:T(8,128)(2,1)S(1)}, bf16[32,2176]{1,0:T(8,128)(2,1)S(1)}, u32[]{:S(2)}, u32[]{:S(2)}) collective-permute-start(bf16[32,2176]{1,0:T(8,128)(2,1)S(1)} %collective-permute-done.3.refs_1_), channel_id=1, source_target_pairs={{0,1},{1,0},{2,3},{3,2},{4,5},{5,4},{6,7},{7,6},{8,9},{9,8},{10,11... | collective-permute-start | bytes 417800 | tf_op jit(solution)/shard_map/ppermute | solution.py:239
  21.3 2.7 %collective-permute-start.13 = (bf16[32,2176]{1,0:T(8,128)(2,1)S(1)}, bf16[32,2176]{1,0:T(8,128)(2,1)S(1)}, u32[]{:S(2)}, u32[]{:S(2)}) collective-permute-start(bf16[32,2176]{1,0:T(8,128)(2,1)S(1)} %collective-permute-done.4.refs_2_), channel_id=1, source_target_pairs={{0,1},{1,0},{2,3},{3,2},{4,5},{5,4},{6,7},{7,6},{8,9},{9,8},{10,11... | collective-permute-start | bytes 417800 | tf_op jit(solution)/shard_map/ppermute | solution.py:239
  23.5 4.3 %collective-permute-start.9 = (bf16[64,2048]{1,0:T(8,128)(2,1)S(1)}, bf16[64,2048]{1,0:T(8,128)(2,1)S(1)}, u32[]{:S(2)}, u32[]{:S(2)}) collective-permute-start(bf16[64,2048]{1,0:T(8,128)(2,1)S(1)} %get-tuple-element.46), channel_id=1, source_target_pairs={{0,1},{1,0},{2,3},{3,2},{4,5},{5,4},{6,7},{7,6},{8,9},{9,8},{10,11... | collective-permute-start | bytes 786440 | tf_op jit(solution)/shard_map/ppermute | solution.py:239
  27.3 1.4 %collective-permute-start.16 = (bf16[32,2176]{1,0:T(8,128)(2,1)S(1)}, bf16[32,2176]{1,0:T(8,128)(2,1)S(1)}, u32[]{:S(2)}, u32[]{:S(2)}) collective-permute-start(bf16[32,2176]{1,0:T(8,128)(2,1)S(1)} %collective-permute-done.14.refs_0_), channel_id=1, source_target_pairs={{0,1},{1,0},{2,3},{3,2},{4,5},{5,4},{6,7},{7,6},{8,9},{9,8},{10,11... | collective-permute-start | bytes 417800 | tf_op jit(solution)/shard_map/ppermute | solution.py:239
  27.3 1.6 %collective-permute-start.17 = (bf16[32,2176]{1,0:T(8,128)(2,1)S(1)}, bf16[32,2176]{1,0:T(8,128)(2,1)S(1)}, u32[]{:S(2)}, u32[]{:S(2)}) collective-permute-start(bf16[32,2176]{1,0:T(8,128)(2,1)S(1)} %collective-permute-done.15.refs_1_), channel_id=1, source_target_pairs={{0,1},{1,0},{2,3},{3,2},{4,5},{5,4},{6,7},{7,6},{8,9},{9,8},{10,11... | collective-permute-start | bytes 417800 | tf_op jit(solution)/shard_map/ppermute | solution.py:239
  27.8 6.2 %collective-permute-start.20 = (bf16[96,2048]{1,0:T(8,128)(2,1)S(1)}, bf16[96,2048]{1,0:T(8,128)(2,1)S(1)}, u32[]{:S(2)}, u32[]{:S(2)}) collective-permute-start(bf16[96,2048]{1,0:T(8,128)(2,1)S(1)} %get-tuple-element.52), channel_id=1, source_target_pairs={{0,1},{1,0},{2,3},{3,2},{4,5},{5,4},{6,7},{7,6},{8,9},{9,8},{10,11... | collective-permute-start | bytes 1179656 | tf_op jit(solution)/shard_map/ppermute | solution.py:239
  31.0 4.7 %collective-permute-start.18 = (bf16[64,2048]{1,0:T(8,128)(2,1)S(1)}, bf16[64,2048]{1,0:T(8,128)(2,1)S(1)}, u32[]{:S(2)}, u32[]{:S(2)}) collective-permute-start(bf16[64,2048]{1,0:T(8,128)(2,1)S(1)} %get-tuple-element.58), channel_id=1, source_target_pairs={{0,1},{1,0},{2,3},{3,2},{4,5},{5,4},{6,7},{7,6},{8,9},{9,8},{10,11... | collective-permute-start | bytes 786440 | tf_op jit(solution)/shard_map/ppermute | solution.py:239
  31.4 6.5 %collective-permute-start.1 = (bf16[32,2048]{1,0:T(8,128)(2,1)S(1)}, bf16[32,2048]{1,0:T(8,128)(2,1)S(1)}, u32[]{:S(2)}, u32[]{:S(2)}) collective-permute-start(bf16[32,2048]{1,0:T(8,128)(2,1)S(1)} %get-tuple-element.38), channel_id=1, source_target_pairs={{0,1},{1,0},{2,3},{3,2},{4,5},{5,4},{6,7},{7,6},{8,9},{9,8},{10,11... | collective-permute-start | bytes 393224 | tf_op jit(solution)/shard_map/ppermute | solution.py:239
  31.6 14.7 %collective-permute-start.10 = (bf16[32,2048]{1,0:T(8,128)(2,1)S(1)}, bf16[32,2048]{1,0:T(8,128)(2,1)S(1)}, u32[]{:S(2)}, u32[]{:S(2)}) collective-permute-start(bf16[32,2048]{1,0:T(8,128)(2,1)S(1)} %get-tuple-element.47), channel_id=1, source_target_pairs={{0,8},{4,12},{8,0},{12,4},{1,9},{5,13},{9,1},{13,5},{2,10},{6,14},... | collective-permute-start | bytes 393224 | tf_op jit(solution)/shard_map/ppermute | solution.py:234
  34.1 6.4 %collective-permute-start.22 = (bf16[32,2048]{1,0:T(8,128)(2,1)S(1)}, bf16[32,2048]{1,0:T(8,128)(2,1)S(1)}, u32[]{:S(2)}, u32[]{:S(2)}) collective-permute-start(bf16[32,2048]{1,0:T(8,128)(2,1)S(1)} %get-tuple-element.63), channel_id=1, source_target_pairs={{0,2},{1,3},{2,0},{3,1},{4,6},{5,7},{6,4},{7,5},{8,10},{9,11},{10,... | collective-permute-start | bytes 393224 | tf_op jit(solution)/shard_map/ppermute | solution.py:228
  35.7 10.4 %collective-permute-start.24 = (bf16[32,2048]{1,0:T(8,128)(2,1)S(1)}, bf16[32,2048]{1,0:T(8,128)(2,1)S(1)}, u32[]{:S(2)}, u32[]{:S(2)}) collective-permute-start(bf16[32,2048]{1,0:T(8,128)(2,1)S(1)} %get-tuple-element.64), channel_id=1, source_target_pairs={{0,2},{1,3},{2,0},{3,1},{4,6},{5,7},{6,4},{7,5},{8,10},{9,11},{10,... | collective-permute-start | bytes 393224 | tf_op jit(solution)/shard_map/ppermute | solution.py:228
  36.3 11.7 %collective-permute-start.21 = (bf16[32,2048]{1,0:T(8,128)(2,1)S(1)}, bf16[32,2048]{1,0:T(8,128)(2,1)S(1)}, u32[]{:S(2)}, u32[]{:S(2)}) collective-permute-start(bf16[32,2048]{1,0:T(8,128)(2,1)S(1)} %get-tuple-element.61), channel_id=1, source_target_pairs={{0,2},{1,3},{2,0},{3,1},{4,6},{5,7},{6,4},{7,5},{8,10},{9,11},{10,... | collective-permute-start | bytes 393224 | tf_op jit(solution)/shard_map/ppermute | solution.py:228
  37.8 10.2 %collective-permute-start.19 = (bf16[32,2048]{1,0:T(8,128)(2,1)S(1)}, bf16[32,2048]{1,0:T(8,128)(2,1)S(1)}, u32[]{:S(2)}, u32[]{:S(2)}) collective-permute-start(bf16[32,2048]{1,0:T(8,128)(2,1)S(1)} %get-tuple-element.59), channel_id=1, source_target_pairs={{0,10},{1,11},{2,8},{3,9},{4,14},{5,15},{6,12},{7,13},{8,2},{9,3},... | collective-permute-start | bytes 393224 | tf_op jit(solution)/shard_map/ppermute | solution.py:236
  40.5 7.5 %collective-permute-start.23 = (bf16[32,2048]{1,0:T(8,128)(2,1)S(1)}, bf16[32,2048]{1,0:T(8,128)(2,1)S(1)}, u32[]{:S(2)}, u32[]{:S(2)}) collective-permute-start(bf16[32,2048]{1,0:T(8,128)(2,1)S(1)} %total.5), channel_id=1, source_target_pairs={{0,4},{4,0},{8,12},{12,8},{1,5},{5,1},{9,13},{13,9},{2,6},{6,2},{1... | collective-permute-start | bytes 393224 | tf_op jit(solution)/shard_map/ppermute | solution.py:234
  46.2 5.0 %collective-permute-start.25 = (bf16[32,2048]{1,0:T(8,128)(2,1)S(1)}, bf16[32,2048]{1,0:T(8,128)(2,1)S(1)}, u32[]{:S(2)}, u32[]{:S(2)}) collective-permute-start(bf16[32,2048]{1,0:T(8,128)(2,1)S(1)} %total.6), channel_id=1, source_target_pairs={{0,12},{4,8},{8,4},{12,0},{1,13},{5,9},{9,5},{13,1},{2,14},{6,10},... | collective-permute-start | bytes 393224 | tf_op jit(solution)/shard_map/ppermute | solution.py:234

commit v4 on v3

--- a/solution.py
+++ b/solution.py
@@ -272,7 +272,7 @@
     for dz, _ in reversed(column):
         for dx in xs[1:]:
             near[dz, dx] = [along_x(t, dx) for t in near[dz, 0]]
-    for c in names:
+    for c in column + across + close:
         far[c] = [swap(t) for t in near[c]]
     last, waits = give, []
     for group in (column, across + close, corner):
@@ -289,11 +289,12 @@
 
     def send(c):
         more = [along_x(sums[c[0], dx], dx) for dx in xs[1:]] if c[0] not in (0, 2) else []
-        return to_chip(add_up([sums[c]] + more, jnp.bfloat16) if more else sums[c], *c)
-
-    early = [(dz, dx) for dz in zs[2:3] for dx in xs] + across
+        return to_chip(add_up([sums[c]] + more, jnp.bfloat16, None) if more else sums[c], *c)
+
+    early = [(2, 0)] + [(2, dx) for dx in xs[1:]] + across
     late = [c for c in across + [(dz, 0) for dz in zs[1:]] if c not in early]
-    part = add_up([sums[0, 0]] + [send(c) for c in early], jnp.float32, 10**10) if early else sums[0, 0]
+    part = add_up([sums[0, 0]] + [send(c) for c in early], jnp.float32, 10000000000) if early else sums[0, 0]
+    late = late[::-1]
     return add_up([part] + [send(c) for c in late], tokens.dtype)
 
 

time: 52.3 us -> 52.3 us (level)
  no operation moved by 1% of the time
where the time goes in v4:
time: 52.3 us; the launch traced here: 51.9 us
  waiting for transfers between devices  19.7 us (38%)
  starting transfers between devices  17.7 us (34%)
  Pallas kernels  14.4 us (28%)
    pallas_call x4, Pallas kernels, ffn(): pl.pallas_call(functools.partial(first_ffn_kernel if first else ffn_kerne...  12.4 us
    ppermute x6, waiting for transfers between devices, along_x(): return lax.ppermute(t, 'rank', [(i, i ^ dx * cores) for i in range(n_rank)])  9.88 us
    ppermute x6, waiting for transfers between devices, to_chip(): return lax.ppermute(t, 'node', [(i, i ^ dz) for i in range(n_node)])  7.45 us
    ppermute x6, starting transfers between devices, to_chip(): return lax.ppermute(t, 'node', [(i, i ^ dz) for i in range(n_node)])  6.11 us
    ppermute x6, starting transfers between devices, along_x(): return lax.ppermute(t, 'rank', [(i, i ^ dx * cores) for i in range(n_rank)])  6.1 us
    ppermute x12, starting transfers between devices, swap(): return lax.ppermute(t, 'rank', [(i, i ^ 1) for i in range(n_rank)])  2.76 us
    ppermute x2, starting transfers between devices, to_chip(): lax.ppermute(t, ('node', 'rank'), [(i, i ^ step) for i in range(n_node *...  2.73 us
    ppermute x2, waiting for transfers between devices, to_chip(): lax.ppermute(t, ('node', 'rank'), [(i, i ^ step) for i in range(n_node *...  1.37 us
  transfers between devices with their start and end apart: 26, of which 11 were waited for; matrix products, arithmetic and copies ran while one was open for 0% of the time, Pallas kernels for 24%

profile of v4, /device:TPU:8, one launch (start us, length us, event | category | flops | bytes accessed | tf_op | source)
XLA Modules:
  0.0 51.9 jit_solution(8732956836273011525)
XLA Ops:
  0.0 1.0 %prepare.1 = (bf16[32,2176]{1,0:T(8,128)(2,1)S(1)}, f32[8,128]{1,0:T(8,128)S(1)}) custom-call(bf16[32,2048]{1,0:T(8,128)(2,1)} %tokens_in.1, s32[10,32]{1,0:T(8,128)} %bitcast.2, s32[10,32]{1,0:T(8,128)} %bitcast.3, s32[32]{0:T(128)} %plan_in.1), custom_call_target="tpu_custom_call" | custom-call | tf_op jit(solution)/shard_map/prepare/pallas_call | solution.py:90
  1.0 0.1 collective-permute-start
  1.1 1.6 %collective-permute-start.6 = (bf16[32,2176]{1,0:T(8,128)(2,1)S(1)}, bf16[32,2176]{1,0:T(8,128)(2,1)S(1)}, u32[]{:S(2)}, u32[]{:S(2)}) collective-permute-start(bf16[32,2176]{1,0:T(8,128)(2,1)S(1)} %get-tuple-element.36.refs_0_), channel_id=1, source_target_pairs={{0,12},{4,8},{8,4},{12,0},{1,13},{5,9},{9,5},{13,1},{2,14},{6,10},... | collective-permute-start | bytes 417800 | tf_op jit(solution)/shard_map/ppermute | solution.py:234
  2.7 1.1 %collective-permute-start.5 = (bf16[32,2176]{1,0:T(8,128)(2,1)S(1)}, bf16[32,2176]{1,0:T(8,128)(2,1)S(1)}, u32[]{:S(2)}, u32[]{:S(2)}) collective-permute-start(bf16[32,2176]{1,0:T(8,128)(2,1)S(1)} %get-tuple-element.36.refs_0_), channel_id=1, source_target_pairs={{0,8},{4,12},{8,0},{12,4},{1,9},{5,13},{9,1},{13,5},{2,10},{6,14},... | collective-permute-start | bytes 417800 | tf_op jit(solution)/shard_map/ppermute | solution.py:234
  3.8 2.3 %collective-permute-start.4 = (bf16[32,2176]{1,0:T(8,128)(2,1)S(1)}, bf16[32,2176]{1,0:T(8,128)(2,1)S(1)}, u32[]{:S(2)}, u32[]{:S(2)}) collective-permute-start(bf16[32,2176]{1,0:T(8,128)(2,1)S(1)} %get-tuple-element.36.refs_0_), channel_id=1, source_target_pairs={{0,6},{1,7},{2,4},{3,5},{4,2},{5,3},{6,0},{7,1},{8,14},{9,15},{10,... | collective-permute-start | bytes 417800 | tf_op jit(solution)/shard_map/ppermute | solution.py:236
  6.1 0.8 %collective-permute-start.3 = (bf16[32,2176]{1,0:T(8,128)(2,1)S(1)}, bf16[32,2176]{1,0:T(8,128)(2,1)S(1)}, u32[]{:S(2)}, u32[]{:S(2)}) collective-permute-start(bf16[32,2176]{1,0:T(8,128)(2,1)S(1)} %get-tuple-element.36.refs_0_), channel_id=1, source_target_pairs={{0,4},{4,0},{8,12},{12,8},{1,5},{5,1},{9,13},{13,9},{2,6},{6,2},{1... | collective-permute-start | bytes 417800 | tf_op jit(solution)/shard_map/ppermute | solution.py:234
  6.9 0.4 collective-permute-start.2
  7.3 5.2 %ffn_first_64.1 = (f32[32,2048]{1,0:T(8,128)S(1)}, bf16[32,2048]{1,0:T(8,128)(2,1)S(1)}, bf16[2,2048,512]{2,1,0:T(8,128)(2,1)S(1)}, bf16[2,2048,512]{2,1,0:T(8,128)(2,1)S(1)}, bf16[2,512,2048]{2,1,0:T(8,128)(2,1)S(1)}) custom-call(f32[8,128]{1,0:T(8,128)S(1)} %get-tuple-element.54.mine_ref, bf16[32,2176]{1,0:T(8,128)(2,1)S(1)} %get-tuple-element.36.refs_0_, ...), custom_call_target="tpu_custom_call" | custom-call | flops 805306368 | bytes 12582912 | tf_op jit(solution)/shard_map/ffn_first_64/pallas_call | solution.py:169
  12.5 1.0 %collective-permute-done.6.refs_1_ = bf16[32,2176]{1,0:T(8,128)(2,1)S(1)} collective-permute-done((bf16[32,2176]{1,0:T(8,128)(2,1)S(1)}, bf16[32,2176]{1,0:T(8,128)(2,1)S(1)}, u32[]{:S(2)}, u32[]{:S(2)}) %collective-permute-start.6) | collective-permute-done | bytes 139296 | tf_op jit(solution)/shard_map/ppermute | solution.py:234
  13.6 1.7 %collective-permute-done.5.refs_0_ = bf16[32,2176]{1,0:T(8,128)(2,1)S(1)} collective-permute-done((bf16[32,2176]{1,0:T(8,128)(2,1)S(1)}, bf16[32,2176]{1,0:T(8,128)(2,1)S(1)}, u32[]{:S(2)}, u32[]{:S(2)}) %collective-permute-start.5) | collective-permute-done | bytes 139296 | tf_op jit(solution)/shard_map/ppermute | solution.py:234
  15.2 1.4 %collective-permute-done.4.refs_2_ = bf16[32,2176]{1,0:T(8,128)(2,1)S(1)} collective-permute-done((bf16[32,2176]{1,0:T(8,128)(2,1)S(1)}, bf16[32,2176]{1,0:T(8,128)(2,1)S(1)}, u32[]{:S(2)}, u32[]{:S(2)}) %collective-permute-start.4) | collective-permute-done | bytes 139296 | tf_op jit(solution)/shard_map/ppermute | solution.py:236
  16.6 1.6 %collective-permute-done.3.refs_1_ = bf16[32,2176]{1,0:T(8,128)(2,1)S(1)} collective-permute-done((bf16[32,2176]{1,0:T(8,128)(2,1)S(1)}, bf16[32,2176]{1,0:T(8,128)(2,1)S(1)}, u32[]{:S(2)}, u32[]{:S(2)}) %collective-permute-start.3) | collective-permute-done | bytes 139296 | tf_op jit(solution)/shard_map/ppermute | solution.py:234
  18.2 0.5 collective-permute-start.8
  18.7 1.5 %collective-permute-start.14 = (bf16[32,2176]{1,0:T(8,128)(2,1)S(1)}, bf16[32,2176]{1,0:T(8,128)(2,1)S(1)}, u32[]{:S(2)}, u32[]{:S(2)}) collective-permute-start(bf16[32,2176]{1,0:T(8,128)(2,1)S(1)} %collective-permute-done.5.refs_0_), channel_id=1, source_target_pairs={{0,2},{1,3},{2,0},{3,1},{4,6},{5,7},{6,4},{7,5},{8,10},{9,11},{10,... | collective-permute-start | bytes 417800 | tf_op jit(solution)/shard_map/ppermute | solution.py:228
  20.2 0.5 %collective-permute-start.15 = (bf16[32,2176]{1,0:T(8,128)(2,1)S(1)}, bf16[32,2176]{1,0:T(8,128)(2,1)S(1)}, u32[]{:S(2)}, u32[]{:S(2)}) collective-permute-start(bf16[32,2176]{1,0:T(8,128)(2,1)S(1)} %collective-permute-done.6.refs_1_), channel_id=1, source_target_pairs={{0,2},{1,3},{2,0},{3,1},{4,6},{5,7},{6,4},{7,5},{8,10},{9,11},{10,... | collective-permute-start | bytes 417800 | tf_op jit(solution)/shard_map/ppermute | solution.py:228
  20.8 0.0 collective-permute-start.11
  20.8 0.5 collective-permute-start.12
  21.3 0.1 collective-permute-start.13
  21.3 2.1 %ffn_128.2 = (f32[64,2048]{1,0:T(8,128)S(1)}, bf16[64,2048]{1,0:T(8,128)(2,1)S(1)}) custom-call(f32[8,128]{1,0:T(8,128)S(1)} %get-tuple-element.54.mine_ref, bf16[32,2176]{1,0:T(8,128)(2,1)S(1)} %collective-permute-done.5.refs_0_, bf16[32,2176]{1,0:T(8,128)(2,1)S(1)} %collective-permute-done.6.refs_1_, bf16[32,2176]{1,0:T(8,128)(2,1)S(1)} %collective-permute-done.7.refs_2_, ...), custom_call_target="tpu_custom_call" | custom-call | flops 1610612736 | bytes 12582912 | tf_op jit(solution)/shard_map/ffn_128/pallas_call | solution.py:169
  23.5 0.5 collective-permute-start.9
  24.0 0.0 collective-permute-done.12.refs_4_
  24.0 0.0 collective-permute-done.13.refs_5_
  24.0 2.9 %ffn_192.1 = (f32[96,2048]{1,0:T(8,128)S(1)}, bf16[96,2048]{1,0:T(8,128)(2,1)S(1)}) custom-call(f32[8,128]{1,0:T(8,128)S(1)} %get-tuple-element.54.mine_ref, bf16[32,2176]{1,0:T(8,128)(2,1)S(1)} %collective-permute-done.2.refs_0_, bf16[32,2176]{1,0:T(8,128)(2,1)S(1)} %collective-permute-done.3.refs_1_, bf16[32,2176]{1,0:T(8,128)(2,1)S(1)} %collective-permute-done.4.refs_2_, ...), custom_call_target="tpu_custom_call" | custom-call | flops 2415919104 | bytes 12582912 | tf_op jit(solution)/shard_map/ffn_192/pallas_call | solution.py:169
  26.9 0.4 collective-permute-done.15.refs_1_
  27.3 0.0 collective-permute-done.14.refs_0_
  27.3 0.0 collective-permute-start.16
  27.3 0.5 collective-permute-start.17
  27.8 0.0 collective-permute-start.20
  27.8 0.1 join_64.2
  27.9 0.8 %collective-permute-done.16.refs_2_ = bf16[32,2176]{1,0:T(8,128)(2,1)S(1)} collective-permute-done((bf16[32,2176]{1,0:T(8,128)(2,1)S(1)}, bf16[32,2176]{1,0:T(8,128)(2,1)S(1)}, u32[]{:S(2)}, u32[]{:S(2)}) %collective-permute-start.16) | collective-permute-done | bytes 139296 | tf_op jit(solution)/shard_map/ppermute | solution.py:239
  28.7 0.2 collective-permute-done.17.refs_3_
  28.9 2.1 %ffn_128.3 = (f32[64,2048]{1,0:T(8,128)S(1)}, bf16[64,2048]{1,0:T(8,128)(2,1)S(1)}) custom-call(f32[8,128]{1,0:T(8,128)S(1)} %get-tuple-element.54.mine_ref, bf16[32,2176]{1,0:T(8,128)(2,1)S(1)} %collective-permute-done.14.refs_0_, bf16[32,2176]{1,0:T(8,128)(2,1)S(1)} %collective-permute-done.15.refs_1_, ...), custom_call_target="tpu_custom_call" | custom-call | flops 1610612736 | bytes 12582912 | tf_op jit(solution)/shard_map/ffn_128/pallas_call | solution.py:169
  31.0 0.4 collective-permute-start.18
  31.4 0.2 collective-permute-start.1
  31.6 2.4 %collective-permute-start.10 = (bf16[32,2048]{1,0:T(8,128)(2,1)S(1)}, bf16[32,2048]{1,0:T(8,128)(2,1)S(1)}, u32[]{:S(2)}, u32[]{:S(2)}) collective-permute-start(bf16[32,2048]{1,0:T(8,128)(2,1)S(1)} %get-tuple-element.47), channel_id=1, source_target_pairs={{0,8},{4,12},{8,0},{12,4},{1,9},{5,13},{9,1},{13,5},{2,10},{6,14},... | collective-permute-start | bytes 393224 | tf_op jit(solution)/shard_map/ppermute | solution.py:234
  34.0 0.1 join_96.1
  34.1 1.6 %collective-permute-start.24 = (bf16[32,2048]{1,0:T(8,128)(2,1)S(1)}, bf16[32,2048]{1,0:T(8,128)(2,1)S(1)}, u32[]{:S(2)}, u32[]{:S(2)}) collective-permute-start(bf16[32,2048]{1,0:T(8,128)(2,1)S(1)} %get-tuple-element.64), channel_id=1, source_target_pairs={{0,2},{1,3},{2,0},{3,1},{4,6},{5,7},{6,4},{7,5},{8,10},{9,11},{10,... | collective-permute-start | bytes 393224 | tf_op jit(solution)/shard_map/ppermute | solution.py:228
  35.7 0.6 %collective-permute-start.22 = (bf16[32,2048]{1,0:T(8,128)(2,1)S(1)}, bf16[32,2048]{1,0:T(8,128)(2,1)S(1)}, u32[]{:S(2)}, u32[]{:S(2)}) collective-permute-start(bf16[32,2048]{1,0:T(8,128)(2,1)S(1)} %get-tuple-element.62), channel_id=1, source_target_pairs={{0,2},{1,3},{2,0},{3,1},{4,6},{5,7},{6,4},{7,5},{8,10},{9,11},{10,... | collective-permute-start | bytes 393224 | tf_op jit(solution)/shard_map/ppermute | solution.py:228
  36.3 1.5 %collective-permute-start.21 = (bf16[32,2048]{1,0:T(8,128)(2,1)S(1)}, bf16[32,2048]{1,0:T(8,128)(2,1)S(1)}, u32[]{:S(2)}, u32[]{:S(2)}) collective-permute-start(bf16[32,2048]{1,0:T(8,128)(2,1)S(1)} %get-tuple-element.61), channel_id=1, source_target_pairs={{0,2},{1,3},{2,0},{3,1},{4,6},{5,7},{6,4},{7,5},{8,10},{9,11},{10,... | collective-permute-start | bytes 393224 | tf_op jit(solution)/shard_map/ppermute | solution.py:228
  37.8 0.4 collective-permute-start.19
  38.3 2.2 %collective-permute-done.24.refs_1_ = bf16[32,2048]{1,0:T(8,128)(2,1)S(1)} collective-permute-done((bf16[32,2048]{1,0:T(8,128)(2,1)S(1)}, bf16[32,2048]{1,0:T(8,128)(2,1)S(1)}, u32[]{:S(2)}, u32[]{:S(2)}) %collective-permute-start.24) | collective-permute-done | bytes 131104 | tf_op jit(solution)/shard_map/ppermute | solution.py:228
  40.5 0.1 collective-permute-start.25
  40.6 5.5 %collective-permute-done.22.refs_1_ = bf16[32,2048]{1,0:T(8,128)(2,1)S(1)} collective-permute-done((bf16[32,2048]{1,0:T(8,128)(2,1)S(1)}, bf16[32,2048]{1,0:T(8,128)(2,1)S(1)}, u32[]{:S(2)}, u32[]{:S(2)}) %collective-permute-start.22) | collective-permute-done | bytes 131104 | tf_op jit(solution)/shard_map/ppermute | solution.py:228
  46.2 0.1 collective-permute-start.23
  46.2 1.7 %collective-permute-done.21.refs_3_ = bf16[32,2048]{1,0:T(8,128)(2,1)S(1)} collective-permute-done((bf16[32,2048]{1,0:T(8,128)(2,1)S(1)}, bf16[32,2048]{1,0:T(8,128)(2,1)S(1)}, u32[]{:S(2)}, u32[]{:S(2)}) %collective-permute-start.21) | collective-permute-done | bytes 131104 | tf_op jit(solution)/shard_map/ppermute | solution.py:228
  48.0 0.1 total.4.refs_0_
  48.1 3.1 %collective-permute-done.23.refs_1_ = bf16[32,2048]{1,0:T(8,128)(2,1)S(1)} collective-permute-done((bf16[32,2048]{1,0:T(8,128)(2,1)S(1)}, bf16[32,2048]{1,0:T(8,128)(2,1)S(1)}, u32[]{:S(2)}, u32[]{:S(2)}) %collective-permute-start.23) | collective-permute-done | bytes 131104 | tf_op jit(solution)/shard_map/ppermute | solution.py:234
  51.2 0.7 %total.7 = bf16[32,2048]{1,0:T(8,128)(2,1)} custom-call(f32[32,2048]{1,0:T(8,128)S(1)} %total.4.refs_0_, bf16[32,2048]{1,0:T(8,128)(2,1)S(1)} %collective-permute-done.23.refs_1_, bf16[32,2048]{1,0:T(8,128)(2,1)S(1)} %collective-permute-done.25.refs_2_), custom_call_target="tpu_custom_call" | custom-call | tf_op jit(solution)/shard_map/total/pallas_call | solution.py:210
  (17 shorter events, 0.2 us)
Async XLA Ops:
  1.0 5.9 %collective-permute-start = (bf16[32,2176]{1,0:T(8,128)(2,1)S(1)}, bf16[32,2176]{1,0:T(8,128)(2,1)S(1)}, u32[]{:S(2)}, u32[]{:S(2)}) collective-permute-start(bf16[32,2176]{1,0:T(8,128)(2,1)S(1)} %get-tuple-element.36.refs_0_), channel_id=1, source_target_pairs={{0,1},{1,0},{2,3},{3,2},{4,5},{5,4},{6,7},{7,6},{8,9},{9,8},{10,11... | collective-permute-start | bytes 417800 | tf_op jit(solution)/shard_map/ppermute | solution.py:239
  1.1 12.5 %collective-permute-start.6 = (bf16[32,2176]{1,0:T(8,128)(2,1)S(1)}, bf16[32,2176]{1,0:T(8,128)(2,1)S(1)}, u32[]{:S(2)}, u32[]{:S(2)}) collective-permute-start(bf16[32,2176]{1,0:T(8,128)(2,1)S(1)} %get-tuple-element.36.refs_0_), channel_id=1, source_target_pairs={{0,12},{4,8},{8,4},{12,0},{1,13},{5,9},{9,5},{13,1},{2,14},{6,10},... | collective-permute-start | bytes 417800 | tf_op jit(solution)/shard_map/ppermute | solution.py:234
  2.7 12.5 %collective-permute-start.5 = (bf16[32,2176]{1,0:T(8,128)(2,1)S(1)}, bf16[32,2176]{1,0:T(8,128)(2,1)S(1)}, u32[]{:S(2)}, u32[]{:S(2)}) collective-permute-start(bf16[32,2176]{1,0:T(8,128)(2,1)S(1)} %get-tuple-element.36.refs_0_), channel_id=1, source_target_pairs={{0,8},{4,12},{8,0},{12,4},{1,9},{5,13},{9,1},{13,5},{2,10},{6,14},... | collective-permute-start | bytes 417800 | tf_op jit(solution)/shard_map/ppermute | solution.py:234
  3.8 12.8 %collective-permute-start.4 = (bf16[32,2176]{1,0:T(8,128)(2,1)S(1)}, bf16[32,2176]{1,0:T(8,128)(2,1)S(1)}, u32[]{:S(2)}, u32[]{:S(2)}) collective-permute-start(bf16[32,2176]{1,0:T(8,128)(2,1)S(1)} %get-tuple-element.36.refs_0_), channel_id=1, source_target_pairs={{0,6},{1,7},{2,4},{3,5},{4,2},{5,3},{6,0},{7,1},{8,14},{9,15},{10,... | collective-permute-start | bytes 417800 | tf_op jit(solution)/shard_map/ppermute | solution.py:236
  6.1 12.1 %collective-permute-start.3 = (bf16[32,2176]{1,0:T(8,128)(2,1)S(1)}, bf16[32,2176]{1,0:T(8,128)(2,1)S(1)}, u32[]{:S(2)}, u32[]{:S(2)}) collective-permute-start(bf16[32,2176]{1,0:T(8,128)(2,1)S(1)} %get-tuple-element.36.refs_0_), channel_id=1, source_target_pairs={{0,4},{4,0},{8,12},{12,8},{1,5},{5,1},{9,13},{13,9},{2,6},{6,2},{1... | collective-permute-start | bytes 417800 | tf_op jit(solution)/shard_map/ppermute | solution.py:234
  6.9 11.3 %collective-permute-start.2 = (bf16[32,2176]{1,0:T(8,128)(2,1)S(1)}, bf16[32,2176]{1,0:T(8,128)(2,1)S(1)}, u32[]{:S(2)}, u32[]{:S(2)}) collective-permute-start(bf16[32,2176]{1,0:T(8,128)(2,1)S(1)} %get-tuple-element.36.refs_0_), channel_id=1, source_target_pairs={{0,2},{1,3},{2,0},{3,1},{4,6},{5,7},{6,4},{7,5},{8,10},{9,11},{10,... | collective-permute-start | bytes 417800 | tf_op jit(solution)/shard_map/ppermute | solution.py:228
  18.2 2.5 %collective-permute-start.7 = (bf16[32,2176]{1,0:T(8,128)(2,1)S(1)}, bf16[32,2176]{1,0:T(8,128)(2,1)S(1)}, u32[]{:S(2)}, u32[]{:S(2)}) collective-permute-start(bf16[32,2176]{1,0:T(8,128)(2,1)S(1)} %collective-permute-done.5.refs_0_), channel_id=1, source_target_pairs={{0,1},{1,0},{2,3},{3,2},{4,5},{5,4},{6,7},{7,6},{8,9},{9,8},{10,11... | collective-permute-start | bytes 417800 | tf_op jit(solution)/shard_map/ppermute | solution.py:239
  18.2 3.1 %collective-permute-start.8 = (bf16[32,2176]{1,0:T(8,128)(2,1)S(1)}, bf16[32,2176]{1,0:T(8,128)(2,1)S(1)}, u32[]{:S(2)}, u32[]{:S(2)}) collective-permute-start(bf16[32,2176]{1,0:T(8,128)(2,1)S(1)} %collective-permute-done.6.refs_1_), channel_id=1, source_target_pairs={{0,1},{1,0},{2,3},{3,2},{4,5},{5,4},{6,7},{7,6},{8,9},{9,8},{10,11... | collective-permute-start | bytes 417800 | tf_op jit(solution)/shard_map/ppermute | solution.py:239
  18.7 8.6 %collective-permute-start.14 = (bf16[32,2176]{1,0:T(8,128)(2,1)S(1)}, bf16[32,2176]{1,0:T(8,128)(2,1)S(1)}, u32[]{:S(2)}, u32[]{:S(2)}) collective-permute-start(bf16[32,2176]{1,0:T(8,128)(2,1)S(1)} %collective-permute-done.5.refs_0_), channel_id=1, source_target_pairs={{0,2},{1,3},{2,0},{3,1},{4,6},{5,7},{6,4},{7,5},{8,10},{9,11},{10,... | collective-permute-start | bytes 417800 | tf_op jit(solution)/shard_map/ppermute | solution.py:228
  20.2 7.1 %collective-permute-start.15 = (bf16[32,2176]{1,0:T(8,128)(2,1)S(1)}, bf16[32,2176]{1,0:T(8,128)(2,1)S(1)}, u32[]{:S(2)}, u32[]{:S(2)}) collective-permute-start(bf16[32,2176]{1,0:T(8,128)(2,1)S(1)} %collective-permute-done.6.refs_1_), channel_id=1, source_target_pairs={{0,2},{1,3},{2,0},{3,1},{4,6},{5,7},{6,4},{7,5},{8,10},{9,11},{10,... | collective-permute-start | bytes 417800 | tf_op jit(solution)/shard_map/ppermute | solution.py:228
  20.8 2.7 %collective-permute-start.11 = (bf16[32,2176]{1,0:T(8,128)(2,1)S(1)}, bf16[32,2176]{1,0:T(8,128)(2,1)S(1)}, u32[]{:S(2)}, u32[]{:S(2)}) collective-permute-start(bf16[32,2176]{1,0:T(8,128)(2,1)S(1)} %collective-permute-done.2.refs_0_), channel_id=1, source_target_pairs={{0,1},{1,0},{2,3},{3,2},{4,5},{5,4},{6,7},{7,6},{8,9},{9,8},{10,11... | collective-permute-start | bytes 417800 | tf_op jit(solution)/shard_map/ppermute | solution.py:239
  20.8 3.2 %collective-permute-start.12 = (bf16[32,2176]{1,0:T(8,128)(2,1)S(1)}, bf16[32,2176]{1,0:T(8,128)(2,1)S(1)}, u32[]{:S(2)}, u32[]{:S(2)}) collective-permute-start(bf16[32,2176]{1,0:T(8,128)(2,1)S(1)} %collective-permute-done.3.refs_1_), channel_id=1, source_target_pairs={{0,1},{1,0},{2,3},{3,2},{4,5},{5,4},{6,7},{7,6},{8,9},{9,8},{10,11... | collective-permute-start | bytes 417800 | tf_op jit(solution)/shard_map/ppermute | solution.py:239
  21.3 2.7 %collective-permute-start.13 = (bf16[32,2176]{1,0:T(8,128)(2,1)S(1)}, bf16[32,2176]{1,0:T(8,128)(2,1)S(1)}, u32[]{:S(2)}, u32[]{:S(2)}) collective-permute-start(bf16[32,2176]{1,0:T(8,128)(2,1)S(1)} %collective-permute-done.4.refs_2_), channel_id=1, source_target_pairs={{0,1},{1,0},{2,3},{3,2},{4,5},{5,4},{6,7},{7,6},{8,9},{9,8},{10,11... | collective-permute-start | bytes 417800 | tf_op jit(solution)/shard_map/ppermute | solution.py:239
  23.5 4.3 %collective-permute-start.9 = (bf16[64,2048]{1,0:T(8,128)(2,1)S(1)}, bf16[64,2048]{1,0:T(8,128)(2,1)S(1)}, u32[]{:S(2)}, u32[]{:S(2)}) collective-permute-start(bf16[64,2048]{1,0:T(8,128)(2,1)S(1)} %get-tuple-element.46), channel_id=1, source_target_pairs={{0,1},{1,0},{2,3},{3,2},{4,5},{5,4},{6,7},{7,6},{8,9},{9,8},{10,11... | collective-permute-start | bytes 786440 | tf_op jit(solution)/shard_map/ppermute | solution.py:239
  27.3 1.4 %collective-permute-start.16 = (bf16[32,2176]{1,0:T(8,128)(2,1)S(1)}, bf16[32,2176]{1,0:T(8,128)(2,1)S(1)}, u32[]{:S(2)}, u32[]{:S(2)}) collective-permute-start(bf16[32,2176]{1,0:T(8,128)(2,1)S(1)} %collective-permute-done.14.refs_0_), channel_id=1, source_target_pairs={{0,1},{1,0},{2,3},{3,2},{4,5},{5,4},{6,7},{7,6},{8,9},{9,8},{10,11... | collective-permute-start | bytes 417800 | tf_op jit(solution)/shard_map/ppermute | solution.py:239
  27.3 1.6 %collective-permute-start.17 = (bf16[32,2176]{1,0:T(8,128)(2,1)S(1)}, bf16[32,2176]{1,0:T(8,128)(2,1)S(1)}, u32[]{:S(2)}, u32[]{:S(2)}) collective-permute-start(bf16[32,2176]{1,0:T(8,128)(2,1)S(1)} %collective-permute-done.15.refs_1_), channel_id=1, source_target_pairs={{0,1},{1,0},{2,3},{3,2},{4,5},{5,4},{6,7},{7,6},{8,9},{9,8},{10,11... | collective-permute-start | bytes 417800 | tf_op jit(solution)/shard_map/ppermute | solution.py:239
  27.8 6.2 %collective-permute-start.20 = (bf16[96,2048]{1,0:T(8,128)(2,1)S(1)}, bf16[96,2048]{1,0:T(8,128)(2,1)S(1)}, u32[]{:S(2)}, u32[]{:S(2)}) collective-permute-start(bf16[96,2048]{1,0:T(8,128)(2,1)S(1)} %get-tuple-element.52), channel_id=1, source_target_pairs={{0,1},{1,0},{2,3},{3,2},{4,5},{5,4},{6,7},{7,6},{8,9},{9,8},{10,11... | collective-permute-start | bytes 1179656 | tf_op jit(solution)/shard_map/ppermute | solution.py:239
  31.0 4.7 %collective-permute-start.18 = (bf16[64,2048]{1,0:T(8,128)(2,1)S(1)}, bf16[64,2048]{1,0:T(8,128)(2,1)S(1)}, u32[]{:S(2)}, u32[]{:S(2)}) collective-permute-start(bf16[64,2048]{1,0:T(8,128)(2,1)S(1)} %get-tuple-element.58), channel_id=1, source_target_pairs={{0,1},{1,0},{2,3},{3,2},{4,5},{5,4},{6,7},{7,6},{8,9},{9,8},{10,11... | collective-permute-start | bytes 786440 | tf_op jit(solution)/shard_map/ppermute | solution.py:239
  31.4 6.5 %collective-permute-start.1 = (bf16[32,2048]{1,0:T(8,128)(2,1)S(1)}, bf16[32,2048]{1,0:T(8,128)(2,1)S(1)}, u32[]{:S(2)}, u32[]{:S(2)}) collective-permute-start(bf16[32,2048]{1,0:T(8,128)(2,1)S(1)} %get-tuple-element.38), channel_id=1, source_target_pairs={{0,1},{1,0},{2,3},{3,2},{4,5},{5,4},{6,7},{7,6},{8,9},{9,8},{10,11... | collective-permute-start | bytes 393224 | tf_op jit(solution)/shard_map/ppermute | solution.py:239
  31.6 14.7 %collective-permute-start.10 = (bf16[32,2048]{1,0:T(8,128)(2,1)S(1)}, bf16[32,2048]{1,0:T(8,128)(2,1)S(1)}, u32[]{:S(2)}, u32[]{:S(2)}) collective-permute-start(bf16[32,2048]{1,0:T(8,128)(2,1)S(1)} %get-tuple-element.47), channel_id=1, source_target_pairs={{0,8},{4,12},{8,0},{12,4},{1,9},{5,13},{9,1},{13,5},{2,10},{6,14},... | collective-permute-start | bytes 393224 | tf_op jit(solution)/shard_map/ppermute | solution.py:234
  34.1 6.4 %collective-permute-start.24 = (bf16[32,2048]{1,0:T(8,128)(2,1)S(1)}, bf16[32,2048]{1,0:T(8,128)(2,1)S(1)}, u32[]{:S(2)}, u32[]{:S(2)}) collective-permute-start(bf16[32,2048]{1,0:T(8,128)(2,1)S(1)} %get-tuple-element.64), channel_id=1, source_target_pairs={{0,2},{1,3},{2,0},{3,1},{4,6},{5,7},{6,4},{7,5},{8,10},{9,11},{10,... | collective-permute-start | bytes 393224 | tf_op jit(solution)/shard_map/ppermute | solution.py:228
  35.7 10.4 %collective-permute-start.22 = (bf16[32,2048]{1,0:T(8,128)(2,1)S(1)}, bf16[32,2048]{1,0:T(8,128)(2,1)S(1)}, u32[]{:S(2)}, u32[]{:S(2)}) collective-permute-start(bf16[32,2048]{1,0:T(8,128)(2,1)S(1)} %get-tuple-element.62), channel_id=1, source_target_pairs={{0,2},{1,3},{2,0},{3,1},{4,6},{5,7},{6,4},{7,5},{8,10},{9,11},{10,... | collective-permute-start | bytes 393224 | tf_op jit(solution)/shard_map/ppermute | solution.py:228
  36.3 11.7 %collective-permute-start.21 = (bf16[32,2048]{1,0:T(8,128)(2,1)S(1)}, bf16[32,2048]{1,0:T(8,128)(2,1)S(1)}, u32[]{:S(2)}, u32[]{:S(2)}) collective-permute-start(bf16[32,2048]{1,0:T(8,128)(2,1)S(1)} %get-tuple-element.61), channel_id=1, source_target_pairs={{0,2},{1,3},{2,0},{3,1},{4,6},{5,7},{6,4},{7,5},{8,10},{9,11},{10,... | collective-permute-start | bytes 393224 | tf_op jit(solution)/shard_map/ppermute | solution.py:228
  37.8 10.2 %collective-permute-start.19 = (bf16[32,2048]{1,0:T(8,128)(2,1)S(1)}, bf16[32,2048]{1,0:T(8,128)(2,1)S(1)}, u32[]{:S(2)}, u32[]{:S(2)}) collective-permute-start(bf16[32,2048]{1,0:T(8,128)(2,1)S(1)} %get-tuple-element.59), channel_id=1, source_target_pairs={{0,10},{1,11},{2,8},{3,9},{4,14},{5,15},{6,12},{7,13},{8,2},{9,3},... | collective-permute-start | bytes 393224 | tf_op jit(solution)/shard_map/ppermute | solution.py:236
  40.5 7.5 %collective-permute-start.25 = (bf16[32,2048]{1,0:T(8,128)(2,1)S(1)}, bf16[32,2048]{1,0:T(8,128)(2,1)S(1)}, u32[]{:S(2)}, u32[]{:S(2)}) collective-permute-start(bf16[32,2048]{1,0:T(8,128)(2,1)S(1)} %total.6), channel_id=1, source_target_pairs={{0,4},{4,0},{8,12},{12,8},{1,5},{5,1},{9,13},{13,9},{2,6},{6,2},{1... | collective-permute-start | bytes 393224 | tf_op jit(solution)/shard_map/ppermute | solution.py:234
  46.2 5.0 %collective-permute-start.23 = (bf16[32,2048]{1,0:T(8,128)(2,1)S(1)}, bf16[32,2048]{1,0:T(8,128)(2,1)S(1)}, u32[]{:S(2)}, u32[]{:S(2)}) collective-permute-start(bf16[32,2048]{1,0:T(8,128)(2,1)S(1)} %total.5), channel_id=1, source_target_pairs={{0,12},{4,8},{8,4},{12,0},{1,13},{5,9},{9,5},{13,1},{2,14},{6,10},... | collective-permute-start | bytes 393224 | tf_op jit(solution)/shard_map/ppermute | solution.py:234

commit v5 on v3

--- a/solution.py
+++ b/solution.py
@@ -111,18 +111,18 @@
     gap = rounded(top)
     ids, high, low = (meta[:, i * gap : i * gap + top] for i in range(3))
     weight = (high * 256.0 + low) * (1.0 / 65536.0)
-    total = None
+    hidden = []
     for e in range(wg_ref.shape[0]):
         scale = jnp.sum(jnp.where(ids == mine_ref[0:1, e : e + 1], weight, 0.0), axis=1, keepdims=True)
         ready(e, 0)
         gate = jnp.dot(x, wg_ref[e], preferred_element_type=jnp.float32)
         ready(e, 1)
         up = jnp.dot(x, wu_ref[e], preferred_element_type=jnp.float32)
-        hidden = (gate / (1.0 + jnp.exp(-gate)) * up).astype(jnp.bfloat16)
+        hidden.append((gate / (1.0 + jnp.exp(-gate)) * up * scale).astype(jnp.bfloat16))
+    for e in range(wd_ref.shape[0]):
         ready(e, 2)
-        part = jnp.dot(hidden, wd_ref[e], preferred_element_type=jnp.float32) * scale
-        total = part if total is None else total + part
-    return total
+    down = wd_ref[...].reshape(-1, wd_ref.shape[2])
+    return jnp.dot(jnp.concatenate(hidden, axis=1), down, preferred_element_type=jnp.float32)
 
 
 def gather_rows(ins, rows, width):

time: 52.3 us -> 52.1 us (level)
  no operation moved by 1% of the time
where the time goes in v5:
time: 52.1 us; the launch traced here: 51.7 us
  waiting for transfers between devices  19.6 us (38%)
  starting transfers between devices  17.7 us (34%)
  Pallas kernels  14.3 us (27%)
    pallas_call x4, Pallas kernels, ffn(): pl.pallas_call(functools.partial(first_ffn_kernel if first else ffn_kerne...  12.3 us
    ppermute x6, waiting for transfers between devices, along_x(): return lax.ppermute(t, 'rank', [(i, i ^ dx * cores) for i in range(n_rank)])  10.1 us
    ppermute x6, waiting for transfers between devices, to_chip(): return lax.ppermute(t, 'node', [(i, i ^ dz) for i in range(n_node)])  7.1 us
    ppermute x6, starting transfers between devices, to_chip(): return lax.ppermute(t, 'node', [(i, i ^ dz) for i in range(n_node)])  6.1 us
    ppermute x6, starting transfers between devices, along_x(): return lax.ppermute(t, 'rank', [(i, i ^ dx * cores) for i in range(n_rank)])  6.1 us
    ppermute x12, starting transfers between devices, swap(): return lax.ppermute(t, 'rank', [(i, i ^ 1) for i in range(n_rank)])  2.76 us
    ppermute x2, starting transfers between devices, to_chip(): lax.ppermute(t, ('node', 'rank'), [(i, i ^ step) for i in range(n_node *...  2.74 us
    ppermute x2, waiting for transfers between devices, to_chip(): lax.ppermute(t, ('node', 'rank'), [(i, i ^ step) for i in range(n_node *...  1.37 us
  transfers between devices with their start and end apart: 26, of which 11 were waited for; matrix products, arithmetic and copies ran while one was open for 0% of the time, Pallas kernels for 24%

profile of v5, /device:TPU:8, one launch (start us, length us, event | category | flops | bytes accessed | tf_op | source)
XLA Modules:
  0.0 51.7 jit_solution(8423627049806991360)
XLA Ops:
  0.0 1.0 %prepare.1 = (bf16[32,2176]{1,0:T(8,128)(2,1)S(1)}, f32[8,128]{1,0:T(8,128)S(1)}) custom-call(bf16[32,2048]{1,0:T(8,128)(2,1)} %tokens_in.1, s32[10,32]{1,0:T(8,128)} %bitcast.2, s32[10,32]{1,0:T(8,128)} %bitcast.3, s32[32]{0:T(128)} %plan_in.1), custom_call_target="tpu_custom_call" | custom-call | tf_op jit(solution)/shard_map/prepare/pallas_call | solution.py:90
  1.0 0.1 collective-permute-start
  1.1 1.6 %collective-permute-start.6 = (bf16[32,2176]{1,0:T(8,128)(2,1)S(1)}, bf16[32,2176]{1,0:T(8,128)(2,1)S(1)}, u32[]{:S(2)}, u32[]{:S(2)}) collective-permute-start(bf16[32,2176]{1,0:T(8,128)(2,1)S(1)} %get-tuple-element.36.refs_0_), channel_id=1, source_target_pairs={{0,12},{4,8},{8,4},{12,0},{1,13},{5,9},{9,5},{13,1},{2,14},{6,10},... | collective-permute-start | bytes 417800 | tf_op jit(solution)/shard_map/ppermute | solution.py:234
  2.7 1.1 %collective-permute-start.5 = (bf16[32,2176]{1,0:T(8,128)(2,1)S(1)}, bf16[32,2176]{1,0:T(8,128)(2,1)S(1)}, u32[]{:S(2)}, u32[]{:S(2)}) collective-permute-start(bf16[32,2176]{1,0:T(8,128)(2,1)S(1)} %get-tuple-element.36.refs_0_), channel_id=1, source_target_pairs={{0,8},{4,12},{8,0},{12,4},{1,9},{5,13},{9,1},{13,5},{2,10},{6,14},... | collective-permute-start | bytes 417800 | tf_op jit(solution)/shard_map/ppermute | solution.py:234
  3.8 2.3 %collective-permute-start.4 = (bf16[32,2176]{1,0:T(8,128)(2,1)S(1)}, bf16[32,2176]{1,0:T(8,128)(2,1)S(1)}, u32[]{:S(2)}, u32[]{:S(2)}) collective-permute-start(bf16[32,2176]{1,0:T(8,128)(2,1)S(1)} %get-tuple-element.36.refs_0_), channel_id=1, source_target_pairs={{0,6},{1,7},{2,4},{3,5},{4,2},{5,3},{6,0},{7,1},{8,14},{9,15},{10,... | collective-permute-start | bytes 417800 | tf_op jit(solution)/shard_map/ppermute | solution.py:236
  6.1 0.8 %collective-permute-start.3 = (bf16[32,2176]{1,0:T(8,128)(2,1)S(1)}, bf16[32,2176]{1,0:T(8,128)(2,1)S(1)}, u32[]{:S(2)}, u32[]{:S(2)}) collective-permute-start(bf16[32,2176]{1,0:T(8,128)(2,1)S(1)} %get-tuple-element.36.refs_0_), channel_id=1, source_target_pairs={{0,4},{4,0},{8,12},{12,8},{1,5},{5,1},{9,13},{13,9},{2,6},{6,2},{1... | collective-permute-start | bytes 417800 | tf_op jit(solution)/shard_map/ppermute | solution.py:234
  6.9 0.0 collective-permute-done.refs_1_
  6.9 0.4 collective-permute-start.2
  7.3 5.6 %ffn_first_64.1 = (f32[32,2048]{1,0:T(8,128)S(1)}, bf16[32,2048]{1,0:T(8,128)(2,1)S(1)}, bf16[2,2048,512]{2,1,0:T(8,128)(2,1)S(1)}, bf16[2,2048,512]{2,1,0:T(8,128)(2,1)S(1)}, bf16[2,512,2048]{2,1,0:T(8,128)(2,1)S(1)}) custom-call(f32[8,128]{1,0:T(8,128)S(1)} %get-tuple-element.54.mine_ref, bf16[32,2176]{1,0:T(8,128)(2,1)S(1)} %get-tuple-element.36.refs_0_, ...), custom_call_target="tpu_custom_call" | custom-call | flops 805306368 | bytes 12582912 | tf_op jit(solution)/shard_map/ffn_first_64/pallas_call | solution.py:169
  12.9 0.7 %collective-permute-done.6.refs_1_ = bf16[32,2176]{1,0:T(8,128)(2,1)S(1)} collective-permute-done((bf16[32,2176]{1,0:T(8,128)(2,1)S(1)}, bf16[32,2176]{1,0:T(8,128)(2,1)S(1)}, u32[]{:S(2)}, u32[]{:S(2)}) %collective-permute-start.6) | collective-permute-done | bytes 139296 | tf_op jit(solution)/shard_map/ppermute | solution.py:234
  13.6 1.7 %collective-permute-done.5.refs_0_ = bf16[32,2176]{1,0:T(8,128)(2,1)S(1)} collective-permute-done((bf16[32,2176]{1,0:T(8,128)(2,1)S(1)}, bf16[32,2176]{1,0:T(8,128)(2,1)S(1)}, u32[]{:S(2)}, u32[]{:S(2)}) %collective-permute-start.5) | collective-permute-done | bytes 139296 | tf_op jit(solution)/shard_map/ppermute | solution.py:234
  15.2 1.4 %collective-permute-done.4.refs_2_ = bf16[32,2176]{1,0:T(8,128)(2,1)S(1)} collective-permute-done((bf16[32,2176]{1,0:T(8,128)(2,1)S(1)}, bf16[32,2176]{1,0:T(8,128)(2,1)S(1)}, u32[]{:S(2)}, u32[]{:S(2)}) %collective-permute-start.4) | collective-permute-done | bytes 139296 | tf_op jit(solution)/shard_map/ppermute | solution.py:236
  16.6 1.6 %collective-permute-done.3.refs_1_ = bf16[32,2176]{1,0:T(8,128)(2,1)S(1)} collective-permute-done((bf16[32,2176]{1,0:T(8,128)(2,1)S(1)}, bf16[32,2176]{1,0:T(8,128)(2,1)S(1)}, u32[]{:S(2)}, u32[]{:S(2)}) %collective-permute-start.3) | collective-permute-done | bytes 139296 | tf_op jit(solution)/shard_map/ppermute | solution.py:234
  18.2 0.0 collective-permute-done.2.refs_0_
  18.2 0.0 collective-permute-start.7
  18.2 0.5 collective-permute-start.8
  18.7 1.5 %collective-permute-start.14 = (bf16[32,2176]{1,0:T(8,128)(2,1)S(1)}, bf16[32,2176]{1,0:T(8,128)(2,1)S(1)}, u32[]{:S(2)}, u32[]{:S(2)}) collective-permute-start(bf16[32,2176]{1,0:T(8,128)(2,1)S(1)} %collective-permute-done.5.refs_0_), channel_id=1, source_target_pairs={{0,2},{1,3},{2,0},{3,1},{4,6},{5,7},{6,4},{7,5},{8,10},{9,11},{10,... | collective-permute-start | bytes 417800 | tf_op jit(solution)/shard_map/ppermute | solution.py:228
  20.2 0.5 %collective-permute-start.15 = (bf16[32,2176]{1,0:T(8,128)(2,1)S(1)}, bf16[32,2176]{1,0:T(8,128)(2,1)S(1)}, u32[]{:S(2)}, u32[]{:S(2)}) collective-permute-start(bf16[32,2176]{1,0:T(8,128)(2,1)S(1)} %collective-permute-done.6.refs_1_), channel_id=1, source_target_pairs={{0,2},{1,3},{2,0},{3,1},{4,6},{5,7},{6,4},{7,5},{8,10},{9,11},{10,... | collective-permute-start | bytes 417800 | tf_op jit(solution)/shard_map/ppermute | solution.py:228
  20.8 0.0 collective-permute-start.11
  20.8 0.0 collective-permute-done.7.refs_2_
  20.8 0.5 collective-permute-start.12
  21.3 0.1 collective-permute-start.13
  21.3 2.0 %ffn_128.2 = (f32[64,2048]{1,0:T(8,128)S(1)}, bf16[64,2048]{1,0:T(8,128)(2,1)S(1)}) custom-call(f32[8,128]{1,0:T(8,128)S(1)} %get-tuple-element.54.mine_ref, bf16[32,2176]{1,0:T(8,128)(2,1)S(1)} %collective-permute-done.5.refs_0_, bf16[32,2176]{1,0:T(8,128)(2,1)S(1)} %collective-permute-done.6.refs_1_, bf16[32,2176]{1,0:T(8,128)(2,1)S(1)} %collective-permute-done.7.refs_2_, ...), custom_call_target="tpu_custom_call" | custom-call | flops 1610612736 | bytes 12582912 | tf_op jit(solution)/shard_map/ffn_128/pallas_call | solution.py:169
  23.3 0.5 collective-permute-start.9
  23.9 2.8 %ffn_192.1 = (f32[96,2048]{1,0:T(8,128)S(1)}, bf16[96,2048]{1,0:T(8,128)(2,1)S(1)}) custom-call(f32[8,128]{1,0:T(8,128)S(1)} %get-tuple-element.54.mine_ref, bf16[32,2176]{1,0:T(8,128)(2,1)S(1)} %collective-permute-done.2.refs_0_, bf16[32,2176]{1,0:T(8,128)(2,1)S(1)} %collective-permute-done.3.refs_1_, bf16[32,2176]{1,0:T(8,128)(2,1)S(1)} %collective-permute-done.4.refs_2_, ...), custom_call_target="tpu_custom_call" | custom-call | flops 2415919104 | bytes 12582912 | tf_op jit(solution)/shard_map/ffn_192/pallas_call | solution.py:169
  26.6 0.6 %collective-permute-done.15.refs_1_ = bf16[32,2176]{1,0:T(8,128)(2,1)S(1)} collective-permute-done((bf16[32,2176]{1,0:T(8,128)(2,1)S(1)}, bf16[32,2176]{1,0:T(8,128)(2,1)S(1)}, u32[]{:S(2)}, u32[]{:S(2)}) %collective-permute-start.15) | collective-permute-done | bytes 139296 | tf_op jit(solution)/shard_map/ppermute | solution.py:228
  27.3 0.5 collective-permute-start.17
  27.8 0.0 collective-permute-start.20
  27.8 0.1 join_64.2
  27.9 0.8 %collective-permute-done.16.refs_2_ = bf16[32,2176]{1,0:T(8,128)(2,1)S(1)} collective-permute-done((bf16[32,2176]{1,0:T(8,128)(2,1)S(1)}, bf16[32,2176]{1,0:T(8,128)(2,1)S(1)}, u32[]{:S(2)}, u32[]{:S(2)}) %collective-permute-start.16) | collective-permute-done | bytes 139296 | tf_op jit(solution)/shard_map/ppermute | solution.py:239
  28.7 0.2 collective-permute-done.17.refs_3_
  28.9 2.0 %ffn_128.3 = (f32[64,2048]{1,0:T(8,128)S(1)}, bf16[64,2048]{1,0:T(8,128)(2,1)S(1)}) custom-call(f32[8,128]{1,0:T(8,128)S(1)} %get-tuple-element.54.mine_ref, bf16[32,2176]{1,0:T(8,128)(2,1)S(1)} %collective-permute-done.14.refs_0_, bf16[32,2176]{1,0:T(8,128)(2,1)S(1)} %collective-permute-done.15.refs_1_, ...), custom_call_target="tpu_custom_call" | custom-call | flops 1610612736 | bytes 12582912 | tf_op jit(solution)/shard_map/ffn_128/pallas_call | solution.py:169
  30.8 0.4 collective-permute-start.18
  31.2 0.2 collective-permute-start.1
  31.4 2.4 %collective-permute-start.10 = (bf16[32,2048]{1,0:T(8,128)(2,1)S(1)}, bf16[32,2048]{1,0:T(8,128)(2,1)S(1)}, u32[]{:S(2)}, u32[]{:S(2)}) collective-permute-start(bf16[32,2048]{1,0:T(8,128)(2,1)S(1)} %get-tuple-element.47), channel_id=1, source_target_pairs={{0,8},{4,12},{8,0},{12,4},{1,9},{5,13},{9,1},{13,5},{2,10},{6,14},... | collective-permute-start | bytes 393224 | tf_op jit(solution)/shard_map/ppermute | solution.py:234
  33.9 0.1 join_96.1
  33.9 1.6 %collective-permute-start.22 = (bf16[32,2048]{1,0:T(8,128)(2,1)S(1)}, bf16[32,2048]{1,0:T(8,128)(2,1)S(1)}, u32[]{:S(2)}, u32[]{:S(2)}) collective-permute-start(bf16[32,2048]{1,0:T(8,128)(2,1)S(1)} %get-tuple-element.63), channel_id=1, source_target_pairs={{0,2},{1,3},{2,0},{3,1},{4,6},{5,7},{6,4},{7,5},{8,10},{9,11},{10,... | collective-permute-start | bytes 393224 | tf_op jit(solution)/shard_map/ppermute | solution.py:228
  35.6 0.6 %collective-permute-start.24 = (bf16[32,2048]{1,0:T(8,128)(2,1)S(1)}, bf16[32,2048]{1,0:T(8,128)(2,1)S(1)}, u32[]{:S(2)}, u32[]{:S(2)}) collective-permute-start(bf16[32,2048]{1,0:T(8,128)(2,1)S(1)} %get-tuple-element.64), channel_id=1, source_target_pairs={{0,2},{1,3},{2,0},{3,1},{4,6},{5,7},{6,4},{7,5},{8,10},{9,11},{10,... | collective-permute-start | bytes 393224 | tf_op jit(solution)/shard_map/ppermute | solution.py:228
  36.1 1.5 %collective-permute-start.21 = (bf16[32,2048]{1,0:T(8,128)(2,1)S(1)}, bf16[32,2048]{1,0:T(8,128)(2,1)S(1)}, u32[]{:S(2)}, u32[]{:S(2)}) collective-permute-start(bf16[32,2048]{1,0:T(8,128)(2,1)S(1)} %get-tuple-element.61), channel_id=1, source_target_pairs={{0,2},{1,3},{2,0},{3,1},{4,6},{5,7},{6,4},{7,5},{8,10},{9,11},{10,... | collective-permute-start | bytes 393224 | tf_op jit(solution)/shard_map/ppermute | solution.py:228
  37.7 0.4 collective-permute-start.19
  38.1 2.2 %collective-permute-done.22.refs_1_ = bf16[32,2048]{1,0:T(8,128)(2,1)S(1)} collective-permute-done((bf16[32,2048]{1,0:T(8,128)(2,1)S(1)}, bf16[32,2048]{1,0:T(8,128)(2,1)S(1)}, u32[]{:S(2)}, u32[]{:S(2)}) %collective-permute-start.22) | collective-permute-done | bytes 131104 | tf_op jit(solution)/shard_map/ppermute | solution.py:228
  40.4 0.1 collective-permute-start.23
  40.5 5.5 %collective-permute-done.24.refs_1_ = bf16[32,2048]{1,0:T(8,128)(2,1)S(1)} collective-permute-done((bf16[32,2048]{1,0:T(8,128)(2,1)S(1)}, bf16[32,2048]{1,0:T(8,128)(2,1)S(1)}, u32[]{:S(2)}, u32[]{:S(2)}) %collective-permute-start.24) | collective-permute-done | bytes 131104 | tf_op jit(solution)/shard_map/ppermute | solution.py:228
  46.0 0.1 collective-permute-start.25
  46.1 1.7 %collective-permute-done.21.refs_3_ = bf16[32,2048]{1,0:T(8,128)(2,1)S(1)} collective-permute-done((bf16[32,2048]{1,0:T(8,128)(2,1)S(1)}, bf16[32,2048]{1,0:T(8,128)(2,1)S(1)}, u32[]{:S(2)}, u32[]{:S(2)}) %collective-permute-start.21) | collective-permute-done | bytes 131104 | tf_op jit(solution)/shard_map/ppermute | solution.py:228
  47.8 0.1 total.4.refs_0_
  47.9 3.1 %collective-permute-done.25.refs_2_ = bf16[32,2048]{1,0:T(8,128)(2,1)S(1)} collective-permute-done((bf16[32,2048]{1,0:T(8,128)(2,1)S(1)}, bf16[32,2048]{1,0:T(8,128)(2,1)S(1)}, u32[]{:S(2)}, u32[]{:S(2)}) %collective-permute-start.25) | collective-permute-done | bytes 131104 | tf_op jit(solution)/shard_map/ppermute | solution.py:234
  51.0 0.7 %total.7 = bf16[32,2048]{1,0:T(8,128)(2,1)} custom-call(f32[32,2048]{1,0:T(8,128)S(1)} %total.4.refs_0_, bf16[32,2048]{1,0:T(8,128)(2,1)S(1)} %collective-permute-done.23.refs_1_, bf16[32,2048]{1,0:T(8,128)(2,1)S(1)} %collective-permute-done.25.refs_2_), custom_call_target="tpu_custom_call" | custom-call | tf_op jit(solution)/shard_map/total/pallas_call | solution.py:210
  (17 shorter events, 0.2 us)
Async XLA Ops:
  1.0 5.9 %collective-permute-start = (bf16[32,2176]{1,0:T(8,128)(2,1)S(1)}, bf16[32,2176]{1,0:T(8,128)(2,1)S(1)}, u32[]{:S(2)}, u32[]{:S(2)}) collective-permute-start(bf16[32,2176]{1,0:T(8,128)(2,1)S(1)} %get-tuple-element.36.refs_0_), channel_id=1, source_target_pairs={{0,1},{1,0},{2,3},{3,2},{4,5},{5,4},{6,7},{7,6},{8,9},{9,8},{10,11... | collective-permute-start | bytes 417800 | tf_op jit(solution)/shard_map/ppermute | solution.py:239
  1.1 12.5 %collective-permute-start.6 = (bf16[32,2176]{1,0:T(8,128)(2,1)S(1)}, bf16[32,2176]{1,0:T(8,128)(2,1)S(1)}, u32[]{:S(2)}, u32[]{:S(2)}) collective-permute-start(bf16[32,2176]{1,0:T(8,128)(2,1)S(1)} %get-tuple-element.36.refs_0_), channel_id=1, source_target_pairs={{0,12},{4,8},{8,4},{12,0},{1,13},{5,9},{9,5},{13,1},{2,14},{6,10},... | collective-permute-start | bytes 417800 | tf_op jit(solution)/shard_map/ppermute | solution.py:234
  2.7 12.5 %collective-permute-start.5 = (bf16[32,2176]{1,0:T(8,128)(2,1)S(1)}, bf16[32,2176]{1,0:T(8,128)(2,1)S(1)}, u32[]{:S(2)}, u32[]{:S(2)}) collective-permute-start(bf16[32,2176]{1,0:T(8,128)(2,1)S(1)} %get-tuple-element.36.refs_0_), channel_id=1, source_target_pairs={{0,8},{4,12},{8,0},{12,4},{1,9},{5,13},{9,1},{13,5},{2,10},{6,14},... | collective-permute-start | bytes 417800 | tf_op jit(solution)/shard_map/ppermute | solution.py:234
  3.8 12.8 %collective-permute-start.4 = (bf16[32,2176]{1,0:T(8,128)(2,1)S(1)}, bf16[32,2176]{1,0:T(8,128)(2,1)S(1)}, u32[]{:S(2)}, u32[]{:S(2)}) collective-permute-start(bf16[32,2176]{1,0:T(8,128)(2,1)S(1)} %get-tuple-element.36.refs_0_), channel_id=1, source_target_pairs={{0,6},{1,7},{2,4},{3,5},{4,2},{5,3},{6,0},{7,1},{8,14},{9,15},{10,... | collective-permute-start | bytes 417800 | tf_op jit(solution)/shard_map/ppermute | solution.py:236
  6.1 12.1 %collective-permute-start.3 = (bf16[32,2176]{1,0:T(8,128)(2,1)S(1)}, bf16[32,2176]{1,0:T(8,128)(2,1)S(1)}, u32[]{:S(2)}, u32[]{:S(2)}) collective-permute-start(bf16[32,2176]{1,0:T(8,128)(2,1)S(1)} %get-tuple-element.36.refs_0_), channel_id=1, source_target_pairs={{0,4},{4,0},{8,12},{12,8},{1,5},{5,1},{9,13},{13,9},{2,6},{6,2},{1... | collective-permute-start | bytes 417800 | tf_op jit(solution)/shard_map/ppermute | solution.py:234
  6.9 11.3 %collective-permute-start.2 = (bf16[32,2176]{1,0:T(8,128)(2,1)S(1)}, bf16[32,2176]{1,0:T(8,128)(2,1)S(1)}, u32[]{:S(2)}, u32[]{:S(2)}) collective-permute-start(bf16[32,2176]{1,0:T(8,128)(2,1)S(1)} %get-tuple-element.36.refs_0_), channel_id=1, source_target_pairs={{0,2},{1,3},{2,0},{3,1},{4,6},{5,7},{6,4},{7,5},{8,10},{9,11},{10,... | collective-permute-start | bytes 417800 | tf_op jit(solution)/shard_map/ppermute | solution.py:228
  18.2 2.5 %collective-permute-start.7 = (bf16[32,2176]{1,0:T(8,128)(2,1)S(1)}, bf16[32,2176]{1,0:T(8,128)(2,1)S(1)}, u32[]{:S(2)}, u32[]{:S(2)}) collective-permute-start(bf16[32,2176]{1,0:T(8,128)(2,1)S(1)} %collective-permute-done.5.refs_0_), channel_id=1, source_target_pairs={{0,1},{1,0},{2,3},{3,2},{4,5},{5,4},{6,7},{7,6},{8,9},{9,8},{10,11... | collective-permute-start | bytes 417800 | tf_op jit(solution)/shard_map/ppermute | solution.py:239
  18.2 3.1 %collective-permute-start.8 = (bf16[32,2176]{1,0:T(8,128)(2,1)S(1)}, bf16[32,2176]{1,0:T(8,128)(2,1)S(1)}, u32[]{:S(2)}, u32[]{:S(2)}) collective-permute-start(bf16[32,2176]{1,0:T(8,128)(2,1)S(1)} %collective-permute-done.6.refs_1_), channel_id=1, source_target_pairs={{0,1},{1,0},{2,3},{3,2},{4,5},{5,4},{6,7},{7,6},{8,9},{9,8},{10,11... | collective-permute-start | bytes 417800 | tf_op jit(solution)/shard_map/ppermute | solution.py:239
  18.7 8.6 %collective-permute-start.14 = (bf16[32,2176]{1,0:T(8,128)(2,1)S(1)}, bf16[32,2176]{1,0:T(8,128)(2,1)S(1)}, u32[]{:S(2)}, u32[]{:S(2)}) collective-permute-start(bf16[32,2176]{1,0:T(8,128)(2,1)S(1)} %collective-permute-done.5.refs_0_), channel_id=1, source_target_pairs={{0,2},{1,3},{2,0},{3,1},{4,6},{5,7},{6,4},{7,5},{8,10},{9,11},{10,... | collective-permute-start | bytes 417800 | tf_op jit(solution)/shard_map/ppermute | solution.py:228
  20.2 7.1 %collective-permute-start.15 = (bf16[32,2176]{1,0:T(8,128)(2,1)S(1)}, bf16[32,2176]{1,0:T(8,128)(2,1)S(1)}, u32[]{:S(2)}, u32[]{:S(2)}) collective-permute-start(bf16[32,2176]{1,0:T(8,128)(2,1)S(1)} %collective-permute-done.6.refs_1_), channel_id=1, source_target_pairs={{0,2},{1,3},{2,0},{3,1},{4,6},{5,7},{6,4},{7,5},{8,10},{9,11},{10,... | collective-permute-start | bytes 417800 | tf_op jit(solution)/shard_map/ppermute | solution.py:228
  20.8 2.6 %collective-permute-start.11 = (bf16[32,2176]{1,0:T(8,128)(2,1)S(1)}, bf16[32,2176]{1,0:T(8,128)(2,1)S(1)}, u32[]{:S(2)}, u32[]{:S(2)}) collective-permute-start(bf16[32,2176]{1,0:T(8,128)(2,1)S(1)} %collective-permute-done.2.refs_0_), channel_id=1, source_target_pairs={{0,1},{1,0},{2,3},{3,2},{4,5},{5,4},{6,7},{7,6},{8,9},{9,8},{10,11... | collective-permute-start | bytes 417800 | tf_op jit(solution)/shard_map/ppermute | solution.py:239
  20.8 3.1 %collective-permute-start.12 = (bf16[32,2176]{1,0:T(8,128)(2,1)S(1)}, bf16[32,2176]{1,0:T(8,128)(2,1)S(1)}, u32[]{:S(2)}, u32[]{:S(2)}) collective-permute-start(bf16[32,2176]{1,0:T(8,128)(2,1)S(1)} %collective-permute-done.3.refs_1_), channel_id=1, source_target_pairs={{0,1},{1,0},{2,3},{3,2},{4,5},{5,4},{6,7},{7,6},{8,9},{9,8},{10,11... | collective-permute-start | bytes 417800 | tf_op jit(solution)/shard_map/ppermute | solution.py:239
  21.3 2.6 %collective-permute-start.13 = (bf16[32,2176]{1,0:T(8,128)(2,1)S(1)}, bf16[32,2176]{1,0:T(8,128)(2,1)S(1)}, u32[]{:S(2)}, u32[]{:S(2)}) collective-permute-start(bf16[32,2176]{1,0:T(8,128)(2,1)S(1)} %collective-permute-done.4.refs_2_), channel_id=1, source_target_pairs={{0,1},{1,0},{2,3},{3,2},{4,5},{5,4},{6,7},{7,6},{8,9},{9,8},{10,11... | collective-permute-start | bytes 417800 | tf_op jit(solution)/shard_map/ppermute | solution.py:239
  23.3 4.5 %collective-permute-start.9 = (bf16[64,2048]{1,0:T(8,128)(2,1)S(1)}, bf16[64,2048]{1,0:T(8,128)(2,1)S(1)}, u32[]{:S(2)}, u32[]{:S(2)}) collective-permute-start(bf16[64,2048]{1,0:T(8,128)(2,1)S(1)} %get-tuple-element.46), channel_id=1, source_target_pairs={{0,1},{1,0},{2,3},{3,2},{4,5},{5,4},{6,7},{7,6},{8,9},{9,8},{10,11... | collective-permute-start | bytes 786440 | tf_op jit(solution)/shard_map/ppermute | solution.py:239
  27.3 1.4 %collective-permute-start.16 = (bf16[32,2176]{1,0:T(8,128)(2,1)S(1)}, bf16[32,2176]{1,0:T(8,128)(2,1)S(1)}, u32[]{:S(2)}, u32[]{:S(2)}) collective-permute-start(bf16[32,2176]{1,0:T(8,128)(2,1)S(1)} %collective-permute-done.14.refs_0_), channel_id=1, source_target_pairs={{0,1},{1,0},{2,3},{3,2},{4,5},{5,4},{6,7},{7,6},{8,9},{9,8},{10,11... | collective-permute-start | bytes 417800 | tf_op jit(solution)/shard_map/ppermute | solution.py:239
  27.3 1.6 %collective-permute-start.17 = (bf16[32,2176]{1,0:T(8,128)(2,1)S(1)}, bf16[32,2176]{1,0:T(8,128)(2,1)S(1)}, u32[]{:S(2)}, u32[]{:S(2)}) collective-permute-start(bf16[32,2176]{1,0:T(8,128)(2,1)S(1)} %collective-permute-done.15.refs_1_), channel_id=1, source_target_pairs={{0,1},{1,0},{2,3},{3,2},{4,5},{5,4},{6,7},{7,6},{8,9},{9,8},{10,11... | collective-permute-start | bytes 417800 | tf_op jit(solution)/shard_map/ppermute | solution.py:239
  27.8 6.1 %collective-permute-start.20 = (bf16[96,2048]{1,0:T(8,128)(2,1)S(1)}, bf16[96,2048]{1,0:T(8,128)(2,1)S(1)}, u32[]{:S(2)}, u32[]{:S(2)}) collective-permute-start(bf16[96,2048]{1,0:T(8,128)(2,1)S(1)} %get-tuple-element.52), channel_id=1, source_target_pairs={{0,1},{1,0},{2,3},{3,2},{4,5},{5,4},{6,7},{7,6},{8,9},{9,8},{10,11... | collective-permute-start | bytes 1179656 | tf_op jit(solution)/shard_map/ppermute | solution.py:239
  30.8 4.7 %collective-permute-start.18 = (bf16[64,2048]{1,0:T(8,128)(2,1)S(1)}, bf16[64,2048]{1,0:T(8,128)(2,1)S(1)}, u32[]{:S(2)}, u32[]{:S(2)}) collective-permute-start(bf16[64,2048]{1,0:T(8,128)(2,1)S(1)} %get-tuple-element.58), channel_id=1, source_target_pairs={{0,1},{1,0},{2,3},{3,2},{4,5},{5,4},{6,7},{7,6},{8,9},{9,8},{10,11... | collective-permute-start | bytes 786440 | tf_op jit(solution)/shard_map/ppermute | solution.py:239
  31.2 6.5 %collective-permute-start.1 = (bf16[32,2048]{1,0:T(8,128)(2,1)S(1)}, bf16[32,2048]{1,0:T(8,128)(2,1)S(1)}, u32[]{:S(2)}, u32[]{:S(2)}) collective-permute-start(bf16[32,2048]{1,0:T(8,128)(2,1)S(1)} %get-tuple-element.38), channel_id=1, source_target_pairs={{0,1},{1,0},{2,3},{3,2},{4,5},{5,4},{6,7},{7,6},{8,9},{9,8},{10,11... | collective-permute-start | bytes 393224 | tf_op jit(solution)/shard_map/ppermute | solution.py:239
  31.4 14.7 %collective-permute-start.10 = (bf16[32,2048]{1,0:T(8,128)(2,1)S(1)}, bf16[32,2048]{1,0:T(8,128)(2,1)S(1)}, u32[]{:S(2)}, u32[]{:S(2)}) collective-permute-start(bf16[32,2048]{1,0:T(8,128)(2,1)S(1)} %get-tuple-element.47), channel_id=1, source_target_pairs={{0,8},{4,12},{8,0},{12,4},{1,9},{5,13},{9,1},{13,5},{2,10},{6,14},... | collective-permute-start | bytes 393224 | tf_op jit(solution)/shard_map/ppermute | solution.py:234
  33.9 6.4 %collective-permute-start.22 = (bf16[32,2048]{1,0:T(8,128)(2,1)S(1)}, bf16[32,2048]{1,0:T(8,128)(2,1)S(1)}, u32[]{:S(2)}, u32[]{:S(2)}) collective-permute-start(bf16[32,2048]{1,0:T(8,128)(2,1)S(1)} %get-tuple-element.63), channel_id=1, source_target_pairs={{0,2},{1,3},{2,0},{3,1},{4,6},{5,7},{6,4},{7,5},{8,10},{9,11},{10,... | collective-permute-start | bytes 393224 | tf_op jit(solution)/shard_map/ppermute | solution.py:228
  35.6 10.4 %collective-permute-start.24 = (bf16[32,2048]{1,0:T(8,128)(2,1)S(1)}, bf16[32,2048]{1,0:T(8,128)(2,1)S(1)}, u32[]{:S(2)}, u32[]{:S(2)}) collective-permute-start(bf16[32,2048]{1,0:T(8,128)(2,1)S(1)} %get-tuple-element.64), channel_id=1, source_target_pairs={{0,2},{1,3},{2,0},{3,1},{4,6},{5,7},{6,4},{7,5},{8,10},{9,11},{10,... | collective-permute-start | bytes 393224 | tf_op jit(solution)/shard_map/ppermute | solution.py:228
  36.1 11.7 %collective-permute-start.21 = (bf16[32,2048]{1,0:T(8,128)(2,1)S(1)}, bf16[32,2048]{1,0:T(8,128)(2,1)S(1)}, u32[]{:S(2)}, u32[]{:S(2)}) collective-permute-start(bf16[32,2048]{1,0:T(8,128)(2,1)S(1)} %get-tuple-element.61), channel_id=1, source_target_pairs={{0,2},{1,3},{2,0},{3,1},{4,6},{5,7},{6,4},{7,5},{8,10},{9,11},{10,... | collective-permute-start | bytes 393224 | tf_op jit(solution)/shard_map/ppermute | solution.py:228
  37.7 10.2 %collective-permute-start.19 = (bf16[32,2048]{1,0:T(8,128)(2,1)S(1)}, bf16[32,2048]{1,0:T(8,128)(2,1)S(1)}, u32[]{:S(2)}, u32[]{:S(2)}) collective-permute-start(bf16[32,2048]{1,0:T(8,128)(2,1)S(1)} %get-tuple-element.59), channel_id=1, source_target_pairs={{0,10},{1,11},{2,8},{3,9},{4,14},{5,15},{6,12},{7,13},{8,2},{9,3},... | collective-permute-start | bytes 393224 | tf_op jit(solution)/shard_map/ppermute | solution.py:236
  40.4 7.5 %collective-permute-start.23 = (bf16[32,2048]{1,0:T(8,128)(2,1)S(1)}, bf16[32,2048]{1,0:T(8,128)(2,1)S(1)}, u32[]{:S(2)}, u32[]{:S(2)}) collective-permute-start(bf16[32,2048]{1,0:T(8,128)(2,1)S(1)} %total.5), channel_id=1, source_target_pairs={{0,4},{4,0},{8,12},{12,8},{1,5},{5,1},{9,13},{13,9},{2,6},{6,2},{1... | collective-permute-start | bytes 393224 | tf_op jit(solution)/shard_map/ppermute | solution.py:234
  46.0 5.0 %collective-permute-start.25 = (bf16[32,2048]{1,0:T(8,128)(2,1)S(1)}, bf16[32,2048]{1,0:T(8,128)(2,1)S(1)}, u32[]{:S(2)}, u32[]{:S(2)}) collective-permute-start(bf16[32,2048]{1,0:T(8,128)(2,1)S(1)} %total.6), channel_id=1, source_target_pairs={{0,12},{4,8},{8,4},{12,0},{1,13},{5,9},{9,5},{13,1},{2,14},{6,10},... | collective-permute-start | bytes 393224 | tf_op jit(solution)/shard_map/ppermute | solution.py:234
